TPU v7x, 32 devices: a whole 2x2x4 slice. The times are simulated.
32 devices in a mesh: cells: 2 (over x), spots: 8 (over z, y), genes: 2 (over core).
Axes of the slice: x: 2, y: 2, z: 4, core: 2. Of those that a mesh axis runs over, the one named last changes fastest.
Arguments:
- logits: float32 [16384, 8192], P('cells', ('spots', 'genes')), may hold values from -6 to 6
- filter_logits: float32 [16384], P('cells'), may hold values from -6 to 6
- expression: bfloat16 [16384, 2048], P(('cells', 'spots'), 'genes'), may hold values from -6 to 6
- spot_expression: float32 [8192, 2048], P('spots', 'genes'), may hold values from -6 to 6
- cell_mask: int32 [16384], P('cells'), may hold values from 0 to 1, as said below
- spot_counts: int32 [8192], P(('spots', 'genes')), may hold values from 1 to 32
Outputs:
- predicted: float32 [8192, 2048], P('spots', 'genes')
- total_loss: float32 [], replicated
- grad_logits: float32 [16384, 8192], P('cells', ('spots', 'genes'))
- filter_grad: float32 [16384], P('cells')
Inputs may be any that keep to these rules, and one draw needn't show every extreme that they name: `cell_mask`: 1 marks a cell that takes part in the mapping.
All inputs are finite; a program needn't handle non-finite values.
Results may differ from a plain program's by a relative error of at most 0.0034.
Values may be sent and summed in bfloat16 or wider, within the bound.
No kernel may reach another device: no remote copies, remote signals or barrier semaphores. Data moves between devices by JAX's collectives and lax.ppermute only.
A program may use at most 192 MiB of HBM per device.

v0:
```python
import jax
import jax.numpy as jnp
from jax import lax
from jax.sharding import PartitionSpec as P

epsilon = 1e-06


def body(logits, filter_logits, expression, spot_expression, cell_mask, spot_counts):
    enable = cell_mask.astype(jnp.float32)
    counts = spot_counts.astype(jnp.float32)
    cells_total = logits.shape[0] * lax.axis_size("cells")
    spots_total = logits.shape[1] * lax.axis_size("spots") * lax.axis_size("genes")
    genes_total = expression.shape[1] * lax.axis_size("genes")
    masked = jnp.where(enable[:, None] > 0, logits, -1e30)
    col_top = lax.pmax(jnp.max(masked, axis=0), "cells")
    exponent = enable[:, None] * jnp.exp(logits - col_top[None, :])
    retain = jax.nn.sigmoid(filter_logits)
    count_part = jnp.sum(enable * retain)
    col_total, cell_count = lax.psum((jnp.sum(exponent, axis=0), count_part), "cells")
    mapping = exponent / col_total[None, :]
    mapped = retain[:, None] * mapping
    density = lax.psum(jnp.sum(mapped, axis=0), "cells")
    mapped_low = mapped.astype(jnp.bfloat16)
    expr_panel = lax.all_gather(expression, "spots", axis=0, tiled=True)
    partial_pred = lax.dot_general(
        lax.all_gather(mapped_low, "genes", axis=1, tiled=True),
        expr_panel,
        (((0,), (0,)), ((), ())),
        preferred_element_type=jnp.float32,
    )
    predicted = lax.psum(partial_pred, "cells")
    gene_stats = lax.psum(
        jnp.stack(
            [
                jnp.sum(predicted * spot_expression, axis=0),
                jnp.sum(predicted * predicted, axis=0),
                jnp.sum(spot_expression * spot_expression, axis=0),
            ]
        ),
        "spots",
    )
    spot_stats = lax.psum(
        jnp.stack(
            [
                jnp.sum(predicted * spot_expression, axis=1),
                jnp.sum(predicted * predicted, axis=1),
                jnp.sum(spot_expression * spot_expression, axis=1),
            ]
        ),
        "genes",
    )
    gene_scale = lax.rsqrt(gene_stats[1] + epsilon) * lax.rsqrt(gene_stats[2] + epsilon)
    gene_cos = gene_stats[0] * gene_scale
    spot_scale = lax.rsqrt(spot_stats[1] + epsilon) * lax.rsqrt(spot_stats[2] + epsilon)
    spot_cos = spot_stats[0] * spot_scale
    gene_part = jnp.where(lax.axis_index("spots") == 0, jnp.sum(gene_cos), jnp.float32(0.0))
    spot_part = jnp.where(lax.axis_index("genes") == 0, jnp.sum(spot_cos), jnp.float32(0.0))
    dens_total, kl_part, count_total, gene_sum, spot_sum = lax.psum(
        (
            jnp.sum(density),
            jnp.sum(counts * (jnp.log(counts) - jnp.log(density))),
            jnp.sum(counts),
            gene_part,
            spot_part,
        ),
        ("spots", "genes"),
    )
    kl_term = kl_part / count_total - jnp.log(count_total) + jnp.log(dens_total)
    offset = (cell_count - 0.5 * cells_total) / cells_total
    penalty = jnp.sqrt(offset * offset + 0.01)
    total_loss = -gene_sum / genes_total - spot_sum / spots_total + kl_term + penalty
    grad_pred = (
        -(
            spot_expression * gene_scale[None, :]
            - (gene_cos / (gene_stats[1] + epsilon))[None, :] * predicted
        )
        / genes_total
    )
    grad_pred = (
        grad_pred
        - (
            spot_expression * spot_scale[:, None]
            - (spot_cos / (spot_stats[1] + epsilon))[:, None] * predicted
        )
        / spots_total
    )
    grad_low = grad_pred.astype(jnp.bfloat16)
    dens_grad = -counts / (count_total * density) + 1.0 / dens_total
    grad_turned = lax.psum_scatter(
        lax.dot_general(
            grad_low, expr_panel, (((1,), (1,)), ((), ())), preferred_element_type=jnp.float32
        ),
        "genes",
        scatter_dimension=0,
        tiled=True,
    )
    grad_mapped = grad_turned.T + dens_grad[None, :]
    retain_grad = lax.psum(jnp.sum(grad_mapped * mapping, axis=1), ("spots", "genes"))
    retain_grad = retain_grad + enable * offset / (penalty * cells_total)
    filter_grad = retain_grad * retain * (1.0 - retain)
    grad_prob = retain[:, None] * grad_mapped
    col_inner = lax.psum(jnp.sum(mapping * grad_prob, axis=0), "cells")
    grad_logits = mapping * (grad_prob - col_inner[None, :])
    return (predicted, total_loss, grad_logits, filter_grad)


def solution(mesh):
    placed = (
        P("cells", ("spots", "genes")),
        P("cells"),
        P(("cells", "spots"), "genes"),
        P("spots", "genes"),
        P("cells"),
        P(("spots", "genes")),
    )
    return jax.shard_map(
        body,
        mesh=mesh,
        in_specs=placed,
        out_specs=(P("spots", "genes"), P(), P("cells", ("spots", "genes")), P("cells")),
        check_vma=False,
    )
```

profile of v0, /device:TPU:0, one launch (start us, length us, event | category | flops | bytes accessed | tf_op | source)
XLA Modules:
  0.0 715.1 jit_solution(17493120756184955193)
XLA Ops:
  7.2 0.8 broadcast_compare_fusion
  8.0 0.8 convert_element_type.12
  8.7 1.4 multiply_reduce_fusion.8
  10.1 17.4 %copy.12 = f32[8192,512]{0,1:T(8,128)} copy(f32[8192,512]{1,0:T(8,128)} %param.6) | data formatting | bytes 33554432 | tf_op args[0]
  27.6 6.7 select_reduce_fusion
  34.3 5.8 pmax.7
  40.1 8.7 %fusion.2 = f32[512]{0:T(512)S(1)} fusion(f32[8192,512]{0,1:T(8,128)} %copy.12, f32[512]{0:T(512)S(1)} %pmax.7, f32[8192]{0:T(1024)S(1)} %convert_element_type.12), kind=kLoop, calls=%fused_computation.10 | loop fusion | flops 12582400 | bytes 16814080 | tf_op jit(solution)/shard_map/reduce_sum | solution.py:20
  48.8 4.9 psum.91
  53.8 9.1 %multiply_reduce_fusion.1 = (f32[512]{0:T(512)S(1)}, f32[8192,512]{0,1:T(8,128)S(1)}) fusion(f32[8192]{0:T(1024)S(1)} %get-tuple-element.38, f32[512]{0:T(512)S(1)} %psum.91, f32[8192,512]{0,1:T(8,128)} %copy.12, f32[512]{0:T(512)S(1)} %pmax.7, f32[8192]{0:T(1024)S(1)} %convert_element_type.12), kind=kLoop, calls=%fused_computation.7 | loop fusion | flops 20971008 | bytes 33626112 | tf_op jit(solution)/shard_map/reduce_sum | solution.py:23
  62.9 6.2 copy-done
  69.0 4.2 multiply_convert_fusion
  73.3 0.7 all-gather.5.cloned.1.call-update
  74.0 31.2 %all-gather.3.cloned.1.call-done = bf16[8192,1024]{0,1:T(8,128)(2,1)} async-done(((bf16[8192,512]{0,1:T(8,128)(2,1)}), bf16[8192,1024]{0,1:T(8,128)(2,1)}) %all-gather.3.cloned.1.call-update) | async-done | bytes 16777232 | tf_op jit(solution)/shard_map/all_gather | solution.py:27
  105.3 230.9 %all-gather.5.cloned.1.call-done = bf16[8192,1024]{1,0:T(8,128)(2,1)} async-done(((bf16[1024,1024]{1,0:T(8,128)(2,1)}), bf16[8192,1024]{1,0:T(8,128)(2,1)}) %all-gather.5.cloned.1.call-update) | async-done | bytes 16777232 | tf_op jit(solution)/shard_map/all_gather | solution.py:25
  336.2 23.6 %fusion.21 = f32[1024,1024]{1,0:T(8,128)} fusion(bf16[8192,1024]{0,1:T(8,128)(2,1)} %all-gather.3.cloned.1.call-done, bf16[8192,1024]{1,0:T(8,128)(2,1)} %all-gather.5.cloned.1.call-done), kind=kOutput, calls=%fused_computation.51 | convolution fusion | flops 17179869184 | bytes 37748736 | tf_op jit(solution)/shard_map/dot_general | solution.py:26
  359.9 106.1 %all-reduce.5.cloned.1.call-done = f32[1024,1024]{1,0:T(8,128)} async-done(((f32[1024,1024]{1,0:T(8,128)}), f32[1024,1024]{1,0:T(8,128)}) %all-reduce.5.cloned.1.call-update) | async-done | bytes 4194320 | tf_op jit(solution)/shard_map/psum | solution.py:32
  466.0 4.3 multiply_reduce_fusion.6
  470.3 37.1 %psum.93 = f32[3,1024]{1,0:T(4,128)S(1)} all-reduce(f32[3,1024]{1,0:T(4,128)S(1)} %pad_maximum_fusion), channel_id=1, replica_groups=mesh['cells'=2,'spots'=8,'genes'=2] {'spots'}, use_global_device_ids=true, to_apply=%region_8.9 | all-reduce | flops 3072 | bytes 24576 | tf_op jit(solution)/shard_map/psum | solution.py:33
  507.5 3.4 psum.95
  510.9 30.2 %fusion.3 = f32[1024,8192]{1,0:T(8,128)} fusion(bf16[8192,1024]{1,0:T(8,128)(2,1)} %all-gather.5.cloned.1.call-done, f32[1024,1024]{1,0:T(8,128)} %all-reduce.5.cloned.1.call-done, f32[1024,1024]{1,0:T(8,128)} %param.9, f32[1024]{0:T(1024)S(1)} %get-tuple-element.33, f32[1024]{0:T(1024)S(1)} %get-tuple-element.34, f32[1024]{0:T(1024)S(1)} %bitcast.34, ...), kind=kOutput, calls=%fused_computation.16 | convolution fusion | flops 17191403520 | bytes 58736640 | tf_op jit(solution)/shard_map/dot_general | solution.py:91
  541.1 4.9 psum.97
  546.0 0.6 fusion.18
  546.6 30.1 %all-reduce.1 = (f32[]{:T(128)}, f32[]{:T(128)}) all-reduce(f32[]{:T(128)} %get-tuple-element.22, f32[]{:T(128)} %get-tuple-element.20), channel_id=1, replica_groups=mesh['cells'=2,'spots'=8,'genes'=2] {'spots','genes'}, use_global_device_ids=true, to_apply=%region_22.23 | all-reduce | flops 2 | bytes 16 | tf_op jit(solution)/shard_map/psum | solution.py:59
  579.3 0.6 fusion.17
  581.9 0.9 reduce-scatter.2.cloned.1.call-done
  582.7 12.1 %fusion = (f32[8192]{0:T(1024)S(1)}, f32[512]{0:T(512)S(1)}) fusion(f32[8192,512]{0,1:T(8,128)} %copy-done, f32[512,8192]{1,0:T(8,128)} %reduce-scatter.2.cloned.1.call-done, f32[512]{0:T(512)S(1)} %fusion.13, f32[8192]{0:T(1024)S(1)} %get-tuple-element.38), kind=kLoop, calls=%fused_computation.2 | loop fusion | flops 25157120 | bytes 33624064 | tf_op jit(solution)/shard_map/reduce_sum | solution.py:99
  594.9 63.1 %all-reduce = (f32[]{:T(128)}, f32[]{:T(128)}, f32[]{:T(128)}, f32[8192]{0:T(1024)S(1)}) all-reduce(f32[]{:T(128)S(6)} %select_n.12, f32[]{:T(128)S(6)} %select_n.13, f32[]{:T(128)} %get-tuple-element.21, f32[8192]{0:T(1024)S(1)} %get-tuple-element.12), channel_id=1, replica_groups=mesh['cells'=2,'spots'=8,'genes'=2] {'spots','genes'}, use_global_device_ids=true, to_apply=%region_10.11 | all-reduce | flops 8195 | bytes 65560 | tf_op jit(solution)/shard_map/psum | solution.py:59
  659.9 5.6 all-reduce.2
  666.2 17.7 %subtract_multiply_fusion = f32[8192,512]{0,1:T(8,128)} fusion(f32[8192,512]{0,1:T(8,128)} %copy-done, f32[512,8192]{1,0:T(8,128)} %reduce-scatter.2.cloned.1.call-done, f32[512]{0:T(512)S(1)} %get-tuple-element.30, f32[512]{0:T(512)S(1)} %fusion.13, f32[8192]{0:T(1024)S(1)} %get-tuple-element.38), kind=kLoop, calls=%fused_computation.3 | loop fusion | flops 16777216 | bytes 50368512 | tf_op jit(solution)/shard_map/mul | solution.py:104
  683.9 17.5 %copy.13 = f32[8192,512]{1,0:T(8,128)} copy(f32[8192,512]{0,1:T(8,128)} %subtract_multiply_fusion) | data formatting | bytes 33554432
  702.0 0.6 subtract_multiply_fusion.1
  702.6 4.8 copy.15
  (21 shorter events, 1.5 us)
Async XLA Ops:
  7.2 98.1 %all-gather.3.cloned.1.call-start = ((), (), s32[]{:S(2)}) async-start(), calls=%async_computation.1 | async-start | bytes 25165824 | tf_op jit(solution)/shard_map/all_gather | solution.py:27
  62.8 6.2 copy-start
  73.2 263.0 %all-gather.5.cloned.1.call-start = ((), (), s32[]{:S(2)}) async-start(), calls=%async_computation.2 | async-start | bytes 18874368 | tf_op jit(solution)/shard_map/all_gather | solution.py:25
  74.0 392.0 %all-reduce.5.cloned.1.call-start = ((), (), s32[]{:S(2)}) async-start(), calls=%async_computation.3 | async-start | bytes 8388608 | tf_op jit(solution)/shard_map/psum | solution.py:32
  359.8 222.9 %reduce-scatter.2.cloned.1.call-start = ((), (), s32[]{:S(2)}) async-start(), calls=%async_computation.4 | async-start | bytes 50331648 | tf_op jit(solution)/shard_map/reduce_scatter | solution.py:90
  541.0 5.0 copy-start.3
  683.9 18.1 %copy-start.1 = (s32[8192]{0:T(1024)S(1)}, s32[8192]{0:T(1024)}, u32[]{:S(2)}) copy-start(s32[8192]{0:T(1024)} %param.10) | copy-start | bytes 98308
  683.9 18.1 %copy-start.2 = (f32[8192]{0:T(1024)S(1)}, f32[8192]{0:T(1024)}, u32[]{:S(2)}) copy-start(f32[8192]{0:T(1024)} %param.7) | copy-start | bytes 98308
Sparse Core Ops, SparseCore 0:
  73.4 31.8 all-gather.2
  107.4 228.7 all-gather.4
  359.9 106.0 all-reduce.4
  541.2 41.5 reduce-scatter.1
where the time goes:
time: 716 us; the launch traced here: 715 us
  waiting for transfers between devices  370 us (52%)
  blocking collectives  155 us (22%)
  other arithmetic  68.9 us (10%)
  matrix products  53.8 us (8%)
  local copies, waits for them, and re-layouts  45.8 us (6%)
  between operations  21.5 us (3%)
    all_gather x1, waiting for transfers between devices, body(): expr_panel = lax.all_gather(expression, 'spots', axis=0, tiled=True)  231 us
    psum x1, waiting for transfers between devices, body(): predicted = lax.psum(partial_pred, 'cells')  106 us
    psum x2, blocking collectives, body(): lax.psum((jnp.sum(density), jnp.sum(counts * (jnp.log(counts) - jnp.log(d...  93.3 us
    unnamed x11, local copies, waits for them, and re-layouts  45.8 us
    psum x1, blocking collectives, body(): lax.psum(jnp.stack([jnp.sum(predicted * spot_expression, axis=0), jnp.sum...  37.1 us
    all_gather x1, waiting for transfers between devices, body(): lax.all_gather(mapped_low, 'genes', axis=1, tiled=True)  31.2 us
    dot_general x1, matrix products, body(): lax.dot_general(grad_low, expr_panel, (((1,), (1,)), ((), ())), preferred...  30.2 us
    dot_general x1, matrix products, body(): lax.dot_general(lax.all_gather(mapped_low, 'genes', axis=1, tiled=True),...  23.6 us
  transfers between devices with their start and end apart: 4, of which 4 were waited for; matrix products, arithmetic and copies ran while one was open for 0% of the time, Pallas kernels for 0%

commit v1 on v0

v1 whole, which is shorter than its diff:
```python
import functools

import jax
import jax.numpy as jnp
from jax import lax
from jax.experimental import pallas as pl
from jax.experimental.pallas import tpu as pltpu
from jax.sharding import PartitionSpec as P

epsilon = 1e-06
bf16 = jnp.bfloat16
f32 = jnp.float32
PIECES = 8
MIB = 1024 * 1024


def params(limit=48):
    return pltpu.CompilerParams(vmem_limit_bytes=limit * MIB)


def cost(flops=0, bytes_accessed=0, transcendentals=0):
    return pl.CostEstimate(flops=flops, bytes_accessed=bytes_accessed, transcendentals=transcendentals)


def col_stats_kernel(logits_ref, cell_ref, out_ref, top, total, dens):
    step = pl.program_id(0)

    @pl.when(step == 0)
    def _():
        top[...] = jnp.full_like(top, -1e30)
        total[...] = jnp.zeros_like(total)
        dens[...] = jnp.zeros_like(dens)

    rows, spots = logits_ref.shape
    cell = cell_ref[...]
    enable = cell[:, 0:1]
    retain = cell[:, 1:2]
    masked = jnp.where(enable > 0, logits_ref[...], -1e30)
    old = top[...]
    new = jnp.maximum(old, jnp.max(masked.reshape(rows // 8, 8, spots), axis=0))
    shrink = jnp.exp(old - new)
    part = jnp.exp(masked.reshape(rows // 8, 8, spots) - new[None]) * enable.reshape(rows // 8, 8, 1)
    top[...] = new
    total[...] = total[...] * shrink + jnp.sum(part, axis=0)
    dens[...] = dens[...] * shrink + jnp.sum(part * retain.reshape(rows // 8, 8, 1), axis=0)

    @pl.when(step == pl.num_programs(0) - 1)
    def _():
        slots = top[...]
        best = jnp.max(slots, axis=0, keepdims=True)
        scale = jnp.exp(slots - best)
        out_ref[0:1, :] = best
        out_ref[1:2, :] = jnp.sum(total[...] * scale, axis=0, keepdims=True)
        out_ref[2:3, :] = jnp.sum(dens[...] * scale, axis=0, keepdims=True)


def col_stats(logits, cell, block=512):
    cells, spots = logits.shape
    return pl.pallas_call(
        col_stats_kernel,
        grid=(cells // block,),
        in_specs=[
            pl.BlockSpec((block, spots), lambda i: (i, 0)),
            pl.BlockSpec((block, cell.shape[1]), lambda i: (i, 0)),
        ],
        out_specs=pl.BlockSpec((3, spots), lambda i: (0, 0)),
        out_shape=jax.ShapeDtypeStruct((3, spots), f32),
        scratch_shapes=[pltpu.VMEM((8, spots), f32)] * 3,
        compiler_params=params(),
        cost_estimate=cost(cells * spots * 8, cells * spots * 4, cells * spots),
        name="col_stats",
    )(logits, cell)


def mapped_kernel(order_ref, logits_ref, cell_ref, col_ref, out_ref):
    cell = cell_ref[...]
    weight = cell[:, 0:1] * cell[:, 1:2]
    masked = jnp.where(cell[:, 0:1] > 0, logits_ref[...], -1e30)
    mapping = jnp.exp(masked - col_ref[0:1, :]) * col_ref[1:2, :]
    out_ref[...] = (weight * mapping).T.astype(bf16)


def mapped_turned(order, logits, cell, col, block=512):
    cells, spots = logits.shape
    per = cells // PIECES // block

    def source(i, order):
        return (order[i // per] * per + i % per, 0)

    return pl.pallas_call(
        mapped_kernel,
        grid_spec=pltpu.PrefetchScalarGridSpec(
            num_scalar_prefetch=1,
            grid=(cells // block,),
            in_specs=[
                pl.BlockSpec((block, spots), source),
                pl.BlockSpec((block, cell.shape[1]), source),
                pl.BlockSpec((2, spots), lambda i, order: (0, 0)),
            ],
            out_specs=pl.BlockSpec((spots, block), lambda i, order: (0, i)),
        ),
        out_shape=jax.ShapeDtypeStruct((spots, cells), bf16),
        compiler_params=params(),
        cost_estimate=cost(cells * spots * 6, cells * spots * 6, cells * spots),
        name="mapped_turned",
    )(order, logits, cell, col)


def forward_kernel(table, spots, wide, mapped_ref, *refs):
    n = len(table)
    own_refs, other_refs = refs[:n], refs[n : 2 * n]
    pred_ref, panel_ref = refs[2 * n :]
    step = pl.program_id(0)

    @pl.when(step == 0)
    def _():
        pred_ref[...] = jnp.zeros_like(pred_ref)

    for source in range(n):
        used = [r for r in range(PIECES) if table[source][r] is not None]

        @pl.when(functools.reduce(jnp.logical_or, [step == r for r in used]))
        def _(source=source):
            both = jnp.concatenate([own_refs[source][...], other_refs[source][...]], axis=1)
            panel_ref[...] = both
            pred_ref[...] += jnp.dot(mapped_ref[...], both, preferred_element_type=f32)


def block_of(row):
    filled = []
    last = next(v for v in row if v is not None)
    for v in row:
        last = last if v is None else v
        filled.append(last)

    def pick(i):
        at = jnp.int32(filled[0])
        for r in range(1, len(filled)):
            if filled[r] != filled[r - 1]:
                at = jnp.where(i >= r, jnp.int32(filled[r]), at)
        return at

    return pick


def forward(mapped, own, other, table, columns, wide):
    spots, cells = mapped.shape
    rows = cells // PIECES
    specs = []
    for s in range(len(own)):
        pick = block_of(table[s])
        specs.append(pl.BlockSpec((rows, wide), lambda i, pick=pick, c=columns[s]: (pick(i), c)))
    return pl.pallas_call(
        functools.partial(forward_kernel, table, spots, wide),
        grid=(PIECES,),
        in_specs=[pl.BlockSpec((spots, rows), lambda i: (0, i))] + specs + specs,
        out_specs=[
            pl.BlockSpec((spots, 2 * wide), lambda i: (0, 0)),
            pl.BlockSpec((rows, 2 * wide), lambda i: (i, 0)),
        ],
        out_shape=[
            jax.ShapeDtypeStruct((spots, 2 * wide), f32),
            jax.ShapeDtypeStruct((cells, 2 * wide), bf16),
        ],
        compiler_params=params(),
        cost_estimate=cost(4 * spots * cells * wide, 2 * cells * (spots + 4 * wide)),
        name="forward",
    )(mapped, *own, *other)


def stats_kernel(wide, near_ref, far_ref, own_ref, other_ref, pred_ref, gene_ref, spot_ref):
    pred = near_ref[...] + far_ref[...]
    pred_ref[...] = pred
    target = jnp.concatenate([own_ref[...], other_ref[...]], axis=1)
    terms = (pred * target, pred * pred, target * target)
    lane = lax.broadcasted_iota(jnp.int32, spot_ref.shape, 1)
    spot = jnp.zeros(spot_ref.shape, f32)
    for k, term in enumerate(terms):
        gene_ref[k : k + 1, :] = jnp.sum(term, axis=0, keepdims=True)
        spot = jnp.where(lane == k, jnp.sum(term, axis=1, keepdims=True), spot)
    spot_ref[...] = spot


def pred_stats(near, far, target_own, target_other, column, wide):
    spots = near.shape[0]
    whole = pl.BlockSpec((spots, 2 * wide), lambda i: (0, 0))
    part = pl.BlockSpec((spots, wide), lambda i: (0, column))
    return pl.pallas_call(
        functools.partial(stats_kernel, wide),
        grid=(1,),
        in_specs=[whole, whole, part, part],
        out_specs=[
            whole,
            pl.BlockSpec((3, 2 * wide), lambda i: (0, 0)),
            pl.BlockSpec((spots, 4), lambda i: (0, 0)),
        ],
        out_shape=[
            jax.ShapeDtypeStruct((spots, 2 * wide), f32),
            jax.ShapeDtypeStruct((3, 2 * wide), f32),
            jax.ShapeDtypeStruct((spots, 4), f32),
        ],
        compiler_params=params(),
        cost_estimate=cost(spots * wide * 20, spots * wide * 40),
        name="pred_stats",
    )(near, far, target_own, target_other)


def grad_pred_kernel(widths, genes_total, spots_total, spot_ref, gene_ref, own_ref, other_ref, *refs):
    n = len(widths)
    pred_refs = refs[:n]
    turned_ref, inner_ref, sums_ref = refs[n:]
    spot = spot_ref[...]
    spot_pg, spot_pp, spot_gg = spot[:, 0:1], spot[:, 1:2], spot[:, 2:3]
    spot_scale = lax.rsqrt(spot_pp + epsilon) * lax.rsqrt(spot_gg + epsilon)
    spot_cos = spot_pg * spot_scale
    spot_back = spot_cos / (spot_pp + epsilon)
    gene = gene_ref[...]
    gene_scale = lax.rsqrt(gene[1:2, :] + epsilon) * lax.rsqrt(gene[2:3, :] + epsilon)
    gene_cos = gene[0:1, :] * gene_scale
    gene_back = gene_cos / (gene[1:2, :] + epsilon)
    folded = jnp.zeros((spot.shape[0], 128), f32)
    at = 0
    low = 0
    for q in range(n):
        wide = widths[q]
        pred = pred_refs[q][...]
        target = jnp.concatenate([own_ref[:, low : low + wide], other_ref[:, low : low + wide]], axis=1)
        cols = slice(at, at + 2 * wide)
        grad = -(target * gene_scale[:, cols] - gene_back[:, cols] * pred) / genes_total
        grad = grad - (target * spot_scale - spot_back * pred) / spots_total
        grad_low = grad.astype(bf16)
        turned_ref[at : at + 2 * wide, :] = grad_low.astype(f32).T.astype(bf16)
        prod = grad_low.astype(f32) * pred
        for k in range(0, 2 * wide, 128):
            folded = folded + prod[:, k : k + 128]
        at += 2 * wide
        low += wide
    inner_ref[...] = jnp.sum(folded.T, axis=0, keepdims=True)
    lane = lax.broadcasted_iota(jnp.int32, (1, 128), 1)
    gene_sum = jnp.sum(gene_cos, axis=1, keepdims=True)
    spot_sum = jnp.sum(spot_cos, axis=0, keepdims=True)
    sums_ref[...] = jnp.where(lane == 0, gene_sum, jnp.where(lane == 1, spot_sum, 0.0))


def grad_pred(widths, genes_total, spots_total, spot, gene, target_own, target_other, preds):
    spots, half = target_own.shape
    genes = 2 * half
    return pl.pallas_call(
        functools.partial(grad_pred_kernel, widths, genes_total, spots_total),
        out_shape=[
            jax.ShapeDtypeStruct((genes, spots), bf16),
            jax.ShapeDtypeStruct((1, spots), f32),
            jax.ShapeDtypeStruct((1, 128), f32),
        ],
        compiler_params=params(),
        cost_estimate=cost(spots * genes * 14, spots * genes * 10),
        name="grad_pred",
    )(spot, gene, target_own, target_other, *preds)


def backward_kernel(widths, order_ref, logits_ref, cell_ref, col_ref, turned_ref, *refs):
    n = len(widths)
    panel_refs = refs[:n]
    grad_ref, row_ref = refs[n:]
    panel = jnp.concatenate([ref[...] for ref in panel_refs], axis=1)
    inner = jnp.dot(panel, turned_ref[...], preferred_element_type=f32)
    cell = cell_ref[...]
    enable, retain = cell[:, 0:1], cell[:, 1:2]
    grad_mapped = inner + col_ref[2:3, :]
    masked = jnp.where(enable > 0, logits_ref[...], -1e30)
    mapping = enable * (jnp.exp(masked - col_ref[0:1, :]) * col_ref[1:2, :])
    grad_ref[...] = mapping * (retain * grad_mapped - col_ref[3:4, :])
    prod = grad_mapped * mapping
    folded = prod[:, 0:128]
    for k in range(128, prod.shape[1], 128):
        folded = folded + prod[:, k : k + 128]
    row_ref[...] = jnp.sum(folded.T, axis=0, keepdims=True)[None]


def backward(order, logits, cell, col, turned, panels, block=512):
    cells, spots = logits.shape
    genes = turned.shape[0]
    per = cells // PIECES // block
    widths = tuple(p.shape[1] for p in panels)

    def place(i, order):
        return (order[i // per] * per + i % per, 0)

    return pl.pallas_call(
        functools.partial(backward_kernel, widths),
        grid_spec=pltpu.PrefetchScalarGridSpec(
            num_scalar_prefetch=1,
            grid=(cells // block,),
            in_specs=[
                pl.BlockSpec((block, spots), place),
                pl.BlockSpec((block, cell.shape[1]), place),
                pl.BlockSpec((4, spots), lambda i, order: (0, 0)),
                pl.BlockSpec((genes, spots), lambda i, order: (0, 0)),
            ]
            + [pl.BlockSpec((block, w), lambda i, order: (i, 0)) for w in widths],
            out_specs=[
                pl.BlockSpec((block, spots), place),
                pl.BlockSpec((1, 1, block), lambda i, order: place(i, order) + (0,)),
            ],
        ),
        out_shape=[
            jax.ShapeDtypeStruct((cells, spots), f32),
            jax.ShapeDtypeStruct((cells // block, 1, block), f32),
        ],
        compiler_params=params(56),
        cost_estimate=cost(2 * cells * spots * genes, cells * (8 * spots + 2 * genes), cells * spots),
        name="backward",
    )(order, logits, cell, col, turned, *panels)


def swap_cells(x):
    return lax.ppermute(x, "cells", [(0, 1), (1, 0)])


def swap_genes(x):
    return lax.ppermute(x, "genes", [(0, 1), (1, 0)])


def line(spots):
    near = [(2 * z + y, 2 * (z ^ 1) + y) for z in range(4) for y in range(2)]
    middle = [(2 * z + y, 2 * (3 - z) + y) for z in (1, 2) for y in range(2)]
    across = [(i, i ^ 1) for i in range(8)]
    return near, middle, across


def sum_spots_genes(x, mirror=lambda v: v):
    if lax.axis_size("spots") != 8:
        x = lax.psum(x, "spots")
        return x + mirror(swap_genes(x))
    moved = [lax.ppermute(x, "spots", [(i, i ^ d) for i in range(8)]) for d in (2, 4, 6)]
    x = (x + moved[0]) + (moved[1] + moved[2])
    pairs = [lax.ppermute(x, ("spots", "genes"), [(i, i ^ d) for i in range(16)]) for d in (1, 2, 3)]
    return (x + pairs[1]) + mirror(pairs[0] + pairs[2])


def gathered(expression):
    rows, half = expression.shape
    if lax.axis_size("spots") != 8:
        own = lax.all_gather(expression, "spots", axis=0, tiled=True)
        other = swap_genes(own)
        wide = half // 4
        table = (tuple(range(PIECES)),)
        return jnp.arange(PIECES, dtype=jnp.int32), [
            (wide, q * wide, [own], [other], table, (q,)) for q in range(4)
        ]
    near, middle, across = line(8)
    spot = lax.axis_index("spots")
    z, y = spot // 2, spot % 2
    inside = (z == 1) | (z == 2)
    low = z < 2
    column = jnp.stack([z, z ^ 1, jnp.where(low, 2, 1), jnp.where(low, 3, 0)])
    order = jnp.concatenate([2 * column + y, 2 * column + (1 - y)]).astype(jnp.int32)

    def move(x, pairs):
        return lax.ppermute(x, "spots", pairs)

    beside = move(expression, across)
    own_other = swap_genes(expression)
    beside_other = swap_genes(beside)
    unit = half // 8
    plan = [(2 * unit, False), (2 * unit, False), (unit, False), (unit, False), (unit, False), (unit, True)]
    chunks = []
    at = 0
    for wide, early in plan:
        sent = expression[:, at : at + wide]
        if early:
            sent = jnp.concatenate([sent, beside[:, at : at + wide]], axis=0)
        near1 = move(sent, near)
        mid1 = move(sent, middle)
        mid2 = move(near1, middle)
        near2 = move(mid1, near)
        near3 = move(mid2, near)
        rest = jnp.concatenate([near1, jnp.where(inside, mid1, near2), jnp.where(inside, mid2, near3)], axis=0)
        rest_other = swap_genes(rest)
        x = None
        if early:
            table = (
                (0, x, x, x, x, x, x, x),
                (x, 0, 2, 4, x, 1, 3, 5),
                (x, x, x, x, 0, x, x, x),
            )
            own = [expression, rest, beside]
            other = [own_other, rest_other, beside_other]
            columns = (at // wide, 0, at // wide)
        else:
            table = (
                (0, x, x, x, x, x, x, x),
                (x, 0, 1, 2, x, x, x, x),
                (x, x, x, x, 0, x, x, x),
                (x, x, x, x, x, 0, 1, 2),
            )
            far = move(rest, across)
            far_other = swap_genes(far)
            own = [expression, rest, beside, far]
            other = [own_other, rest_other, beside_other, far_other]
            columns = (at // wide, 0, at // wide, 0)
        chunks.append((wide, at, own, other, table, columns))
        at += wide
    return order, chunks


def body(logits, filter_logits, expression, spot_expression, cell_mask, spot_counts):
    core = lax.axis_index("genes")
    cells_total = logits.shape[0] * lax.axis_size("cells")
    spots = logits.shape[1]
    spots_total = spots * lax.axis_size("spots") * lax.axis_size("genes")
    genes_total = expression.shape[1] * lax.axis_size("genes")

    order, chunks = gathered(expression)

    target_own = lax.dynamic_slice_in_dim(spot_expression, core * spots, spots, 0)
    target_other = swap_genes(lax.dynamic_slice_in_dim(spot_expression, (1 - core) * spots, spots, 0))

    enable = cell_mask.astype(f32)
    retain = jax.nn.sigmoid(filter_logits)
    cell = jnp.stack([enable, retain], axis=1)
    part = col_stats(logits, cell)
    part = jnp.concatenate([part, jnp.broadcast_to(jnp.sum(enable * retain), (1, spots))], axis=0)
    away = swap_cells(part)
    col_top = jnp.maximum(part[0], away[0])
    here, there = jnp.exp(part[0] - col_top), jnp.exp(away[0] - col_top)
    col_total = part[1] * here + away[1] * there
    density = (part[2] * here + away[2] * there) / col_total
    cell_count = part[3, 0] + away[3, 0]
    inverse = 1.0 / col_total
    col = jnp.stack([col_top, inverse])
    mapped = mapped_turned(order, logits, cell, col)

    counts = spot_counts.astype(f32)
    totals = sum_spots_genes(
        jnp.stack([jnp.sum(density), jnp.sum(counts * (jnp.log(counts) - jnp.log(density))), jnp.sum(counts)])
    )
    dens_total, kl_part, count_total = totals[0], totals[1], totals[2]
    kl_term = kl_part / count_total - jnp.log(count_total) + jnp.log(dens_total)
    offset = (cell_count - 0.5 * cells_total) / cells_total
    penalty = jnp.sqrt(offset * offset + 0.01)
    dens_grad = -counts / (count_total * density) + 1.0 / dens_total

    widths, preds, panels, genes_stats, spot_stats = [], [], [], [], []
    for wide, at, own, other, table, columns in chunks:
        partial, panel = forward(mapped, own, other, table, columns, wide)
        pred, gene_stat, spot_stat = pred_stats(
            partial, swap_cells(partial), target_own, target_other, at // wide, wide
        )
        widths.append(wide)
        preds.append(pred)
        panels.append(panel)
        genes_stats.append(gene_stat)
        spot_stats.append(spot_stat)

    def mirrored(some):
        def mirror(v):
            out, at = [], 0
            for wide in some:
                out += [v[:, at + wide : at + 2 * wide], v[:, at : at + wide]]
                at += 2 * wide
            return jnp.concatenate(out, axis=1)

        return mirror

    n = len(widths)
    last = n - 2
    early = [q for q in range(n) if q != last]
    early_sum = sum_spots_genes(
        jnp.concatenate([genes_stats[q] for q in early], axis=1), mirrored([widths[q] for q in early])
    )
    last_sum = sum_spots_genes(genes_stats[last], mirrored([widths[last]]))
    split = 2 * sum(widths[:last])
    gene = jnp.concatenate([early_sum[:, :split], last_sum, early_sum[:, split:]], axis=1)
    spot = functools.reduce(jnp.add, spot_stats)

    turned, inner, sums = grad_pred(
        tuple(widths), genes_total, spots_total, spot, gene, target_own, target_other, preds
    )
    col = jnp.stack([col_top, inverse, dens_grad, inner[0] + density * dens_grad])
    grad_logits, row = backward(order, logits, cell, col, turned, panels)

    all_sums = sum_spots_genes(sums)
    copies = lax.axis_size("spots") * lax.axis_size("genes")
    gene_sum, spot_sum = all_sums[0, 0] / copies, all_sums[0, 1]
    total_loss = -gene_sum / genes_total - spot_sum / spots_total + kl_term + penalty

    retain_grad = sum_spots_genes(row.reshape(-1, 128)).reshape(-1)
    retain_grad = retain_grad + enable * offset / (penalty * cells_total)
    filter_grad = retain_grad * retain * (1.0 - retain)

    mine = jnp.concatenate([p[:, :w] for p, w in zip(preds, widths)], axis=1)
    theirs = swap_genes(jnp.concatenate([p[:, w:] for p, w in zip(preds, widths)], axis=1))
    predicted = jnp.where(core == 0, jnp.concatenate([mine, theirs]), jnp.concatenate([theirs, mine]))
    return (predicted, total_loss, grad_logits, filter_grad)


def solution(mesh):
    placed = (
        P("cells", ("spots", "genes")),
        P("cells"),
        P(("cells", "spots"), "genes"),
        P("spots", "genes"),
        P("cells"),
        P(("spots", "genes")),
    )
    return jax.shard_map(
        body,
        mesh=mesh,
        in_specs=placed,
        out_specs=(P("spots", "genes"), P(), P("cells", ("spots", "genes")), P("cells")),
        check_vma=False,
    )
```

time: 716 us -> 536 us (0.75)
  waiting for transfers between devices: 370 us -> 213 us
  blocking collectives: 155 us -> 0 us
  Pallas kernels: 0 us -> 142 us
  starting transfers between devices: 0.16 us -> 108 us
  matrix products: 53.8 us -> 0 us
  other arithmetic: 68.9 us -> 27.9 us
  local copies, waits for them, and re-layouts: 45.8 us -> 32.6 us
  between operations: 21.5 us -> 8.58 us
    all_gather x2 -> x0, waiting for transfers between devices: 262 us -> none  [the longest x1 231 us: body(): expr_panel = lax.all_gather(expression, 'spots', axis=0, tiled=True)]
    ppermute x0 -> x88, waiting for transfers between devices: none -> 213 us  [the longest x36 158 us: move(): return lax.ppermute(x, 'spots', pairs)]
    psum x7 -> x0, blocking collectives: 149 us -> none  [the longest x2 93.3 us: body(): lax.psum((jnp.sum(density), jnp.sum(counts * (jnp.log(counts) - jnp.log(d...]
    pallas_call x0 -> x16, Pallas kernels: none -> 142 us  [the longest x6 64.3 us: forward(): pl.pallas_call(functools.partial(forward_kernel, table, spots, wide), gri...]
    ppermute x0 -> x88, starting transfers between devices: none -> 108 us  [the longest x36 62.5 us: move(): return lax.ppermute(x, 'spots', pairs)]
    psum x1 -> x0, waiting for transfers between devices: 106 us -> none  [body(): predicted = lax.psum(partial_pred, 'cells')]
    dot_general x2 -> x0, matrix products: 53.8 us -> none  [the longest x1 30.2 us: body(): lax.dot_general(grad_low, expr_panel, (((1,), (1,)), ((), ())), preferred...]
    reduce_sum x7 -> x1, other arithmetic: 36.7 us -> 1.4 us  [body(): jnp.sum(enable * retain)]
  transfers between devices with their start and end apart: 4 -> 88, of which waited for: 4 -> 29; matrix products, arithmetic and copies ran while one was open for 0% -> 6% of each run, Pallas kernels for 0% -> 24%
where the time goes in v1:
time: 536 us; the launch traced here: 532 us
  waiting for transfers between devices  213 us (40%)
  Pallas kernels  142 us (26%)
  starting transfers between devices  108 us (20%)
  local copies, waits for them, and re-layouts  32.6 us (6%)
  other arithmetic  27.9 us (5%)
  between operations  8.58 us (2%)
    ppermute x36, waiting for transfers between devices, move(): return lax.ppermute(x, 'spots', pairs)  158 us
    pallas_call x6, Pallas kernels, forward(): pl.pallas_call(functools.partial(forward_kernel, table, spots, wide), gri...  64.3 us
    ppermute x36, starting transfers between devices, move(): return lax.ppermute(x, 'spots', pairs)  62.5 us
    pallas_call x1, Pallas kernels, backward(): pl.pallas_call(functools.partial(backward_kernel, widths), grid_spec=pltp...  33.9 us
    ppermute x7, waiting for transfers between devices, swap_cells(): return lax.ppermute(x, 'cells', [(0, 1), (1, 0)])  33.3 us
    ppermute x15, starting transfers between devices, sum_spots_genes(): lax.ppermute(x, 'spots', [(i, i ^ d) for i in range(8)])  25.2 us
    unnamed x124, local copies, waits for them, and re-layouts  21.6 us
    pallas_call x1, Pallas kernels, mapped_turned(): pl.pallas_call(mapped_kernel, grid_spec=pltpu.PrefetchScalarGridSpec(num_...  18 us
  transfers between devices with their start and end apart: 88, of which 29 were waited for; matrix products, arithmetic and copies ran while one was open for 6% of the time, Pallas kernels for 24%

profile of v1, /device:TPU:0, one launch (start us, length us, event | category | flops | bytes accessed | tf_op | source)
XLA Modules:
  0.0 532.1 jit_solution(6358945603140901331)
XLA Ops:
  7.7 14.4 %col_stats.1 = f32[3,512]{1,0:T(4,128)S(1)} custom-call(f32[8192,512]{1,0:T(8,128)} %logits_ref.5, f32[8192,2]{1,0:T(8,128)S(1)} %copy-done.9), custom_call_target="tpu_custom_call" | custom-call | flops 33554432 | bytes 16777216 | tf_op jit(solution)/shard_map/col_stats/pallas_call | solution.py:59
  28.3 4.4 collective-permute-start.23
  52.2 5.9 %collective-permute-start.14 = (bf16[1024,256]{1,0:T(8,128)(2,1)S(1)}, bf16[1024,256]{1,0:T(8,128)(2,1)}, u32[]{:S(2)}, u32[]{:S(2)}) collective-permute-start(bf16[1024,256]{1,0:T(8,128)(2,1)S(1)} %get-tuple-element.88), channel_id=1, source_target_pairs={{0,4},{2,6},{4,0},{6,2},{8,12},{10,14},{12,8},{14,10},{1,5},{3,7},... | collective-permute-start | bytes 1572872 | tf_op jit(solution)/shard_map/ppermute | solution.py:360
  64.7 11.9 %collective-permute-done.43 = bf16[1024,128]{1,0:T(8,128)(2,1)S(1)} collective-permute-done((bf16[1024,128]{1,0:T(8,128)(2,1)S(1)}, bf16[1024,128]{1,0:T(8,128)(2,1)S(1)}, u32[]{:S(2)}, u32[]{:S(2)}) %collective-permute-start.43) | collective-permute-done | bytes 262176 | tf_op jit(solution)/shard_map/ppermute | solution.py:360
  78.6 4.0 constant_dynamic-slice_fusion
  82.6 4.6 collective-permute-start.25
  88.7 5.0 collective-permute-start.34
  107.9 3.6 collective-permute-done.27
  114.5 20.5 %collective-permute-done.36 = bf16[1024,128]{1,0:T(8,128)(2,1)S(1)} collective-permute-done((bf16[1024,128]{1,0:T(8,128)(2,1)S(1)}, bf16[1024,128]{1,0:T(8,128)(2,1)S(1)}, u32[]{:S(2)}, u32[]{:S(2)}) %collective-permute-start.36) | collective-permute-done | bytes 262176 | tf_op jit(solution)/shard_map/ppermute | solution.py:360
  141.2 53.8 %collective-permute-done.46.refs_3_ = bf16[3072,128]{1,0:T(8,128)(2,1)S(1)} collective-permute-done((bf16[3072,128]{1,0:T(8,128)(2,1)S(1)}, bf16[3072,128]{1,0:T(8,128)(2,1)S(1)}, u32[]{:S(2)}, u32[]{:S(2)}) %collective-permute-start.46) | collective-permute-done | bytes 786464 | tf_op jit(solution)/shard_map/ppermute | solution.py:360
  198.1 17.8 %collective-permute-done.28.refs_3_ = bf16[3072,128]{1,0:T(8,128)(2,1)S(1)} collective-permute-done((bf16[3072,128]{1,0:T(8,128)(2,1)S(1)}, bf16[3072,128]{1,0:T(8,128)(2,1)S(1)}, u32[]{:S(2)}, u32[]{:S(2)}) %collective-permute-start.28) | collective-permute-done | bytes 786464 | tf_op jit(solution)/shard_map/ppermute | solution.py:360
  219.3 15.2 %collective-permute-done.37.refs_3_ = bf16[3072,128]{1,0:T(8,128)(2,1)S(1)} collective-permute-done((bf16[3072,128]{1,0:T(8,128)(2,1)S(1)}, bf16[3072,128]{1,0:T(8,128)(2,1)S(1)}, u32[]{:S(2)}, u32[]{:S(2)}) %collective-permute-start.37) | collective-permute-done | bytes 786464 | tf_op jit(solution)/shard_map/ppermute | solution.py:360
  241.8 8.1 %collective-permute-done.50 = bf16[2048,128]{1,0:T(8,128)(2,1)} collective-permute-done((bf16[2048,128]{1,0:T(8,128)(2,1)S(1)}, bf16[2048,128]{1,0:T(8,128)(2,1)}, u32[]{:S(2)}, u32[]{:S(2)}) %collective-permute-start.50) | collective-permute-done | bytes 524320 | tf_op jit(solution)/shard_map/ppermute | solution.py:360
  256.1 4.3 collective-permute-start.52
  264.5 18.0 %mapped_turned.1.mapped_ref = bf16[512,8192]{1,0:T(8,128)(2,1)} custom-call(s32[8]{0:T(128)S(1)} %pad_add_fusion.order_ref, f32[8192,512]{1,0:T(8,128)} %logits_ref.5, f32[8192,2]{1,0:T(8,128)S(1)} %copy-done.10, f32[2,512]{1,0:T(2,128)S(1)} %pad_maximum_fusion.10.col_ref), custom_call_target="tpu_custom_call" | custom-call | flops 25165824 | bytes 25165824 | tf_op jit(solution)/shard_map/mapped_turned/pallas_call | solution.py:90
  286.4 8.1 %collective-permute-done.54 = bf16[2048,128]{1,0:T(8,128)(2,1)S(1)} collective-permute-done((bf16[2048,128]{1,0:T(8,128)(2,1)}, bf16[2048,128]{1,0:T(8,128)(2,1)S(1)}, u32[]{:S(2)}, u32[]{:S(2)}) %collective-permute-start.54) | collective-permute-done | bytes 524320 | tf_op jit(solution)/shard_map/ppermute | solution.py:360
  294.6 14.0 %collective-permute-done.7.refs_3_ = bf16[3072,256]{1,0:T(8,128)(2,1)} collective-permute-done((bf16[3072,256]{1,0:T(8,128)(2,1)}, bf16[3072,256]{1,0:T(8,128)(2,1)}, u32[]{:S(2)}, u32[]{:S(2)}) %collective-permute-start.7) | collective-permute-done | bytes 1572896 | tf_op jit(solution)/shard_map/ppermute | solution.py:360
  309.1 9.3 %forward.10 = (f32[512,256]{1,0:T(8,128)S(1)}, bf16[8192,256]{1,0:T(8,128)(2,1)}) custom-call(bf16[512,8192]{1,0:T(8,128)(2,1)} %mapped_turned.1.mapped_ref, bf16[1024,1024]{1,0:T(8,128)(2,1)S(1)} %copy-done.7, bf16[3072,128]{1,0:T(8,128)(2,1)S(1)} %pad_maximum_fusion.5.refs_1_, bf16[1024,1024]{1,0:T(8,128)(2,1)} %collective-permute-done.6.refs_2_, ...), custom_call_target="tpu_custom_call" | custom-call | flops 2147483648 | bytes 16777216 | tf_op jit(solution)/shard_map/forward/pallas_call | solution.py:153
  321.7 9.3 %forward.8 = (f32[512,256]{1,0:T(8,128)S(1)}, bf16[8192,256]{1,0:T(8,128)(2,1)}) custom-call(bf16[512,8192]{1,0:T(8,128)(2,1)} %mapped_turned.1.mapped_ref, bf16[1024,1024]{1,0:T(8,128)(2,1)S(1)} %copy-done.7, bf16[3072,128]{1,0:T(8,128)(2,1)S(1)} %copy-done.12, bf16[1024,1024]{1,0:T(8,128)(2,1)} %collective-permute-done.6.refs_2_, ...), custom_call_target="tpu_custom_call" | custom-call | flops 2147483648 | bytes 16777216 | tf_op jit(solution)/shard_map/forward/pallas_call | solution.py:153
  331.0 9.4 %forward.9 = (f32[512,256]{1,0:T(8,128)S(1)}, bf16[8192,256]{1,0:T(8,128)(2,1)}) custom-call(bf16[512,8192]{1,0:T(8,128)(2,1)} %mapped_turned.1.mapped_ref, bf16[1024,1024]{1,0:T(8,128)(2,1)S(1)} %copy-done.7, bf16[3072,128]{1,0:T(8,128)(2,1)S(1)} %copy-done.14, bf16[1024,1024]{1,0:T(8,128)(2,1)} %collective-permute-done.6.refs_2_, ...), custom_call_target="tpu_custom_call" | custom-call | flops 2147483648 | bytes 16777216 | tf_op jit(solution)/shard_map/forward/pallas_call | solution.py:153
  346.6 13.2 %forward.7 = (f32[512,512]{1,0:T(8,128)}, bf16[8192,512]{1,0:T(8,128)(2,1)}) custom-call(bf16[512,8192]{1,0:T(8,128)(2,1)} %mapped_turned.1.mapped_ref, bf16[1024,1024]{1,0:T(8,128)(2,1)} %refs_0_.11, bf16[3072,256]{1,0:T(8,128)(2,1)} %pad_maximum_fusion.1.refs_1_, bf16[1024,1024]{1,0:T(8,128)(2,1)} %collective-permute-done.6.refs_2_, ...), custom_call_target="tpu_custom_call" | custom-call | flops 4294967296 | bytes 25165824 | tf_op jit(solution)/shard_map/forward/pallas_call | solution.py:153
  370.3 13.3 %forward.6 = (f32[512,512]{1,0:T(8,128)}, bf16[8192,512]{1,0:T(8,128)(2,1)}) custom-call(bf16[512,8192]{1,0:T(8,128)(2,1)} %mapped_turned.1.mapped_ref, bf16[1024,1024]{1,0:T(8,128)(2,1)} %refs_0_.11, bf16[3072,256]{1,0:T(8,128)(2,1)} %pad_maximum_fusion.refs_1_, bf16[1024,1024]{1,0:T(8,128)(2,1)} %collective-permute-done.6.refs_2_, ...), custom_call_target="tpu_custom_call" | custom-call | flops 4294967296 | bytes 25165824 | tf_op jit(solution)/shard_map/forward/pallas_call | solution.py:153
  386.5 3.4 collective-permute-done.40.far_ref
  400.2 9.8 %forward.11 = (f32[512,256]{1,0:T(8,128)S(1)}, bf16[8192,256]{1,0:T(8,128)(2,1)}) custom-call(bf16[512,8192]{1,0:T(8,128)(2,1)} %mapped_turned.1.mapped_ref, bf16[1024,1024]{1,0:T(8,128)(2,1)S(1)} %copy-done.8, bf16[6144,128]{1,0:T(8,128)(2,1)} %pad_maximum_fusion.2.refs_1_, bf16[1024,1024]{1,0:T(8,128)(2,1)} %collective-permute-done.6.refs_2_, ...), custom_call_target="tpu_custom_call" | custom-call | flops 2147483648 | bytes 16777216 | tf_op jit(solution)/shard_map/forward/pallas_call | solution.py:153
  414.6 20.3 %collective-permute-done.12.far_ref = f32[512,512]{1,0:T(8,128)} collective-permute-done((f32[512,512]{1,0:T(8,128)}, f32[512,512]{1,0:T(8,128)}, u32[]{:S(2)}, u32[]{:S(2)}) %collective-permute-start.12) | collective-permute-done | bytes 1048608 | tf_op jit(solution)/shard_map/ppermute | solution.py:317
  437.2 8.3 %collective-permute-done.56.far_ref = f32[512,256]{1,0:T(8,128)S(1)} collective-permute-done((f32[512,256]{1,0:T(8,128)S(1)}, f32[512,256]{1,0:T(8,128)S(1)}, u32[]{:S(2)}, u32[]{:S(2)}) %collective-permute-start.56) | collective-permute-done | bytes 524320 | tf_op jit(solution)/shard_map/ppermute | solution.py:317
  446.1 4.5 collective-permute-start.59
  461.1 6.0 %grad_pred.1 = (bf16[2048,512]{1,0:T(8,128)(2,1)}, f32[1,512]{1,0:T(1,128)S(1)}, f32[1,128]{1,0:T(1,128)S(1)}) custom-call(f32[512,4]{1,0:T(8,128)S(1)} %add_add_fusion.spot_ref, f32[3,2048]{1,0:T(4,128)S(1)} %pad_maximum_fusion.8.gene_ref, f32[512,1024]{1,0:T(8,128)} %copy-done, f32[512,1024]{1,0:T(8,128)} %copy-done.1, ...), custom_call_target="tpu_custom_call" | custom-call | flops 14680064 | bytes 10485760 | tf_op jit(solution)/shard_map/grad_pred/pallas_call | solution.py:248
  467.2 3.8 collective-permute-start.71
  472.7 3.6 collective-permute-done.72
  478.5 33.9 %backward.1 = (f32[8192,512]{1,0:T(8,128)}, f32[16,1,512]{2,1,0:T(1,128)}) custom-call(s32[8]{0:T(128)} %copy-done.40, f32[8192,512]{1,0:T(8,128)} %logits_ref.5, f32[8192,2]{1,0:T(8,128)} %copy.13.cell_ref, f32[4,512]{1,0:T(4,128)} %pad_maximum_fusion.9.col_ref, bf16[2048,512]{1,0:T(8,128)(2,1)} %get-tuple-element.65.turned_ref, ...), custom_call_target="tpu_custom_call" | custom-call | flops 17179869184 | bytes 67108864 | tf_op jit(solution)/shard_map/backward/pallas_call | solution.py:289
  525.8 5.2 maximum_select_fusion
  (345 shorter events, 156.6 us)
Async XLA Ops:
  52.2 30.4 %collective-permute-start.14 = (bf16[1024,256]{1,0:T(8,128)(2,1)S(1)}, bf16[1024,256]{1,0:T(8,128)(2,1)}, u32[]{:S(2)}, u32[]{:S(2)}) collective-permute-start(bf16[1024,256]{1,0:T(8,128)(2,1)S(1)} %get-tuple-element.88), channel_id=1, source_target_pairs={{0,4},{2,6},{4,0},{6,2},{8,12},{10,14},{12,8},{14,10},{1,5},{3,7},... | collective-permute-start | bytes 1572872 | tf_op jit(solution)/shard_map/ppermute | solution.py:360
  58.1 29.1 %collective-permute-start.15 = (bf16[1024,256]{1,0:T(8,128)(2,1)S(1)}, bf16[1024,256]{1,0:T(8,128)(2,1)}, u32[]{:S(2)}, u32[]{:S(2)}) collective-permute-start(bf16[1024,256]{1,0:T(8,128)(2,1)S(1)} %get-tuple-element.88), channel_id=1, source_target_pairs={{4,8},{6,10},{8,4},{10,6},{5,9},{7,11},{9,5},{11,7},{20,24},{22,26... | collective-permute-start | bytes 1572872 | tf_op jit(solution)/shard_map/ppermute | solution.py:360
  62.1 25.8 %collective-permute-start.1 = (bf16[1024,256]{1,0:T(8,128)(2,1)S(1)}, bf16[1024,256]{1,0:T(8,128)(2,1)}, u32[]{:S(2)}, u32[]{:S(2)}) collective-permute-start(bf16[1024,256]{1,0:T(8,128)(2,1)S(1)} %get-tuple-element.89), channel_id=1, source_target_pairs={{0,4},{2,6},{4,0},{6,2},{8,12},{10,14},{12,8},{14,10},{1,5},{3,7},... | collective-permute-start | bytes 1572872 | tf_op jit(solution)/shard_map/ppermute | solution.py:360
  97.6 38.9 %collective-permute-start.17 = (bf16[1024,256]{1,0:T(8,128)(2,1)}, bf16[1024,256]{1,0:T(8,128)(2,1)S(1)}, u32[]{:S(2)}, u32[]{:S(2)}) collective-permute-start(bf16[1024,256]{1,0:T(8,128)(2,1)} %collective-permute-done.14), channel_id=1, source_target_pairs={{4,8},{6,10},{8,4},{10,6},{5,9},{7,11},{9,5},{11,7},{20,24},{22,26... | collective-permute-start | bytes 1572872 | tf_op jit(solution)/shard_map/ppermute | solution.py:360
  100.2 36.8 %collective-permute-start.16 = (bf16[1024,256]{1,0:T(8,128)(2,1)}, bf16[1024,256]{1,0:T(8,128)(2,1)S(1)}, u32[]{:S(2)}, u32[]{:S(2)}) collective-permute-start(bf16[1024,256]{1,0:T(8,128)(2,1)} %collective-permute-done.15), channel_id=1, source_target_pairs={{0,4},{2,6},{4,0},{6,2},{8,12},{10,14},{12,8},{14,10},{1,5},{3,7},... | collective-permute-start | bytes 1572872 | tf_op jit(solution)/shard_map/ppermute | solution.py:360
  102.3 35.7 %collective-permute-start.4 = (bf16[1024,256]{1,0:T(8,128)(2,1)}, bf16[1024,256]{1,0:T(8,128)(2,1)S(1)}, u32[]{:S(2)}, u32[]{:S(2)}) collective-permute-start(bf16[1024,256]{1,0:T(8,128)(2,1)} %collective-permute-done.1), channel_id=1, source_target_pairs={{4,8},{6,10},{8,4},{10,6},{5,9},{7,11},{9,5},{11,7},{20,24},{22,26... | collective-permute-start | bytes 1572872 | tf_op jit(solution)/shard_map/ppermute | solution.py:360
  105.9 32.4 %collective-permute-start.3 = (bf16[1024,256]{1,0:T(8,128)(2,1)}, bf16[1024,256]{1,0:T(8,128)(2,1)S(1)}, u32[]{:S(2)}, u32[]{:S(2)}) collective-permute-start(bf16[1024,256]{1,0:T(8,128)(2,1)} %collective-permute-done.2), channel_id=1, source_target_pairs={{0,4},{2,6},{4,0},{6,2},{8,12},{10,14},{12,8},{14,10},{1,5},{3,7},... | collective-permute-start | bytes 1572872 | tf_op jit(solution)/shard_map/ppermute | solution.py:360
  135.0 82.6 %collective-permute-start.6 = (bf16[1024,1024]{1,0:T(8,128)(2,1)S(1)}, bf16[1024,1024]{1,0:T(8,128)(2,1)}, u32[]{:S(2)}, u32[]{:S(2)}) collective-permute-start(bf16[1024,1024]{1,0:T(8,128)(2,1)S(1)} %copy-done.6), channel_id=1, source_target_pairs={{0,2},{2,0},{4,6},{6,4},{8,10},{10,8},{12,14},{14,12},{1,3},{3,1},... | collective-permute-start | bytes 6291464 | tf_op jit(solution)/shard_map/ppermute | solution.py:360
  136.5 58.4 %collective-permute-start.46 = (bf16[3072,128]{1,0:T(8,128)(2,1)S(1)}, bf16[3072,128]{1,0:T(8,128)(2,1)S(1)}, u32[]{:S(2)}, u32[]{:S(2)}) collective-permute-start(bf16[3072,128]{1,0:T(8,128)(2,1)S(1)} %pad_maximum_fusion.5.refs_1_), channel_id=1, source_target_pairs={{0,2},{2,0},{4,6},{6,4},{8,10},{10,8},{12,14},{14,12},{1,3},{3,1},... | collective-permute-start | bytes 2359304 | tf_op jit(solution)/shard_map/ppermute | solution.py:360
  137.0 57.9 %collective-permute-start.47 = (bf16[3072,128]{1,0:T(8,128)(2,1)S(1)}, bf16[3072,128]{1,0:T(8,128)(2,1)S(1)}, u32[]{:S(2)}, u32[]{:S(2)}) collective-permute-start(bf16[3072,128]{1,0:T(8,128)(2,1)S(1)} %pad_maximum_fusion.5.refs_1_), channel_id=1, source_target_pairs={{0,1},{1,0},{2,3},{3,2},{4,5},{5,4},{6,7},{7,6},{8,9},{9,8},{10,11... | collective-permute-start | bytes 2359304 | tf_op jit(solution)/shard_map/ppermute | solution.py:321
  138.1 58.3 %collective-permute-start.18 = (bf16[1024,256]{1,0:T(8,128)(2,1)S(1)}, bf16[1024,256]{1,0:T(8,128)(2,1)S(1)}, u32[]{:S(2)}, u32[]{:S(2)}) collective-permute-start(bf16[1024,256]{1,0:T(8,128)(2,1)S(1)} %collective-permute-done.17), channel_id=1, source_target_pairs={{0,4},{2,6},{4,0},{6,2},{8,12},{10,14},{12,8},{14,10},{1,5},{3,7},... | collective-permute-start | bytes 1572872 | tf_op jit(solution)/shard_map/ppermute | solution.py:360
  138.2 59.7 %collective-permute-start.5 = (bf16[1024,256]{1,0:T(8,128)(2,1)S(1)}, bf16[1024,256]{1,0:T(8,128)(2,1)S(1)}, u32[]{:S(2)}, u32[]{:S(2)}) collective-permute-start(bf16[1024,256]{1,0:T(8,128)(2,1)S(1)} %collective-permute-done.4), channel_id=1, source_target_pairs={{0,4},{2,6},{4,0},{6,2},{8,12},{10,14},{12,8},{14,10},{1,5},{3,7},... | collective-permute-start | bytes 1572872 | tf_op jit(solution)/shard_map/ppermute | solution.py:360
  195.0 43.7 %collective-permute-start.8 = (bf16[1024,1024]{1,0:T(8,128)(2,1)S(1)}, bf16[1024,1024]{1,0:T(8,128)(2,1)S(1)}, u32[]{:S(2)}, u32[]{:S(2)}) collective-permute-start(bf16[1024,1024]{1,0:T(8,128)(2,1)S(1)} %copy-done.6), channel_id=1, source_target_pairs={{0,1},{1,0},{2,3},{3,2},{4,5},{5,4},{6,7},{7,6},{8,9},{9,8},{10,11... | collective-permute-start | bytes 6291464 | tf_op jit(solution)/shard_map/ppermute | solution.py:321
  195.9 44.3 %collective-permute-start.13 = (f32[512,1024]{1,0:T(8,128)S(1)}, f32[512,1024]{1,0:T(8,128)S(1)}, u32[]{:S(2)}, u32[]{:S(2)}) collective-permute-start(f32[512,1024]{1,0:T(8,128)S(1)} %copy-done.42), channel_id=1, source_target_pairs={{0,1},{1,0},{2,3},{3,2},{4,5},{5,4},{6,7},{7,6},{8,9},{9,8},{10,11... | collective-permute-start | bytes 6291464 | tf_op jit(solution)/shard_map/ppermute | solution.py:321
  238.7 47.2 %collective-permute-start.19 = (bf16[3072,256]{1,0:T(8,128)(2,1)}, bf16[3072,256]{1,0:T(8,128)(2,1)}, u32[]{:S(2)}, u32[]{:S(2)}) collective-permute-start(bf16[3072,256]{1,0:T(8,128)(2,1)} %pad_maximum_fusion.1.refs_1_), channel_id=1, source_target_pairs={{0,2},{2,0},{4,6},{6,4},{8,10},{10,8},{12,14},{14,12},{1,3},{3,1},... | collective-permute-start | bytes 4718600 | tf_op jit(solution)/shard_map/ppermute | solution.py:360
  241.7 66.9 %collective-permute-start.10 = (bf16[1024,1024]{1,0:T(8,128)(2,1)}, bf16[1024,1024]{1,0:T(8,128)(2,1)}, u32[]{:S(2)}, u32[]{:S(2)}) collective-permute-start(bf16[1024,1024]{1,0:T(8,128)(2,1)} %collective-permute-done.6.refs_2_), channel_id=1, source_target_pairs={{0,1},{1,0},{2,3},{3,2},{4,5},{5,4},{6,7},{7,6},{8,9},{9,8},{10,11... | collective-permute-start | bytes 6291464 | tf_op jit(solution)/shard_map/ppermute | solution.py:321
  249.9 32.5 %collective-permute-start.53 = (bf16[2048,128]{1,0:T(8,128)(2,1)}, bf16[2048,128]{1,0:T(8,128)(2,1)}, u32[]{:S(2)}, u32[]{:S(2)}) collective-permute-start(bf16[2048,128]{1,0:T(8,128)(2,1)} %collective-permute-done.50), channel_id=1, source_target_pairs={{4,8},{6,10},{8,4},{10,6},{5,9},{7,11},{9,5},{11,7},{20,24},{22,26... | collective-permute-start | bytes 1572872 | tf_op jit(solution)/shard_map/ppermute | solution.py:360
  254.6 54.0 %collective-permute-start.7 = (bf16[3072,256]{1,0:T(8,128)(2,1)}, bf16[3072,256]{1,0:T(8,128)(2,1)}, u32[]{:S(2)}, u32[]{:S(2)}) collective-permute-start(bf16[3072,256]{1,0:T(8,128)(2,1)} %pad_maximum_fusion.refs_1_), channel_id=1, source_target_pairs={{0,2},{2,0},{4,6},{6,4},{8,10},{10,8},{12,14},{14,12},{1,3},{3,1},... | collective-permute-start | bytes 4718600 | tf_op jit(solution)/shard_map/ppermute | solution.py:360
  256.1 28.5 %collective-permute-start.52 = (bf16[2048,128]{1,0:T(8,128)(2,1)}, bf16[2048,128]{1,0:T(8,128)(2,1)}, u32[]{:S(2)}, u32[]{:S(2)}) collective-permute-start(bf16[2048,128]{1,0:T(8,128)(2,1)} %collective-permute-done.51), channel_id=1, source_target_pairs={{0,4},{2,6},{4,0},{6,2},{8,12},{10,14},{12,8},{14,10},{1,5},{3,7},... | collective-permute-start | bytes 1572872 | tf_op jit(solution)/shard_map/ppermute | solution.py:360
  284.7 33.8 %collective-permute-start.39 = (bf16[3072,128]{1,0:T(8,128)(2,1)S(1)}, bf16[3072,128]{1,0:T(8,128)(2,1)S(1)}, u32[]{:S(2)}, u32[]{:S(2)}) collective-permute-start(bf16[3072,128]{1,0:T(8,128)(2,1)S(1)} %copy-done.26), channel_id=1, source_target_pairs={{0,1},{1,0},{2,3},{3,2},{4,5},{5,4},{6,7},{7,6},{8,9},{9,8},{10,11... | collective-permute-start | bytes 2359304 | tf_op jit(solution)/shard_map/ppermute | solution.py:321
  285.9 56.4 %collective-permute-start.20 = (bf16[3072,256]{1,0:T(8,128)(2,1)}, bf16[3072,256]{1,0:T(8,128)(2,1)S(1)}, u32[]{:S(2)}, u32[]{:S(2)}) collective-permute-start(bf16[3072,256]{1,0:T(8,128)(2,1)} %pad_maximum_fusion.1.refs_1_), channel_id=1, source_target_pairs={{0,1},{1,0},{2,3},{3,2},{4,5},{5,4},{6,7},{7,6},{8,9},{9,8},{10,11... | collective-permute-start | bytes 4718600 | tf_op jit(solution)/shard_map/ppermute | solution.py:321
  294.6 48.9 %collective-permute-start.21 = (bf16[3072,256]{1,0:T(8,128)(2,1)}, bf16[3072,256]{1,0:T(8,128)(2,1)}, u32[]{:S(2)}, u32[]{:S(2)}) collective-permute-start(bf16[3072,256]{1,0:T(8,128)(2,1)} %collective-permute-done.19.refs_3_), channel_id=1, source_target_pairs={{0,1},{1,0},{2,3},{3,2},{4,5},{5,4},{6,7},{7,6},{8,9},{9,8},{10,11... | collective-permute-start | bytes 4718600 | tf_op jit(solution)/shard_map/ppermute | solution.py:321
  308.6 56.5 %collective-permute-start.9 = (bf16[3072,256]{1,0:T(8,128)(2,1)}, bf16[3072,256]{1,0:T(8,128)(2,1)S(1)}, u32[]{:S(2)}, u32[]{:S(2)}) collective-permute-start(bf16[3072,256]{1,0:T(8,128)(2,1)} %pad_maximum_fusion.refs_1_), channel_id=1, source_target_pairs={{0,1},{1,0},{2,3},{3,2},{4,5},{5,4},{6,7},{7,6},{8,9},{9,8},{10,11... | collective-permute-start | bytes 4718600 | tf_op jit(solution)/shard_map/ppermute | solution.py:321
  308.6 57.4 %collective-permute-start.11 = (bf16[3072,256]{1,0:T(8,128)(2,1)}, bf16[3072,256]{1,0:T(8,128)(2,1)}, u32[]{:S(2)}, u32[]{:S(2)}) collective-permute-start(bf16[3072,256]{1,0:T(8,128)(2,1)} %collective-permute-done.7.refs_3_), channel_id=1, source_target_pairs={{0,1},{1,0},{2,3},{3,2},{4,5},{5,4},{6,7},{7,6},{8,9},{9,8},{10,11... | collective-permute-start | bytes 4718600 | tf_op jit(solution)/shard_map/ppermute | solution.py:321
  343.5 56.0 %collective-permute-start.55 = (bf16[6144,128]{1,0:T(8,128)(2,1)}, bf16[6144,128]{1,0:T(8,128)(2,1)}, u32[]{:S(2)}, u32[]{:S(2)}) collective-permute-start(bf16[6144,128]{1,0:T(8,128)(2,1)} %pad_maximum_fusion.2.refs_1_), channel_id=1, source_target_pairs={{0,1},{1,0},{2,3},{3,2},{4,5},{5,4},{6,7},{7,6},{8,9},{9,8},{10,11... | collective-permute-start | bytes 4718600 | tf_op jit(solution)/shard_map/ppermute | solution.py:321
  383.6 28.9 %collective-permute-start.22 = (f32[512,512]{1,0:T(8,128)}, f32[512,512]{1,0:T(8,128)}, u32[]{:S(2)}, u32[]{:S(2)}) collective-permute-start(f32[512,512]{1,0:T(8,128)} %get-tuple-element.41.near_ref), channel_id=1, source_target_pairs={{0,16},{16,0},{1,17},{17,1},{2,18},{18,2},{3,19},{19,3},{4,20},{20... | collective-permute-start | bytes 3145736 | tf_op jit(solution)/shard_map/ppermute | solution.py:317
  384.9 50.1 %collective-permute-start.12 = (f32[512,512]{1,0:T(8,128)}, f32[512,512]{1,0:T(8,128)}, u32[]{:S(2)}, u32[]{:S(2)}) collective-permute-start(f32[512,512]{1,0:T(8,128)} %get-tuple-element.39.near_ref), channel_id=1, source_target_pairs={{0,16},{16,0},{1,17},{17,1},{2,18},{18,2},{3,19},{19,3},{4,20},{20... | collective-permute-start | bytes 3145736 | tf_op jit(solution)/shard_map/ppermute | solution.py:317
  410.0 35.4 %collective-permute-start.56 = (f32[512,256]{1,0:T(8,128)S(1)}, f32[512,256]{1,0:T(8,128)S(1)}, u32[]{:S(2)}, u32[]{:S(2)}) collective-permute-start(f32[512,256]{1,0:T(8,128)S(1)} %get-tuple-element.49.near_ref), channel_id=1, source_target_pairs={{0,16},{16,0},{1,17},{17,1},{2,18},{18,2},{3,19},{19,3},{4,20},{20... | collective-permute-start | bytes 1572872 | tf_op jit(solution)/shard_map/ppermute | solution.py:317
  455.7 70.0 %collective-permute-start.57 = (f32[512,1024]{1,0:T(8,128)}, f32[512,1024]{1,0:T(8,128)}, u32[]{:S(2)}, u32[]{:S(2)}) collective-permute-start(f32[512,1024]{1,0:T(8,128)} %get-tuple-element.95), channel_id=1, source_target_pairs={{0,1},{1,0},{2,3},{3,2},{4,5},{5,4},{6,7},{7,6},{8,9},{9,8},{10,11... | collective-permute-start | bytes 6291464 | tf_op jit(solution)/shard_map/ppermute | solution.py:321
  476.3 36.1 %collective-permute-start.73 = (f32[1,128]{1,0:T(1,128)S(1)}, f32[1,128]{1,0:T(1,128)S(1)}, u32[]{:S(2)}, u32[]{:S(2)}) collective-permute-start(f32[1,128]{1,0:T(1,128)S(1)} %add_add_fusion.8), channel_id=1, source_target_pairs={{0,2},{1,3},{2,0},{3,1},{4,6},{5,7},{6,4},{7,5},{8,10},{9,11},{10,... | collective-permute-start | bytes 1544 | tf_op jit(solution)/shard_map/ppermute | solution.py:337
  477.9 35.6 %collective-permute-start.74 = (f32[1,128]{1,0:T(1,128)S(1)}, f32[1,128]{1,0:T(1,128)S(1)}, u32[]{:S(2)}, u32[]{:S(2)}) collective-permute-start(f32[1,128]{1,0:T(1,128)S(1)} %add_add_fusion.8), channel_id=1, source_target_pairs={{0,1},{1,0},{2,3},{3,2},{4,5},{5,4},{6,7},{7,6},{8,9},{9,8},{10,11... | collective-permute-start | bytes 1544 | tf_op jit(solution)/shard_map/ppermute | solution.py:337
  477.9 39.0 %collective-permute-start.75 = (f32[1,128]{1,0:T(1,128)S(1)}, f32[1,128]{1,0:T(1,128)S(1)}, u32[]{:S(2)}, u32[]{:S(2)}) collective-permute-start(f32[1,128]{1,0:T(1,128)S(1)} %add_add_fusion.8), channel_id=1, source_target_pairs={{0,3},{1,2},{2,1},{3,0},{4,7},{5,6},{6,5},{7,4},{8,11},{9,10},{10,... | collective-permute-start | bytes 1544 | tf_op jit(solution)/shard_map/ppermute | solution.py:337
  (109 other events, 2060.2 us)

commit v2 on v1

v2 whole, which is shorter than its diff:
```python
import functools

import jax
import jax.numpy as jnp
from jax import lax
from jax.experimental import pallas as pl
from jax.experimental.pallas import tpu as pltpu
from jax.sharding import PartitionSpec as P

epsilon = 1e-06
bf16 = jnp.bfloat16
f32 = jnp.float32
PIECES = 8
MIB = 1024 * 1024
VMEM = pl.BlockSpec(memory_space=pltpu.VMEM)


def params(limit):
    return pltpu.CompilerParams(vmem_limit_bytes=limit * MIB)


def cost(flops=0, bytes_accessed=0, transcendentals=0):
    return pl.CostEstimate(flops=flops, bytes_accessed=bytes_accessed, transcendentals=transcendentals)


def hold(*values):
    return lax.optimization_barrier(values)


def col_stats_kernel(logits_ref, enable_ref, retain_ref, out_ref, top, total, dens):
    step = pl.program_id(0)

    @pl.when(step == 0)
    def _():
        top[...] = jnp.full_like(top, -1e29)
        total[...] = jnp.zeros_like(total)
        dens[...] = jnp.zeros_like(dens)

    rows, spots = logits_ref.shape
    enable = enable_ref[...].T
    retain = retain_ref[...].T
    blocks = []
    new = top[...]
    for k in range(rows // 128):
        block = jnp.where(enable[:, k : k + 1] > 0, logits_ref[128 * k : 128 * (k + 1), :], -1e30)
        blocks.append(block.reshape(16, 8, spots))
        new = jnp.maximum(new, jnp.max(blocks[-1], axis=0))
    shrink = jnp.exp(top[...] - new)
    top[...] = new
    sums = total[...] * shrink
    kept = dens[...] * shrink
    for k in range(rows // 128):
        part = jnp.exp(blocks[k] - new[None])
        share = jnp.broadcast_to(retain[:, k : k + 1], (128, spots)).reshape(16, 8, spots)
        sums = sums + jnp.sum(part, axis=0)
        kept = kept + jnp.sum(part * share, axis=0)
    total[...] = sums
    dens[...] = kept

    @pl.when(step == pl.num_programs(0) - 1)
    def _():
        best = jnp.max(new, axis=0, keepdims=True)
        scale = jnp.exp(new - best)
        out_ref[0:1, :] = best
        out_ref[1:2, :] = jnp.sum(sums * scale, axis=0, keepdims=True)
        out_ref[2:3, :] = jnp.sum(kept * scale, axis=0, keepdims=True)


def col_stats(logits, enable, retain, block=1024):
    cells, spots = logits.shape
    cell = pl.BlockSpec((block // 128, 128), lambda i: (i, 0))
    return pl.pallas_call(
        col_stats_kernel,
        grid=(cells // block,),
        in_specs=[pl.BlockSpec((block, spots), lambda i: (i, 0)), cell, cell],
        out_specs=pl.BlockSpec((3, spots), lambda i: (0, 0)),
        out_shape=jax.ShapeDtypeStruct((3, spots), f32),
        scratch_shapes=[pltpu.VMEM((8, spots), f32)] * 3,
        compiler_params=params(20),
        cost_estimate=cost(cells * spots * 8, cells * spots * 4, cells * spots),
        name="col_stats",
    )(logits, enable, retain)


def mapped_kernel(order_ref, logits_ref, enable_ref, retain_ref, shift_ref, out_ref):
    rows, spots = logits_ref.shape
    enable = enable_ref[...].T
    retain = retain_ref[...].T
    shift = shift_ref[...]
    for k in range(rows // 128):
        block = jnp.where(enable[:, k : k + 1] > 0, logits_ref[128 * k : 128 * (k + 1), :], -1e30)
        mapped = retain[:, k : k + 1] * jnp.exp(block - shift)
        out_ref[:, 128 * k : 128 * (k + 1)] = mapped.astype(bf16).T


def mapped_turned(order, logits, enable, retain, shift):
    cells, spots = logits.shape
    block = cells // PIECES
    cell = pl.BlockSpec((block // 128, 128), lambda i, order: (order[i], 0))
    return pl.pallas_call(
        mapped_kernel,
        grid_spec=pltpu.PrefetchScalarGridSpec(
            num_scalar_prefetch=1,
            grid=(PIECES,),
            in_specs=[
                pl.BlockSpec((block, spots), lambda i, order: (order[i], 0)),
                cell,
                cell,
                pl.BlockSpec((1, spots), lambda i, order: (0, 0)),
            ],
            out_specs=pl.BlockSpec((spots, block), lambda i, order: (0, i)),
        ),
        out_shape=jax.ShapeDtypeStruct((spots, cells), bf16),
        compiler_params=params(20),
        cost_estimate=cost(cells * spots * 6, cells * spots * 6, cells * spots),
        name="mapped_turned",
    )(order, logits, enable, retain, shift)


def forward_kernel(table, rows, mapped_ref, *refs):
    n = (len(refs) - 2) // 2
    own_refs, other_refs = refs[:n], refs[n : 2 * n]
    pred_ref, panel_ref = refs[2 * n :]
    total = None
    for r, (source, block) in enumerate(table):
        part = slice(block * rows, (block + 1) * rows)
        both = jnp.concatenate([own_refs[source][part, :], other_refs[source][part, :]], axis=1)
        here = slice(r * rows, (r + 1) * rows)
        panel_ref[here, :] = both
        more = jnp.dot(mapped_ref[:, here], both, preferred_element_type=f32)
        total = more if total is None else total + more
    pred_ref[...] = total


def forward(mapped, own, other, table, column, wide):
    spots, cells = mapped.shape
    rows = cells // PIECES
    specs = []
    for x in own:
        cut = x.shape[1] != wide
        specs.append(pl.BlockSpec((x.shape[0], wide), lambda i: (0, column)) if cut else VMEM)
    return pl.pallas_call(
        functools.partial(forward_kernel, table, rows),
        grid=(1,),
        in_specs=[VMEM] + specs + specs,
        out_specs=[VMEM, VMEM],
        out_shape=[
            jax.ShapeDtypeStruct((spots, 2 * wide), f32),
            pltpu.VMEM((cells, 2 * wide), bf16),
        ],
        compiler_params=params(12),
        cost_estimate=cost(4 * spots * cells * wide, 2 * cells * (spots + 4 * wide)),
        name="forward",
    )(mapped, *own, *other)


def stats_kernel(wide, near_ref, far_ref, own_ref, other_ref, pred_ref, gene_ref, spot_ref):
    pred = near_ref[...] + far_ref[...]
    pred_ref[...] = pred
    target = jnp.concatenate([own_ref[...], other_ref[...]], axis=1)
    terms = (pred * target, pred * pred, target * target)
    lane = lax.broadcasted_iota(jnp.int32, spot_ref.shape, 1)
    spot = jnp.zeros(spot_ref.shape, f32)
    for k, term in enumerate(terms):
        gene_ref[k : k + 1, :] = jnp.sum(term, axis=0, keepdims=True)
        spot = jnp.where(lane == k, jnp.sum(term, axis=1, keepdims=True), spot)
    spot_ref[...] = spot


def pred_stats(near, far, target_own, target_other, column, wide):
    spots = near.shape[0]
    whole = pl.BlockSpec((spots, 2 * wide), lambda i: (0, 0))
    part = pl.BlockSpec((spots, wide), lambda i: (0, column))
    return pl.pallas_call(
        functools.partial(stats_kernel, wide),
        grid=(1,),
        in_specs=[whole, whole, part, part],
        out_specs=[
            whole,
            pl.BlockSpec((3, 2 * wide), lambda i: (0, 0)),
            pl.BlockSpec((spots, 4), lambda i: (0, 0)),
        ],
        out_shape=[
            jax.ShapeDtypeStruct((spots, 2 * wide), f32),
            jax.ShapeDtypeStruct((3, 2 * wide), f32),
            jax.ShapeDtypeStruct((spots, 4), f32),
        ],
        compiler_params=params(16),
        cost_estimate=cost(spots * wide * 20, spots * wide * 40),
        name="pred_stats",
    )(near, far, target_own, target_other)


def grad_pred_kernel(widths, genes_total, spots_total, spot_ref, gene_ref, own_ref, other_ref, *refs):
    n = len(widths)
    pred_refs = refs[:n]
    turned_ref, inner_ref, sums_ref = refs[n:]
    spot = spot_ref[...]
    spot_pg, spot_pp, spot_gg = spot[:, 0:1], spot[:, 1:2], spot[:, 2:3]
    spot_scale = lax.rsqrt(spot_pp + epsilon) * lax.rsqrt(spot_gg + epsilon)
    spot_cos = spot_pg * spot_scale
    spot_back = spot_cos / (spot_pp + epsilon)
    gene = gene_ref[...]
    gene_scale = lax.rsqrt(gene[1:2, :] + epsilon) * lax.rsqrt(gene[2:3, :] + epsilon)
    gene_cos = gene[0:1, :] * gene_scale
    gene_back = gene_cos / (gene[1:2, :] + epsilon)
    folded = jnp.zeros((spot.shape[0], 128), f32)
    at = 0
    low = 0
    for q in range(n):
        wide = widths[q]
        pred = pred_refs[q][...]
        target = jnp.concatenate([own_ref[:, low : low + wide], other_ref[:, low : low + wide]], axis=1)
        cols = slice(at, at + 2 * wide)
        grad = -(target * gene_scale[:, cols] - gene_back[:, cols] * pred) / genes_total
        grad = grad - (target * spot_scale - spot_back * pred) / spots_total
        grad_low = grad.astype(bf16)
        turned_ref[at : at + 2 * wide, :] = grad_low.T
        prod = grad_low.astype(f32) * pred
        for k in range(0, 2 * wide, 128):
            folded = folded + prod[:, k : k + 128]
        at += 2 * wide
        low += wide
    inner_ref[...] = jnp.sum(folded.T, axis=0, keepdims=True)
    lane = lax.broadcasted_iota(jnp.int32, (1, 128), 1)
    gene_sum = jnp.sum(gene_cos, axis=1, keepdims=True)
    spot_sum = jnp.sum(spot_cos, axis=0, keepdims=True)
    sums_ref[...] = jnp.where(lane == 0, gene_sum, jnp.where(lane == 1, spot_sum, 0.0))


def grad_pred(widths, genes_total, spots_total, spot, gene, target_own, target_other, preds):
    spots, half = target_own.shape
    genes = 2 * half
    return pl.pallas_call(
        functools.partial(grad_pred_kernel, widths, genes_total, spots_total),
        in_specs=[VMEM] * (4 + len(preds)),
        out_specs=[VMEM] * 3,
        out_shape=[
            pltpu.VMEM((genes, spots), bf16),
            jax.ShapeDtypeStruct((1, spots), f32),
            jax.ShapeDtypeStruct((1, 128), f32),
        ],
        compiler_params=params(12),
        cost_estimate=cost(spots * genes * 14, spots * genes * 10),
        name="grad_pred",
    )(spot, gene, target_own, target_other, *preds)


def backward_kernel(widths, order_ref, logits_ref, enable_ref, retain_ref, col_ref, turned_ref, *refs):
    n = len(widths)
    panel_refs = refs[:n]
    grad_ref, row_ref = refs[n:]
    rows, spots = logits_ref.shape
    first = pl.multiple_of(pl.program_id(0) * rows, rows)
    enable = enable_ref[...].T
    retain = retain_ref[...].T
    shift, dens, inner = col_ref[0:1, :], col_ref[1:2, :], col_ref[2:3, :]
    part = rows // 2
    for h in range(2):
        here = pl.ds(first + h * part, part)
        panel = jnp.concatenate([ref[here, :] for ref in panel_refs], axis=1)
        grad_mapped = jnp.dot(panel, turned_ref[...], preferred_element_type=f32) + dens
        for k in range(part // 128):
            at = h * (part // 128) + k
            lines = slice(128 * at, 128 * (at + 1))
            block = jnp.where(enable[:, at : at + 1] > 0, logits_ref[lines, :], -1e30)
            mapping = jnp.exp(block - shift)
            grad = grad_mapped[128 * k : 128 * (k + 1), :]
            grad_ref[lines, :] = mapping * (retain[:, at : at + 1] * grad - inner)
            prod = grad * mapping
            folded = prod[:, 0:128]
            for c in range(128, spots, 128):
                folded = folded + prod[:, c : c + 128]
            row_ref[at : at + 1, :] = jnp.sum(folded.T, axis=0, keepdims=True)


def backward(order, logits, enable, retain, col, turned, panels):
    cells, spots = logits.shape
    genes = turned.shape[0]
    block = cells // PIECES
    widths = tuple(p.shape[1] for p in panels)
    cell = pl.BlockSpec((block // 128, 128), lambda i, order: (order[i], 0))
    return pl.pallas_call(
        functools.partial(backward_kernel, widths),
        grid_spec=pltpu.PrefetchScalarGridSpec(
            num_scalar_prefetch=1,
            grid=(PIECES,),
            in_specs=[
                pl.BlockSpec((block, spots), lambda i, order: (order[i], 0)),
                cell,
                cell,
                pl.BlockSpec((3, spots), lambda i, order: (0, 0)),
            ]
            + [VMEM] * (1 + len(panels)),
            out_specs=[pl.BlockSpec((block, spots), lambda i, order: (order[i], 0)), cell],
        ),
        out_shape=[
            jax.ShapeDtypeStruct((cells, spots), f32),
            jax.ShapeDtypeStruct((cells // 128, 128), f32),
        ],
        compiler_params=params(20),
        cost_estimate=cost(2 * cells * spots * genes, cells * 8 * spots, cells * spots),
        name="backward",
    )(order, logits, enable, retain, col, turned, *panels)


def stack_kernel(inside_ref, near_ref, mid1_ref, near2_ref, mid2_ref, near3_ref, *out_refs):
    rows = near_ref.shape[0]
    cut = out_refs[0].shape[1]
    inside = inside_ref[0] > 0
    for k, out in enumerate(out_refs):
        cols = slice(k * cut, (k + 1) * cut)
        out[0:rows, :] = near_ref[:, cols]

        @pl.when(inside)
        def _():
            out[rows : 2 * rows, :] = mid1_ref[:, cols]
            out[2 * rows : 3 * rows, :] = mid2_ref[:, cols]

        @pl.when(jnp.logical_not(inside))
        def _():
            out[rows : 2 * rows, :] = near2_ref[:, cols]
            out[2 * rows : 3 * rows, :] = near3_ref[:, cols]


def stack(inside, near, mid1, near2, mid2, near3, parts=1):
    rows, wide = near.shape
    return pl.pallas_call(
        stack_kernel,
        in_specs=[pl.BlockSpec(memory_space=pltpu.SMEM)] + [VMEM] * 5,
        out_specs=[VMEM] * parts,
        out_shape=[jax.ShapeDtypeStruct((3 * rows, wide // parts), bf16)] * parts,
        compiler_params=params(12),
        cost_estimate=cost(0, 12 * rows * wide),
        name="stack",
    )(inside, near, mid1, near2, mid2, near3)


def lay_kernel(core_ref, theirs_ref, *refs):
    out_ref = refs[-1]
    mine = pl.program_id(0) == core_ref[0]

    @pl.when(mine)
    def _():
        at = 0
        for ref in refs[:-1]:
            out_ref[:, at : at + ref.shape[1]] = ref[...]
            at += ref.shape[1]

    @pl.when(jnp.logical_not(mine))
    def _():
        out_ref[...] = theirs_ref[...]


def lay(core, theirs, preds):
    spots, half = theirs.shape
    return pl.pallas_call(
        lay_kernel,
        grid_spec=pltpu.PrefetchScalarGridSpec(
            num_scalar_prefetch=1,
            grid=(2,),
            in_specs=[pl.BlockSpec((spots, half), lambda i, core: (0, 0))]
            + [pl.BlockSpec((spots, p.shape[1] // 2), lambda i, core: (0, 0)) for p in preds],
            out_specs=pl.BlockSpec((spots, half), lambda i, core: (i, 0)),
        ),
        out_shape=jax.ShapeDtypeStruct((2 * spots, half), f32),
        compiler_params=params(20),
        cost_estimate=cost(0, spots * half * 16),
        name="lay",
    )(core, theirs, *preds)


def swap_cells(x):
    return lax.ppermute(x, "cells", [(0, 1), (1, 0)])


def swap_genes(x):
    return lax.ppermute(x, "genes", [(0, 1), (1, 0)])


def sum_spots_genes(x, mirror=lambda v: v):
    if lax.axis_size("spots") != 8:
        x = lax.psum(x, "spots")
        return x + mirror(swap_genes(x))
    moved = [lax.ppermute(x, "spots", [(i, i ^ d) for i in range(8)]) for d in (2, 4, 6)]
    x = (x + moved[0]) + (moved[1] + moved[2])
    pairs = [lax.ppermute(x, ("spots", "genes"), [(i, i ^ d) for i in range(16)]) for d in (1, 2, 3)]
    return (x + pairs[1]) + mirror(pairs[0] + pairs[2])


class Step:
    def __init__(self, logits, filter_logits, expression, spot_expression, cell_mask):
        self.logits = logits
        self.expression = expression
        self.core = lax.axis_index("genes")
        self.enable = cell_mask.astype(f32).reshape(-1, 128)
        self.retain = jax.nn.sigmoid(filter_logits).reshape(-1, 128)
        self.spots = logits.shape[1]
        mine = lax.dynamic_slice_in_dim(spot_expression, self.core * self.spots, self.spots, 0)
        theirs = lax.dynamic_slice_in_dim(spot_expression, (1 - self.core) * self.spots, self.spots, 0)
        self.target_own = mine
        self.target_sent = theirs
        self.half = expression.shape[1]

    def local_stats(self, logits):
        part = col_stats(logits, self.enable, self.retain)
        count = jnp.broadcast_to(jnp.sum(self.enable * self.retain), (1, self.spots))
        return jnp.concatenate([part, count], axis=0)

    def merge_stats(self, part, away):
        top = jnp.maximum(part[0], away[0])
        here, there = jnp.exp(part[0] - top), jnp.exp(away[0] - top)
        total = part[1] * here + away[1] * there
        self.density = (part[2] * here + away[2] * there) / total
        self.cell_count = part[3, 0] + away[3, 0]
        self.shift = (top + jnp.log(total))[None, :]

    def turned(self, order, shift):
        return mapped_turned(order, self.logits, self.enable, self.retain, shift)

    def stats(self, partial, away, at, wide):
        return pred_stats(partial, away, self.target_own, self.target_other, at // wide, wide)

    def gathered_whole(self):
        own = lax.all_gather(self.expression, "spots", axis=0, tiled=True)
        other = swap_genes(own)
        self.target_other = swap_genes(self.target_sent)
        part = self.local_stats(self.logits)
        self.merge_stats(part, swap_cells(part))
        order = jnp.arange(PIECES, dtype=jnp.int32)
        mapped = self.turned(order, self.shift)
        wide = self.half // 4
        table = tuple((0, r) for r in range(PIECES))
        chunks = []
        for q in range(4):
            cols = slice(q * wide, (q + 1) * wide)
            partial, panel = forward(mapped, [own[:, cols]], [other[:, cols]], table, 0, wide)
            chunks.append((wide, panel) + tuple(self.stats(partial, swap_cells(partial), q * wide, wide)))
        return order, chunks

    def gathered_line(self):
        near_pairs = [(2 * z + y, 2 * (z ^ 1) + y) for z in range(4) for y in range(2)]
        middle_pairs = [(2 * z + y, 2 * (3 - z) + y) for z in (1, 2) for y in range(2)]
        across_pairs = [(i, i ^ 1) for i in range(8)]

        def near(x):
            return lax.ppermute(x, "spots", near_pairs)

        def middle(x):
            return lax.ppermute(x, "spots", middle_pairs)

        def across(x):
            return lax.ppermute(x, "spots", across_pairs)

        spot = lax.axis_index("spots")
        z, y = spot // 2, spot % 2
        inside = (z == 1) | (z == 2)
        inside_flag = inside.astype(jnp.int32).reshape(1)
        column = jnp.stack([z, z ^ 1, jnp.where(z < 2, 2, 1), jnp.where(z < 2, 3, 0)])
        order = jnp.concatenate([2 * column + y, 2 * column + (1 - y)]).astype(jnp.int32)
        unit = self.half // 8
        expr = self.expression
        late_table = ((0, 0), (1, 0), (1, 1), (1, 2), (2, 0), (3, 0), (3, 1), (3, 2))
        split_table = ((0, 0), (1, 0), (1, 1), (2, 0), (3, 0), (4, 0), (4, 1), (5, 0))
        early_table = ((0, 0), (1, 0), (1, 2), (1, 4), (2, 0), (1, 1), (1, 3), (1, 5))

        def cut(x, at, wide):
            return x[:, at * unit : (at + wide) * unit]

        s0, s1 = cut(expr, 0, 2), cut(expr, 2, 2)
        a0, b0 = near(s0), middle(s0)
        beside = across(expr)
        a1, b1 = near(s1), middle(s1)
        expr_other = swap_genes(expr)
        part = self.local_stats(self.logits)
        a0, b0, part, target = hold(a0, b0, part, self.target_sent)
        a02, b02 = near(b0), middle(a0)
        away = swap_cells(part)
        target_other = swap_genes(target)
        s2, s3 = cut(expr, 4, 2), cut(expr, 6, 1)
        a1, b1, away, s2, s3, expr_other = hold(a1, b1, away, s2, s3, expr_other)
        a12, b12 = near(b1), middle(a1)
        self.merge_stats(part, away)
        mapped = self.turned(order, self.shift)
        a02, b02, mapped, self.target_other = hold(a02, b02, mapped, target_other)
        a03 = near(b02)
        nm0 = jnp.concatenate([a0, jnp.where(inside, b0, a02)], axis=0)
        y0nm = across(nm0)
        a12, b12, s2, nm0 = hold(a12, b12, s2, nm0)
        a13 = near(b12)
        a2, b2 = near(s2), middle(s2)
        nm0_other = swap_genes(nm0)
        a03, b02, s3 = hold(a03, b02, s3)
        f0 = jnp.where(inside, b02, a03)
        y0f = across(f0)
        f0_other = swap_genes(f0)
        a3, b3 = near(s3), middle(s3)
        a13, b12, beside, nm0_other = hold(a13, b12, beside, nm0_other)
        (rest1,) = stack(inside_flag, a1, b1, a12, b12, a13)
        y1 = across(rest1)
        rest1_other = swap_genes(rest1)
        beside_other = swap_genes(beside)
        sf = jnp.concatenate([cut(expr, 7, 1), cut(beside, 7, 1)], axis=0)
        a2, b2, y0nm, rest1, sf, f0_other = hold(a2, b2, y0nm, rest1, sf, f0_other)
        a22, b22 = near(b2), middle(a2)
        y0nm_other = swap_genes(y0nm)
        a3, b3, y0f, rest1_other = hold(a3, b3, y0f, rest1_other)
        a32, b32 = near(b3), middle(a3)
        y0f_other = swap_genes(y0f)
        a22, b22, y0f_other, y0nm_other, beside_other = hold(a22, b22, y0f_other, y0nm_other, beside_other)
        a23 = near(b22)
        partial0, panel0 = forward(
            mapped,
            [expr, nm0, f0, beside, y0nm, y0f],
            [expr_other, nm0_other, f0_other, beside_other, y0nm_other, y0f_other],
            split_table,
            0,
            2 * unit,
        )
        a32, b32, partial0, sf = hold(a32, b32, partial0, sf)
        a33 = near(b32)
        af, bf = near(sf), middle(sf)
        away0 = swap_cells(partial0)
        a23, b22 = hold(a23, b22)
        rest2, rest3 = stack(inside_flag, a2, b2, a22, b22, a23, parts=2)
        y2 = across(rest2)
        y3 = across(rest3)
        rest2_other, rest3_other = swap_genes(rest2), swap_genes(rest3)
        a33, y1, rest2 = hold(a33, y1, rest2)
        (rest4,) = stack(inside_flag, a3, b3, a32, b32, a33)
        y4 = across(rest4)
        rest4_other = swap_genes(rest4)
        y1_other = swap_genes(y1)
        af, bf, y1_other, rest4, rest2_other = hold(af, bf, y1_other, rest4, rest2_other)
        af2, bf2 = near(bf), middle(af)
        partial1, panel1 = forward(
            mapped,
            [expr, rest1, beside, y1],
            [expr_other, rest1_other, beside_other, y1_other],
            late_table,
            1,
            2 * unit,
        )
        af2, bf2, y2, partial1, away0 = hold(af2, bf2, y2, partial1, away0)
        af3 = near(bf2)
        away1 = swap_cells(partial1)
        y2_other = swap_genes(y2)
        stats0 = self.stats(partial0, away0, 0, 2 * unit)
        y2_other, rest3_other, rest4_other = hold(y2_other, rest3_other, rest4_other)
        partial2, panel2 = forward(
            mapped, [expr, rest2, beside, y2], [expr_other, rest2_other, beside_other, y2_other], late_table, 4, unit
        )
        y3, partial2 = hold(y3, partial2)
        away2 = swap_cells(partial2)
        y3_other = swap_genes(y3)
        af3, y3_other = hold(af3, y3_other)
        (restf,) = stack(inside_flag, af, bf, af2, bf2, af3)
        restf_other = swap_genes(restf)
        partial3, panel3 = forward(
            mapped, [expr, rest3, beside, y3], [expr_other, rest3_other, beside_other, y3_other], late_table, 5, unit
        )
        restf_other, partial3, away1 = hold(restf_other, partial3, away1)
        away3 = swap_cells(partial3)
        partialf, panelf = forward(
            mapped,
            [expr, restf, beside],
            [expr_other, restf_other, beside_other],
            early_table,
            7,
            unit,
        )
        y4, partialf = hold(y4, partialf)
        y4_other = swap_genes(y4)
        awayf = swap_cells(partialf)
        partial4, panel4 = forward(
            mapped, [expr, rest4, beside, y4], [expr_other, rest4_other, beside_other, y4_other], late_table, 6, unit
        )
        away4 = swap_cells(partial4)
        chunks = [(2 * unit, panel0) + tuple(stats0)]
        rows = [
            (partial1, away1, 2, 2, panel1),
            (partial2, away2, 4, 1, panel2),
            (partial3, away3, 5, 1, panel3),
            (partial4, away4, 6, 1, panel4),
            (partialf, awayf, 7, 1, panelf),
        ]
        for partial, away, at, wide, panel in rows:
            chunks.append((wide * unit, panel) + tuple(self.stats(partial, away, at * unit, wide * unit)))
        return order, chunks


def body(logits, filter_logits, expression, spot_expression, cell_mask, spot_counts):
    cells_total = logits.shape[0] * lax.axis_size("cells")
    spots = logits.shape[1]
    spots_total = spots * lax.axis_size("spots") * lax.axis_size("genes")
    genes_total = expression.shape[1] * lax.axis_size("genes")
    step = Step(logits, filter_logits, expression, spot_expression, cell_mask)
    order, chunks = step.gathered_line() if lax.axis_size("spots") == 8 else step.gathered_whole()
    widths, panels, preds, gene_stats, spot_stats = zip(*chunks)
    density = step.density

    counts = spot_counts.astype(f32)
    kl_parts = jnp.stack([jnp.sum(density), jnp.sum(counts * (jnp.log(counts) - jnp.log(density))), jnp.sum(counts)])

    def mirrored(some):
        def mirror(v):
            out, at = [], 0
            for wide in some:
                out += [v[:, at + wide : at + 2 * wide], v[:, at : at + wide]]
                at += 2 * wide
            return jnp.concatenate(out + [v[:, at:]], axis=1)

        return mirror

    early = len(widths) // 2
    early_sum = sum_spots_genes(
        jnp.concatenate(gene_stats[:early] + (jnp.broadcast_to(kl_parts[:, None], (3, 128)),), axis=1),
        mirrored(widths[:early]),
    )
    late_sum = sum_spots_genes(jnp.concatenate(gene_stats[early:], axis=1), mirrored(widths[early:]))
    split = 2 * sum(widths[:early])
    gene = jnp.concatenate([early_sum[:, :split], late_sum], axis=1)
    dens_total, kl_part, count_total = early_sum[0, split], early_sum[1, split], early_sum[2, split]
    kl_term = kl_part / count_total - jnp.log(count_total) + jnp.log(dens_total)
    offset = (step.cell_count - 0.5 * cells_total) / cells_total
    penalty = jnp.sqrt(offset * offset + 0.01)
    dens_grad = -counts / (count_total * density) + 1.0 / dens_total
    spot = functools.reduce(jnp.add, spot_stats)

    turned, inner, sums = grad_pred(
        widths, genes_total, spots_total, spot, gene, step.target_own, step.target_other, preds
    )
    theirs = swap_genes(jnp.concatenate([p[:, w:] for p, w in zip(preds, widths)], axis=1))
    col = jnp.concatenate([step.shift, dens_grad[None], inner + (density * dens_grad)[None]], axis=0)
    grad_logits, row = backward(order, logits, step.enable, step.retain, col, turned, panels)

    row_sums = sum_spots_genes(jnp.concatenate([row, sums], axis=0))
    copies = lax.axis_size("spots") * lax.axis_size("genes")
    gene_sum, spot_sum = row_sums[-1, 0] / copies, row_sums[-1, 1]
    total_loss = -gene_sum / genes_total - spot_sum / spots_total + kl_term + penalty
    retain_grad = row_sums[:-1] + step.enable * offset / (penalty * cells_total)
    filter_grad = (retain_grad * step.retain * (1.0 - step.retain)).reshape(-1)

    predicted = lay(step.core.astype(jnp.int32).reshape(1), theirs, preds)
    return (predicted, total_loss, grad_logits, filter_grad)


def solution(mesh):
    placed = (
        P("cells", ("spots", "genes")),
        P("cells"),
        P(("cells", "spots"), "genes"),
        P("spots", "genes"),
        P("cells"),
        P(("spots", "genes")),
    )
    return jax.shard_map(
        body,
        mesh=mesh,
        in_specs=placed,
        out_specs=(P("spots", "genes"), P(), P("cells", ("spots", "genes")), P("cells")),
        check_vma=False,
    )
```

time: 536 us -> 407 us (0.76)
  Pallas kernels: 142 us -> 91.7 us
  waiting for transfers between devices: 213 us -> 164 us
  starting transfers between devices: 108 us -> 82.6 us
  other arithmetic: 27.9 us -> 7.66 us
  local copies, waits for them, and re-layouts: 32.6 us -> 50.4 us
    ppermute x36 -> x32, waiting for transfers between devices: 158 us -> 105 us  [the longest x15 86.3 us: near(): return lax.ppermute(x, 'spots', near_pairs)]
    pallas_call x6 -> x11, Pallas kernels: 64.3 us -> 34.1 us  [the longest x6 27.1 us: forward(): pl.pallas_call(functools.partial(forward_kernel, table, rows), grid=(1,),...]
    unnamed x124 -> x121, local copies, waits for them, and re-layouts: 21.6 us -> 39 us
    ppermute x7, waiting for transfers between devices: 33.3 us -> 46.9 us  [swap_cells(): return lax.ppermute(x, 'cells', [(0, 1), (1, 0)])]
    ppermute x15 -> x9, starting transfers between devices: 25.2 us -> 13.3 us  [sum_spots_genes(): lax.ppermute(x, 'spots', [(i, i ^ d) for i in range(8)])]
    ppermute x36 -> x32, starting transfers between devices: 62.5 us -> 51.4 us  [the longest x15 35.1 us: near(): return lax.ppermute(x, 'spots', near_pairs)]
    concatenate x9 -> x6, other arithmetic: 9.36 us -> 0.21 us  [the longest x1 0.08 us: gathered_line(): jnp.concatenate([2 * column + y, 2 * column + (1 - y)]).astype(jnp.int32)]
    ppermute x15 -> x9, waiting for transfers between devices: 14.6 us -> 5.93 us  [sum_spots_genes(): lax.ppermute(x, 'spots', [(i, i ^ d) for i in range(8)])]
  transfers between devices with their start and end apart: 88 -> 74, of which waited for: 29 -> 25; matrix products, arithmetic and copies ran while one was open for 6% -> 5% of each run, Pallas kernels for 24% -> 21%
where the time goes in v2:
time: 407 us; the launch traced here: 405 us
  waiting for transfers between devices  164 us (40%)
  Pallas kernels  91.7 us (23%)
  starting transfers between devices  82.6 us (20%)
  local copies, waits for them, and re-layouts  50.4 us (12%)
  between operations  8.84 us (2%)
  other arithmetic  7.66 us (2%)
    ppermute x15, waiting for transfers between devices, near(): return lax.ppermute(x, 'spots', near_pairs)  86.3 us
    ppermute x7, waiting for transfers between devices, swap_cells(): return lax.ppermute(x, 'cells', [(0, 1), (1, 0)])  46.9 us
    unnamed x121, local copies, waits for them, and re-layouts  39 us
    ppermute x15, starting transfers between devices, near(): return lax.ppermute(x, 'spots', near_pairs)  35.1 us
    pallas_call x1, Pallas kernels, backward(): pl.pallas_call(functools.partial(backward_kernel, widths), grid_spec=pltp...  27.1 us
    pallas_call x6, Pallas kernels, forward(): pl.pallas_call(functools.partial(forward_kernel, table, rows), grid=(1,),...  27.1 us
    ppermute x7, waiting for transfers between devices, across(): return lax.ppermute(x, 'spots', across_pairs)  19.1 us
    ppermute x9, starting transfers between devices, sum_spots_genes(): lax.ppermute(x, 'spots', [(i, i ^ d) for i in range(8)])  13.3 us
  transfers between devices with their start and end apart: 74, of which 25 were waited for; matrix products, arithmetic and copies ran while one was open for 5% of the time, Pallas kernels for 21%

profile of v2, /device:TPU:0, one launch (start us, length us, event | category | flops | bytes accessed | tf_op | source)
XLA Modules:
  0.0 405.5 jit_solution(8049355702638748153)
XLA Ops:
  7.7 5.8 %copy-done.3 = f32[8192,512]{1,0:T(8,128)S(1)} copy-done((f32[8192,512]{1,0:T(8,128)S(1)}, f32[8192,512]{1,0:T(8,128)}, u32[]{:S(2)}) %copy-start.3) | copy-done | bytes 16777240
  13.4 6.5 %col_stats.1 = f32[3,512]{1,0:T(4,128)S(1)} custom-call(f32[8192,512]{1,0:T(8,128)S(1)} %copy-done.3, f32[64,128]{1,0:T(8,128)S(1)} %convert_bitcast_fusion.enable_ref, f32[64,128]{1,0:T(8,128)S(1)} %get-tuple-element.238.retain_ref), custom_call_target="tpu_custom_call" | custom-call | flops 33554432 | bytes 16777216 | tf_op jit(solution)/shard_map/col_stats/pallas_call | solution.py:72
  22.8 4.4 %collective-permute-start.4 = (bf16[1024,256]{1,0:T(8,128)(2,1)}, bf16[1024,256]{1,0:T(8,128)(2,1)}, u32[]{:S(2)}, u32[]{:S(2)}) collective-permute-start(bf16[1024,256]{1,0:T(8,128)(2,1)} %get-tuple-element.233), channel_id=1, source_target_pairs={{0,4},{2,6},{4,0},{6,2},{8,12},{10,14},{12,8},{14,10},{1,5},{3,7},... | collective-permute-start | bytes 1572872 | tf_op jit(solution)/shard_map/ppermute | solution.py:447
  30.2 9.4 %collective-permute-done.4.near_ref = bf16[1024,256]{1,0:T(8,128)(2,1)} collective-permute-done((bf16[1024,256]{1,0:T(8,128)(2,1)}, bf16[1024,256]{1,0:T(8,128)(2,1)}, u32[]{:S(2)}, u32[]{:S(2)}) %collective-permute-start.4) | collective-permute-done | bytes 524320 | tf_op jit(solution)/shard_map/ppermute | solution.py:447
  48.9 5.7 %collective-permute-done.2 = bf16[1024,256]{1,0:T(8,128)(2,1)} collective-permute-done((bf16[1024,256]{1,0:T(8,128)(2,1)S(1)}, bf16[1024,256]{1,0:T(8,128)(2,1)}, u32[]{:S(2)}, u32[]{:S(2)}) %collective-permute-start.2) | collective-permute-done | bytes 524320 | tf_op jit(solution)/shard_map/ppermute | solution.py:447
  57.5 5.8 %copy-done.4 = f32[8192,512]{1,0:T(8,128)S(1)} copy-done((f32[8192,512]{1,0:T(8,128)S(1)}, f32[8192,512]{1,0:T(8,128)}, u32[]{:S(2)}) %copy-start.4) | copy-done | bytes 16777240
  63.2 11.1 %mapped_turned.1.mapped_ref = bf16[512,8192]{1,0:T(8,128)(2,1)S(1)} custom-call(s32[8]{0:T(128)S(1)} %pad_add_fusion.order_ref, f32[8192,512]{1,0:T(8,128)S(1)} %copy-done.4, f32[64,128]{1,0:T(8,128)S(1)} %convert_bitcast_fusion.enable_ref, f32[64,128]{1,0:T(8,128)S(1)} %get-tuple-element.238.retain_ref, f32[1,512]{1,0:T(1,128)S(1)} %get-tuple-element.243.shift_ref), custom_call_target="tpu_custom_call" | custom-call | flops 25165824 | bytes 25165824 | tf_op jit(solution)/shard_map/mapped_turned/pallas_call | solution.py:100
  84.3 11.2 %collective-permute-done.9 = bf16[1024,256]{1,0:T(8,128)(2,1)S(1)} collective-permute-done((bf16[1024,256]{1,0:T(8,128)(2,1)S(1)}, bf16[1024,256]{1,0:T(8,128)(2,1)S(1)}, u32[]{:S(2)}, u32[]{:S(2)}) %collective-permute-start.9) | collective-permute-done | bytes 524320 | tf_op jit(solution)/shard_map/ppermute | solution.py:447
  98.2 8.7 %collective-permute-done.15.near3_ref = bf16[1024,256]{1,0:T(8,128)(2,1)} collective-permute-done((bf16[1024,256]{1,0:T(8,128)(2,1)}, bf16[1024,256]{1,0:T(8,128)(2,1)}, u32[]{:S(2)}, u32[]{:S(2)}) %collective-permute-start.15) | collective-permute-done | bytes 524320 | tf_op jit(solution)/shard_map/ppermute | solution.py:447
  110.3 7.2 %collective-permute-done.21.near_ref = bf16[1024,256]{1,0:T(8,128)(2,1)} collective-permute-done((bf16[1024,256]{1,0:T(8,128)(2,1)}, bf16[1024,256]{1,0:T(8,128)(2,1)}, u32[]{:S(2)}, u32[]{:S(2)}) %collective-permute-start.21) | collective-permute-done | bytes 524320 | tf_op jit(solution)/shard_map/ppermute | solution.py:447
  121.9 5.6 %collective-permute-done.10.near_ref = bf16[1024,128]{1,0:T(8,128)(2,1)S(1)} collective-permute-done((bf16[1024,128]{1,0:T(8,128)(2,1)S(1)}, bf16[1024,128]{1,0:T(8,128)(2,1)S(1)}, u32[]{:S(2)}, u32[]{:S(2)}) %collective-permute-start.10) | collective-permute-done | bytes 262176 | tf_op jit(solution)/shard_map/ppermute | solution.py:447
  127.4 3.6 collective-permute-start.25
  134.0 8.2 %collective-permute-done.25.near2_ref = bf16[1024,256]{1,0:T(8,128)(2,1)S(1)} collective-permute-done((bf16[1024,256]{1,0:T(8,128)(2,1)S(1)}, bf16[1024,256]{1,0:T(8,128)(2,1)S(1)}, u32[]{:S(2)}, u32[]{:S(2)}) %collective-permute-start.25) | collective-permute-done | bytes 524320 | tf_op jit(solution)/shard_map/ppermute | solution.py:447
  142.3 7.9 %collective-permute-start.19 = (bf16[1024,128]{1,0:T(8,128)(2,1)S(1)}, bf16[1024,128]{1,0:T(8,128)(2,1)S(1)}, u32[]{:S(2)}, u32[]{:S(2)}) collective-permute-start(bf16[1024,128]{1,0:T(8,128)(2,1)S(1)} %collective-permute-done.11.mid1_ref), channel_id=1, source_target_pairs={{0,4},{2,6},{4,0},{6,2},{8,12},{10,14},{12,8},{14,10},{1,5},{3,7},... | collective-permute-start | bytes 786440 | tf_op jit(solution)/shard_map/ppermute | solution.py:447
  157.3 6.8 %forward.6 = (f32[512,512]{1,0:T(8,128)S(1)}, bf16[8192,512]{1,0:T(8,128)(2,1)S(1)}) custom-call(bf16[512,8192]{1,0:T(8,128)(2,1)S(1)} %copy-done.1, bf16[1024,1024]{1,0:T(8,128)(2,1)} %refs_0_.11, bf16[2048,256]{1,0:T(8,128)(2,1)S(1)} %pad_maximum_fusion.refs_1_, bf16[1024,256]{1,0:T(8,128)(2,1)S(1)} %broadcast_select_fusion.1.refs_2_, ...), custom_call_target="tpu_custom_call" | custom-call | flops 4294967296 | bytes 25165824 | tf_op jit(solution)/shard_map/forward/pallas_call | solution.py:142
  168.8 5.0 %collective-permute-done.32.near3_ref = bf16[1024,128]{1,0:T(8,128)(2,1)S(1)} collective-permute-done((bf16[1024,128]{1,0:T(8,128)(2,1)S(1)}, bf16[1024,128]{1,0:T(8,128)(2,1)S(1)}, u32[]{:S(2)}, u32[]{:S(2)}) %collective-permute-start.32) | collective-permute-done | bytes 262176 | tf_op jit(solution)/shard_map/ppermute | solution.py:447
  176.8 11.3 %collective-permute-done.30.near_ref = bf16[2048,128]{1,0:T(8,128)(2,1)S(1)} collective-permute-done((bf16[2048,128]{1,0:T(8,128)(2,1)S(1)}, bf16[2048,128]{1,0:T(8,128)(2,1)S(1)}, u32[]{:S(2)}, u32[]{:S(2)}) %collective-permute-start.30) | collective-permute-done | bytes 524320 | tf_op jit(solution)/shard_map/ppermute | solution.py:447
  192.7 5.9 %forward.7 = (f32[512,512]{1,0:T(8,128)S(1)}, bf16[8192,512]{1,0:T(8,128)(2,1)S(1)}) custom-call(bf16[512,8192]{1,0:T(8,128)(2,1)S(1)} %copy-done.2, bf16[1024,1024]{1,0:T(8,128)(2,1)} %refs_0_.11, bf16[3072,256]{1,0:T(8,128)(2,1)S(1)} %stack.40.refs_1_, bf16[1024,1024]{1,0:T(8,128)(2,1)} %collective-permute-done.16.refs_3_.refs_2_, ...), custom_call_target="tpu_custom_call" | custom-call | flops 4294967296 | bytes 25165824 | tf_op jit(solution)/shard_map/forward/pallas_call | solution.py:142
  202.4 4.3 %collective-permute-done.39.refs_3_ = bf16[3072,128]{1,0:T(8,128)(2,1)S(1)} collective-permute-done((bf16[3072,128]{1,0:T(8,128)(2,1)S(1)}, bf16[3072,128]{1,0:T(8,128)(2,1)S(1)}, u32[]{:S(2)}, u32[]{:S(2)}) %collective-permute-start.39) | collective-permute-done | bytes 786464 | tf_op jit(solution)/shard_map/ppermute | solution.py:453
  209.0 3.5 forward.8
  212.6 14.1 %collective-permute-done.42.refs_3_ = bf16[3072,128]{1,0:T(8,128)(2,1)S(1)} collective-permute-done((bf16[3072,128]{1,0:T(8,128)(2,1)S(1)}, bf16[3072,128]{1,0:T(8,128)(2,1)S(1)}, u32[]{:S(2)}, u32[]{:S(2)}) %collective-permute-start.42) | collective-permute-done | bytes 786464 | tf_op jit(solution)/shard_map/ppermute | solution.py:453
  227.2 14.0 %collective-permute-done.41.near3_ref = bf16[2048,128]{1,0:T(8,128)(2,1)S(1)} collective-permute-done((bf16[2048,128]{1,0:T(8,128)(2,1)S(1)}, bf16[2048,128]{1,0:T(8,128)(2,1)S(1)}, u32[]{:S(2)}, u32[]{:S(2)}) %collective-permute-start.41) | collective-permute-done | bytes 524320 | tf_op jit(solution)/shard_map/ppermute | solution.py:447
  249.0 29.1 %collective-permute-done.49.far_ref = f32[512,256]{1,0:T(8,128)S(1)} collective-permute-done((f32[512,256]{1,0:T(8,128)S(1)}, f32[512,256]{1,0:T(8,128)S(1)}, u32[]{:S(2)}, u32[]{:S(2)}) %collective-permute-start.49) | collective-permute-done | bytes 524320 | tf_op jit(solution)/shard_map/ppermute | solution.py:374
  279.5 3.7 forward.9
  291.3 3.5 forward.10
  306.5 3.6 forward.11
  313.6 9.3 %collective-permute-done.54.far_ref = f32[512,256]{1,0:T(8,128)S(1)} collective-permute-done((f32[512,256]{1,0:T(8,128)S(1)}, f32[512,256]{1,0:T(8,128)S(1)}, u32[]{:S(2)}, u32[]{:S(2)}) %collective-permute-start.54) | collective-permute-done | bytes 524320 | tf_op jit(solution)/shard_map/ppermute | solution.py:374
  325.2 8.5 %collective-permute-done.53.far_ref = f32[512,256]{1,0:T(8,128)S(1)} collective-permute-done((f32[512,256]{1,0:T(8,128)S(1)}, f32[512,256]{1,0:T(8,128)S(1)}, u32[]{:S(2)}, u32[]{:S(2)}) %collective-permute-start.53) | collective-permute-done | bytes 524320 | tf_op jit(solution)/shard_map/ppermute | solution.py:374
  347.2 4.5 %grad_pred.1 = (bf16[2048,512]{1,0:T(8,128)(2,1)S(1)}, f32[1,512]{1,0:T(1,128)S(1)}, f32[1,128]{1,0:T(1,128)S(1)}) custom-call(f32[512,4]{1,0:T(8,128)S(1)} %add_add_fusion.spot_ref, f32[3,2048]{1,0:T(4,128)S(1)} %pad_maximum_fusion.2.gene_ref, f32[512,1024]{1,0:T(8,128)S(1)} %get-tuple-element.228.own_ref, f32[512,1024]{1,0:T(8,128)} %collective-permute-done.8.other_ref, ...), custom_call_target="tpu_custom_call" | custom-call | flops 14680064 | bytes 10485760 | tf_op jit(solution)/shard_map/grad_pred/pallas_call | solution.py:234
  351.8 27.1 %backward.1 = (f32[8192,512]{1,0:T(8,128)}, f32[64,128]{1,0:T(8,128)S(1)}) custom-call(s32[8]{0:T(128)S(1)} %pad_add_fusion.order_ref, f32[8192,512]{1,0:T(8,128)} %logits_ref.5, f32[64,128]{1,0:T(8,128)S(1)} %convert_bitcast_fusion.enable_ref, f32[64,128]{1,0:T(8,128)S(1)} %get-tuple-element.238.retain_ref, f32[3,512]{1,0:T(4,128)S(1)} %pad_maximum_fusion.4.col_ref, ...), custom_call_target="tpu_custom_call" | custom-call | flops 17179869184 | bytes 33554432 | tf_op jit(solution)/shard_map/backward/pallas_call | solution.py:283
  384.2 3.7 collective-permute-done.70
  400.5 3.8 lay.1
  (303 shorter events, 134.0 us)
Async XLA Ops:
  3.2 19.0 %collective-permute-start = (bf16[1024,256]{1,0:T(8,128)(2,1)}, bf16[1024,256]{1,0:T(8,128)(2,1)S(1)}, u32[]{:S(2)}, u32[]{:S(2)}) collective-permute-start(bf16[1024,256]{1,0:T(8,128)(2,1)} %get-tuple-element.234), channel_id=1, source_target_pairs={{0,4},{2,6},{4,0},{6,2},{8,12},{10,14},{12,8},{14,10},{1,5},{3,7},... | collective-permute-start | bytes 1572872 | tf_op jit(solution)/shard_map/ppermute | solution.py:447
  6.2 16.0 %collective-permute-start.1 = (bf16[1024,256]{1,0:T(8,128)(2,1)}, bf16[1024,256]{1,0:T(8,128)(2,1)S(1)}, u32[]{:S(2)}, u32[]{:S(2)}) collective-permute-start(bf16[1024,256]{1,0:T(8,128)(2,1)} %get-tuple-element.234), channel_id=1, source_target_pairs={{4,8},{6,10},{8,4},{10,6},{5,9},{7,11},{9,5},{11,7},{20,24},{22,26... | collective-permute-start | bytes 1572872 | tf_op jit(solution)/shard_map/ppermute | solution.py:450
  6.9 38.5 %collective-permute-start.7 = (bf16[1024,1024]{1,0:T(8,128)(2,1)}, bf16[1024,1024]{1,0:T(8,128)(2,1)}, u32[]{:S(2)}, u32[]{:S(2)}) collective-permute-start(bf16[1024,1024]{1,0:T(8,128)(2,1)} %refs_0_.11), channel_id=1, source_target_pairs={{0,1},{1,0},{2,3},{3,2},{4,5},{5,4},{6,7},{7,6},{8,9},{9,8},{10,11... | collective-permute-start | bytes 6291464 | tf_op jit(solution)/shard_map/ppermute | solution.py:378
  22.2 55.5 %collective-permute-start.8 = (f32[512,1024]{1,0:T(8,128)}, f32[512,1024]{1,0:T(8,128)}, u32[]{:S(2)}, u32[]{:S(2)}) collective-permute-start(f32[512,1024]{1,0:T(8,128)} %get-tuple-element.116), channel_id=1, source_target_pairs={{0,1},{1,0},{2,3},{3,2},{4,5},{5,4},{6,7},{7,6},{8,9},{9,8},{10,11... | collective-permute-start | bytes 6291464 | tf_op jit(solution)/shard_map/ppermute | solution.py:378
  22.8 16.9 %collective-permute-start.4 = (bf16[1024,256]{1,0:T(8,128)(2,1)}, bf16[1024,256]{1,0:T(8,128)(2,1)}, u32[]{:S(2)}, u32[]{:S(2)}) collective-permute-start(bf16[1024,256]{1,0:T(8,128)(2,1)} %get-tuple-element.233), channel_id=1, source_target_pairs={{0,4},{2,6},{4,0},{6,2},{8,12},{10,14},{12,8},{14,10},{1,5},{3,7},... | collective-permute-start | bytes 1572872 | tf_op jit(solution)/shard_map/ppermute | solution.py:447
  41.4 56.1 %collective-permute-start.16 = (bf16[1024,1024]{1,0:T(8,128)(2,1)}, bf16[1024,1024]{1,0:T(8,128)(2,1)}, u32[]{:S(2)}, u32[]{:S(2)}) collective-permute-start(bf16[1024,1024]{1,0:T(8,128)(2,1)} %refs_0_.11), channel_id=1, source_target_pairs={{0,2},{2,0},{4,6},{6,4},{8,10},{10,8},{12,14},{14,12},{1,3},{3,1},... | collective-permute-start | bytes 6291464 | tf_op jit(solution)/shard_map/ppermute | solution.py:453
  42.9 34.8 %collective-permute-start.3 = (bf16[1024,256]{1,0:T(8,128)(2,1)}, bf16[1024,256]{1,0:T(8,128)(2,1)S(1)}, u32[]{:S(2)}, u32[]{:S(2)}) collective-permute-start(bf16[1024,256]{1,0:T(8,128)(2,1)} %copy-done.35), channel_id=1, source_target_pairs={{4,8},{6,10},{8,4},{10,6},{5,9},{7,11},{9,5},{11,7},{20,24},{22,26... | collective-permute-start | bytes 1572872 | tf_op jit(solution)/shard_map/ppermute | solution.py:450
  45.5 34.3 %collective-permute-start.13 = (bf16[1024,256]{1,0:T(8,128)(2,1)}, bf16[1024,256]{1,0:T(8,128)(2,1)S(1)}, u32[]{:S(2)}, u32[]{:S(2)}) collective-permute-start(bf16[1024,256]{1,0:T(8,128)(2,1)} %collective-permute-done.5.mid1_ref), channel_id=1, source_target_pairs={{0,4},{2,6},{4,0},{6,2},{8,12},{10,14},{12,8},{14,10},{1,5},{3,7},... | collective-permute-start | bytes 1572872 | tf_op jit(solution)/shard_map/ppermute | solution.py:447
  54.6 26.0 %collective-permute-start.14 = (bf16[1024,256]{1,0:T(8,128)(2,1)}, bf16[1024,256]{1,0:T(8,128)(2,1)}, u32[]{:S(2)}, u32[]{:S(2)}) collective-permute-start(bf16[1024,256]{1,0:T(8,128)(2,1)} %collective-permute-done.4.near_ref), channel_id=1, source_target_pairs={{4,8},{6,10},{8,4},{10,6},{5,9},{7,11},{9,5},{11,7},{20,24},{22,26... | collective-permute-start | bytes 1572872 | tf_op jit(solution)/shard_map/ppermute | solution.py:450
  80.5 26.3 %collective-permute-start.17 = (bf16[2048,256]{1,0:T(8,128)(2,1)S(1)}, bf16[2048,256]{1,0:T(8,128)(2,1)}, u32[]{:S(2)}, u32[]{:S(2)}) collective-permute-start(bf16[2048,256]{1,0:T(8,128)(2,1)S(1)} %pad_maximum_fusion.refs_1_), channel_id=1, source_target_pairs={{0,1},{1,0},{2,3},{3,2},{4,5},{5,4},{6,7},{7,6},{8,9},{9,8},{10,11... | collective-permute-start | bytes 3145736 | tf_op jit(solution)/shard_map/ppermute | solution.py:378
  81.9 24.9 %collective-permute-start.15 = (bf16[1024,256]{1,0:T(8,128)(2,1)}, bf16[1024,256]{1,0:T(8,128)(2,1)}, u32[]{:S(2)}, u32[]{:S(2)}) collective-permute-start(bf16[1024,256]{1,0:T(8,128)(2,1)} %collective-permute-done.14.mid2_ref), channel_id=1, source_target_pairs={{0,4},{2,6},{4,0},{6,2},{8,12},{10,14},{12,8},{14,10},{1,5},{3,7},... | collective-permute-start | bytes 1572872 | tf_op jit(solution)/shard_map/ppermute | solution.py:447
  82.8 36.2 %collective-permute-start.23 = (bf16[2048,256]{1,0:T(8,128)(2,1)S(1)}, bf16[2048,256]{1,0:T(8,128)(2,1)}, u32[]{:S(2)}, u32[]{:S(2)}) collective-permute-start(bf16[2048,256]{1,0:T(8,128)(2,1)S(1)} %pad_maximum_fusion.refs_1_), channel_id=1, source_target_pairs={{0,2},{2,0},{4,6},{6,4},{8,10},{10,8},{12,14},{14,12},{1,3},{3,1},... | collective-permute-start | bytes 3145736 | tf_op jit(solution)/shard_map/ppermute | solution.py:453
  96.3 21.1 %collective-permute-start.21 = (bf16[1024,256]{1,0:T(8,128)(2,1)}, bf16[1024,256]{1,0:T(8,128)(2,1)}, u32[]{:S(2)}, u32[]{:S(2)}) collective-permute-start(bf16[1024,256]{1,0:T(8,128)(2,1)} %get-tuple-element.135), channel_id=1, source_target_pairs={{0,4},{2,6},{4,0},{6,2},{8,12},{10,14},{12,8},{14,10},{1,5},{3,7},... | collective-permute-start | bytes 1572872 | tf_op jit(solution)/shard_map/ppermute | solution.py:447
  97.5 20.0 %collective-permute-start.22 = (bf16[1024,256]{1,0:T(8,128)(2,1)}, bf16[1024,256]{1,0:T(8,128)(2,1)S(1)}, u32[]{:S(2)}, u32[]{:S(2)}) collective-permute-start(bf16[1024,256]{1,0:T(8,128)(2,1)} %get-tuple-element.135), channel_id=1, source_target_pairs={{4,8},{6,10},{8,4},{10,6},{5,9},{7,11},{9,5},{11,7},{20,24},{22,26... | collective-permute-start | bytes 1572872 | tf_op jit(solution)/shard_map/ppermute | solution.py:450
  109.7 23.7 %collective-permute-start.18 = (bf16[3072,256]{1,0:T(8,128)(2,1)S(1)}, bf16[3072,256]{1,0:T(8,128)(2,1)S(1)}, u32[]{:S(2)}, u32[]{:S(2)}) collective-permute-start(bf16[3072,256]{1,0:T(8,128)(2,1)S(1)} %stack.40.refs_1_), channel_id=1, source_target_pairs={{0,1},{1,0},{2,3},{3,2},{4,5},{5,4},{6,7},{7,6},{8,9},{9,8},{10,11... | collective-permute-start | bytes 4718600 | tf_op jit(solution)/shard_map/ppermute | solution.py:378
  109.7 41.1 %collective-permute-start.29 = (bf16[1024,1024]{1,0:T(8,128)(2,1)}, bf16[1024,1024]{1,0:T(8,128)(2,1)S(1)}, u32[]{:S(2)}, u32[]{:S(2)}) collective-permute-start(bf16[1024,1024]{1,0:T(8,128)(2,1)} %collective-permute-done.16.refs_3_.refs_2_), channel_id=1, source_target_pairs={{0,1},{1,0},{2,3},{3,2},{4,5},{5,4},{6,7},{7,6},{8,9},{9,8},{10,11... | collective-permute-start | bytes 6291464 | tf_op jit(solution)/shard_map/ppermute | solution.py:378
  127.4 22.7 %collective-permute-start.28 = (bf16[2048,256]{1,0:T(8,128)(2,1)}, bf16[2048,256]{1,0:T(8,128)(2,1)S(1)}, u32[]{:S(2)}, u32[]{:S(2)}) collective-permute-start(bf16[2048,256]{1,0:T(8,128)(2,1)} %collective-permute-done.23.refs_4_), channel_id=1, source_target_pairs={{0,1},{1,0},{2,3},{3,2},{4,5},{5,4},{6,7},{7,6},{8,9},{9,8},{10,11... | collective-permute-start | bytes 3145736 | tf_op jit(solution)/shard_map/ppermute | solution.py:378
  131.8 36.9 %collective-permute-start.33 = (bf16[3072,256]{1,0:T(8,128)(2,1)S(1)}, bf16[3072,256]{1,0:T(8,128)(2,1)S(1)}, u32[]{:S(2)}, u32[]{:S(2)}) collective-permute-start(bf16[3072,256]{1,0:T(8,128)(2,1)S(1)} %stack.40.refs_1_), channel_id=1, source_target_pairs={{0,2},{2,0},{4,6},{6,4},{8,10},{10,8},{12,14},{14,12},{1,3},{3,1},... | collective-permute-start | bytes 4718600 | tf_op jit(solution)/shard_map/ppermute | solution.py:453
  142.3 25.1 %collective-permute-start.19 = (bf16[1024,128]{1,0:T(8,128)(2,1)S(1)}, bf16[1024,128]{1,0:T(8,128)(2,1)S(1)}, u32[]{:S(2)}, u32[]{:S(2)}) collective-permute-start(bf16[1024,128]{1,0:T(8,128)(2,1)S(1)} %collective-permute-done.11.mid1_ref), channel_id=1, source_target_pairs={{0,4},{2,6},{4,0},{6,2},{8,12},{10,14},{12,8},{14,10},{1,5},{3,7},... | collective-permute-start | bytes 786440 | tf_op jit(solution)/shard_map/ppermute | solution.py:447
  150.1 17.2 %collective-permute-start.20 = (bf16[1024,128]{1,0:T(8,128)(2,1)S(1)}, bf16[1024,128]{1,0:T(8,128)(2,1)S(1)}, u32[]{:S(2)}, u32[]{:S(2)}) collective-permute-start(bf16[1024,128]{1,0:T(8,128)(2,1)S(1)} %collective-permute-done.10.near_ref), channel_id=1, source_target_pairs={{4,8},{6,10},{8,4},{10,6},{5,9},{7,11},{9,5},{11,7},{20,24},{22,26... | collective-permute-start | bytes 786440 | tf_op jit(solution)/shard_map/ppermute | solution.py:450
  150.8 16.6 %collective-permute-start.34 = (bf16[1024,256]{1,0:T(8,128)(2,1)S(1)}, bf16[1024,256]{1,0:T(8,128)(2,1)S(1)}, u32[]{:S(2)}, u32[]{:S(2)}) collective-permute-start(bf16[1024,256]{1,0:T(8,128)(2,1)S(1)} %collective-permute-done.26.mid2_ref), channel_id=1, source_target_pairs={{0,4},{2,6},{4,0},{6,2},{8,12},{10,14},{12,8},{14,10},{1,5},{3,7},... | collective-permute-start | bytes 1572872 | tf_op jit(solution)/shard_map/ppermute | solution.py:447
  175.2 26.7 %collective-permute-start.40 = (f32[512,512]{1,0:T(8,128)S(1)}, f32[512,512]{1,0:T(8,128)S(1)}, u32[]{:S(2)}, u32[]{:S(2)}) collective-permute-start(f32[512,512]{1,0:T(8,128)S(1)} %get-tuple-element.148.near_ref), channel_id=1, source_target_pairs={{0,16},{16,0},{1,17},{17,1},{2,18},{18,2},{3,19},{19,3},{4,20},{20... | collective-permute-start | bytes 3145736 | tf_op jit(solution)/shard_map/ppermute | solution.py:374
  188.1 18.6 %collective-permute-start.39 = (bf16[3072,128]{1,0:T(8,128)(2,1)S(1)}, bf16[3072,128]{1,0:T(8,128)(2,1)S(1)}, u32[]{:S(2)}, u32[]{:S(2)}) collective-permute-start(bf16[3072,128]{1,0:T(8,128)(2,1)S(1)} %get-tuple-element.172.refs_1_), channel_id=1, source_target_pairs={{0,2},{2,0},{4,6},{6,4},{8,10},{10,8},{12,14},{14,12},{1,3},{3,1},... | collective-permute-start | bytes 2359304 | tf_op jit(solution)/shard_map/ppermute | solution.py:453
  188.7 18.0 %collective-permute-start.37 = (bf16[2048,128]{1,0:T(8,128)(2,1)S(1)}, bf16[2048,128]{1,0:T(8,128)(2,1)S(1)}, u32[]{:S(2)}, u32[]{:S(2)}) collective-permute-start(bf16[2048,128]{1,0:T(8,128)(2,1)S(1)} %collective-permute-done.31.mid1_ref), channel_id=1, source_target_pairs={{0,4},{2,6},{4,0},{6,2},{8,12},{10,14},{12,8},{14,10},{1,5},{3,7},... | collective-permute-start | bytes 1572872 | tf_op jit(solution)/shard_map/ppermute | solution.py:447
  206.7 20.0 %collective-permute-start.42 = (bf16[3072,128]{1,0:T(8,128)(2,1)S(1)}, bf16[3072,128]{1,0:T(8,128)(2,1)S(1)}, u32[]{:S(2)}, u32[]{:S(2)}) collective-permute-start(bf16[3072,128]{1,0:T(8,128)(2,1)S(1)} %get-tuple-element.171.refs_1_), channel_id=1, source_target_pairs={{0,2},{2,0},{4,6},{6,4},{8,10},{10,8},{12,14},{14,12},{1,3},{3,1},... | collective-permute-start | bytes 2359304 | tf_op jit(solution)/shard_map/ppermute | solution.py:453
  241.3 44.0 %collective-permute-start.47 = (bf16[6144,128]{1,0:T(8,128)(2,1)S(1)}, bf16[6144,128]{1,0:T(8,128)(2,1)S(1)}, u32[]{:S(2)}, u32[]{:S(2)}) collective-permute-start(bf16[6144,128]{1,0:T(8,128)(2,1)S(1)} %stack.43.refs_1_), channel_id=1, source_target_pairs={{0,1},{1,0},{2,3},{3,2},{4,5},{5,4},{6,7},{7,6},{8,9},{9,8},{10,11... | collective-permute-start | bytes 4718600 | tf_op jit(solution)/shard_map/ppermute | solution.py:378
  241.3 43.9 %collective-permute-start.48 = (f32[512,512]{1,0:T(8,128)S(1)}, f32[512,512]{1,0:T(8,128)S(1)}, u32[]{:S(2)}, u32[]{:S(2)}) collective-permute-start(f32[512,512]{1,0:T(8,128)S(1)} %get-tuple-element.168.near_ref), channel_id=1, source_target_pairs={{0,16},{16,0},{1,17},{17,1},{2,18},{18,2},{3,19},{19,3},{4,20},{20... | collective-permute-start | bytes 3145736 | tf_op jit(solution)/shard_map/ppermute | solution.py:374
  242.9 35.3 %collective-permute-start.49 = (f32[512,256]{1,0:T(8,128)S(1)}, f32[512,256]{1,0:T(8,128)S(1)}, u32[]{:S(2)}, u32[]{:S(2)}) collective-permute-start(f32[512,256]{1,0:T(8,128)S(1)} %get-tuple-element.184.near_ref), channel_id=1, source_target_pairs={{0,16},{16,0},{1,17},{17,1},{2,18},{18,2},{3,19},{19,3},{4,20},{20... | collective-permute-start | bytes 1572872 | tf_op jit(solution)/shard_map/ppermute | solution.py:374
  246.1 50.7 %collective-permute-start.51 = (bf16[3072,128]{1,0:T(8,128)(2,1)S(1)}, bf16[3072,128]{1,0:T(8,128)(2,1)S(1)}, u32[]{:S(2)}, u32[]{:S(2)}) collective-permute-start(bf16[3072,128]{1,0:T(8,128)(2,1)S(1)} %stack.42.refs_1_), channel_id=1, source_target_pairs={{0,2},{2,0},{4,6},{6,4},{8,10},{10,8},{12,14},{14,12},{1,3},{3,1},... | collective-permute-start | bytes 2359304 | tf_op jit(solution)/shard_map/ppermute | solution.py:453
  299.3 23.6 %collective-permute-start.54 = (f32[512,256]{1,0:T(8,128)S(1)}, f32[512,256]{1,0:T(8,128)S(1)}, u32[]{:S(2)}, u32[]{:S(2)}) collective-permute-start(f32[512,256]{1,0:T(8,128)S(1)} %get-tuple-element.195.near_ref), channel_id=1, source_target_pairs={{0,16},{16,0},{1,17},{17,1},{2,18},{18,2},{3,19},{19,3},{4,20},{20... | collective-permute-start | bytes 1572872 | tf_op jit(solution)/shard_map/ppermute | solution.py:374
  310.1 23.6 %collective-permute-start.53 = (f32[512,256]{1,0:T(8,128)S(1)}, f32[512,256]{1,0:T(8,128)S(1)}, u32[]{:S(2)}, u32[]{:S(2)}) collective-permute-start(f32[512,256]{1,0:T(8,128)S(1)} %get-tuple-element.193.near_ref), channel_id=1, source_target_pairs={{0,16},{16,0},{1,17},{17,1},{2,18},{18,2},{3,19},{19,3},{4,20},{20... | collective-permute-start | bytes 1572872 | tf_op jit(solution)/shard_map/ppermute | solution.py:374
  341.1 57.3 %collective-permute-start.55 = (f32[512,1024]{1,0:T(8,128)}, f32[512,1024]{1,0:T(8,128)}, u32[]{:S(2)}, u32[]{:S(2)}) collective-permute-start(f32[512,1024]{1,0:T(8,128)} %slice_dynamic-update-slice_fusion.2), channel_id=1, source_target_pairs={{0,1},{1,0},{2,3},{3,2},{4,5},{5,4},{6,7},{7,6},{8,9},{9,8},{10,11... | collective-permute-start | bytes 6291464 | tf_op jit(solution)/shard_map/ppermute | solution.py:378
  (94 other events, 1201.9 us)

commit v3 on v2

v3 whole, which is shorter than its diff:
```python
import functools

import jax
import jax.numpy as jnp
from jax import lax
from jax.experimental import pallas as pl
from jax.experimental.pallas import tpu as pltpu
from jax.sharding import PartitionSpec as P

epsilon = 1e-06
bf16 = jnp.bfloat16
f32 = jnp.float32
PIECES = 8
MIB = 1024 * 1024
VMEM = pl.BlockSpec(memory_space=pltpu.VMEM)


def params(limit):
    return pltpu.CompilerParams(vmem_limit_bytes=limit * MIB)


def cost(flops=0, bytes_accessed=0, transcendentals=0):
    return pl.CostEstimate(flops=1, bytes_accessed=1, transcendentals=0)


def in_hbm(x):
    return pltpu.with_memory_space_constraint(x, pltpu.HBM)


def hold(*values):
    return lax.optimization_barrier(values)


def col_stats_kernel(logits_ref, enable_ref, retain_ref, out_ref, top, total, dens):
    step = pl.program_id(0)

    @pl.when(step == 0)
    def _():
        top[...] = jnp.full_like(top, -1e29)
        total[...] = jnp.zeros_like(total)
        dens[...] = jnp.zeros_like(dens)

    rows, spots = logits_ref.shape
    enable = enable_ref[...].T
    retain = retain_ref[...].T
    blocks = []
    new = top[...]
    for k in range(rows // 128):
        block = jnp.where(enable[:, k : k + 1] > 0, logits_ref[128 * k : 128 * (k + 1), :], -1e30)
        blocks.append(block.reshape(16, 8, spots))
        new = jnp.maximum(new, jnp.max(blocks[-1], axis=0))
    shrink = jnp.exp(top[...] - new)
    top[...] = new
    sums = total[...] * shrink
    kept = dens[...] * shrink
    for k in range(rows // 128):
        part = jnp.exp(blocks[k] - new[None])
        share = jnp.broadcast_to(retain[:, k : k + 1], (128, spots)).reshape(16, 8, spots)
        sums = sums + jnp.sum(part, axis=0)
        kept = kept + jnp.sum(part * share, axis=0)
    total[...] = sums
    dens[...] = kept

    @pl.when(step == pl.num_programs(0) - 1)
    def _():
        best = jnp.max(new, axis=0, keepdims=True)
        scale = jnp.exp(new - best)
        out_ref[0:1, :] = best
        out_ref[1:2, :] = jnp.sum(sums * scale, axis=0, keepdims=True)
        out_ref[2:3, :] = jnp.sum(kept * scale, axis=0, keepdims=True)


def col_stats(logits, enable, retain, block=1024):
    cells, spots = logits.shape
    cell = pl.BlockSpec((block // 128, 128), lambda i: (i, 0))
    return pl.pallas_call(
        col_stats_kernel,
        grid=(cells // block,),
        in_specs=[pl.BlockSpec((block, spots), lambda i: (i, 0)), cell, cell],
        out_specs=pl.BlockSpec((3, spots), lambda i: (0, 0)),
        out_shape=jax.ShapeDtypeStruct((3, spots), f32),
        scratch_shapes=[pltpu.VMEM((8, spots), f32)] * 3,
        compiler_params=params(20),
        cost_estimate=cost(cells * spots * 8, cells * spots * 4, cells * spots),
        name="col_stats",
    )(logits, enable, retain)


def mapped_kernel(order_ref, logits_ref, enable_ref, retain_ref, shift_ref, out_ref):
    rows, spots = logits_ref.shape
    enable = enable_ref[...].T
    retain = retain_ref[...].T
    shift = shift_ref[...]
    for k in range(rows // 128):
        block = jnp.where(enable[:, k : k + 1] > 0, logits_ref[128 * k : 128 * (k + 1), :], -1e30)
        mapped = retain[:, k : k + 1] * jnp.exp(block - shift)
        out_ref[:, 128 * k : 128 * (k + 1)] = mapped.astype(bf16).T


def mapped_turned(order, logits, enable, retain, shift):
    cells, spots = logits.shape
    block = cells // PIECES
    cell = pl.BlockSpec((block // 128, 128), lambda i, order: (order[i], 0))
    return pl.pallas_call(
        mapped_kernel,
        grid_spec=pltpu.PrefetchScalarGridSpec(
            num_scalar_prefetch=1,
            grid=(PIECES,),
            in_specs=[
                pl.BlockSpec((block, spots), lambda i, order: (order[i], 0)),
                cell,
                cell,
                pl.BlockSpec((1, spots), lambda i, order: (0, 0)),
            ],
            out_specs=pl.BlockSpec((spots, block), lambda i, order: (0, i)),
        ),
        out_shape=pltpu.HBM((spots, cells), bf16),
        compiler_params=params(20),
        cost_estimate=cost(cells * spots * 6, cells * spots * 6, cells * spots),
        name="mapped_turned",
    )(order, logits, enable, retain, shift)


def forward_kernel(table, kinds, columns, rows, wide, core_ref, mapped_ref, *refs):
    sources, at = [], 0
    for kind in kinds:
        sources.append(refs[at : at + kind])
        at += kind
    pred_ref, panel_ref, held, turned, first_sems, second_sems, mapped_sems, panel_sems = refs[at:]

    def piece(r, which, column, sems):
        source, block = table[r]
        cols = pl.ds(columns[source] * wide, wide)
        if kinds[source] == 1:
            ref = sources[source][0]
            row = which * (ref.shape[0] // 2) + block * rows
        else:
            ref = sources[source][which]
            row = block * rows
        target = held.at[pl.ds(r * rows, rows), pl.ds(column, wide)]
        return pltpu.make_async_copy(ref.at[pl.ds(row, rows), cols], target, sems.at[r])

    def load(r):
        cols = pl.ds(r * rows, rows)
        return pltpu.make_async_copy(mapped_ref.at[:, cols], turned.at[:, cols], mapped_sems.at[r])

    def save(r):
        here = pl.ds(r * rows, rows)
        return pltpu.make_async_copy(held.at[here, :], panel_ref.at[here, :], panel_sems.at[r])

    for r in range(PIECES):
        if kinds[table[r][0]] == 1:
            piece(r, 0, 0, first_sems).start()
            piece(r, 1, wide, second_sems).start()
        else:
            for core in range(2):

                @pl.when(core_ref[0] == core)
                def _(core=core, r=r):
                    piece(r, 0, core * wide, first_sems).start()
                    piece(r, 1, (1 - core) * wide, second_sems).start()

        load(r).start()
    total = None
    for r in range(PIECES):
        piece(r, 0, 0, first_sems).wait()
        piece(r, 1, 0, second_sems).wait()
        save(r).start()
        load(r).wait()
        here = slice(r * rows, (r + 1) * rows)
        more = jnp.dot(turned[:, here], held[here, :], preferred_element_type=f32)
        total = more if total is None else total + more
    pred_ref[...] = total
    for r in range(PIECES):
        save(r).wait()


def forward(core, mapped, sources, table, columns, wide):
    spots, cells = mapped.shape
    rows = cells // PIECES
    sources = [x if isinstance(x, tuple) else (x,) for x in sources]
    arrays = [in_hbm(x) for source in sources for x in source]
    hbm = pl.BlockSpec(memory_space=pltpu.HBM)
    return pl.pallas_call(
        functools.partial(forward_kernel, table, [len(x) for x in sources], columns, rows, wide),
        in_specs=[pl.BlockSpec(memory_space=pltpu.SMEM), hbm] + [hbm] * len(arrays),
        out_specs=[VMEM, hbm],
        out_shape=[
            jax.ShapeDtypeStruct((spots, 2 * wide), f32),
            pltpu.HBM((cells, 2 * wide), bf16),
        ],
        scratch_shapes=[pltpu.VMEM((cells, 2 * wide), bf16), pltpu.VMEM((spots, cells), bf16)]
        + [pltpu.SemaphoreType.DMA((PIECES,))] * 4,
        compiler_params=params(14 + 16 * wide // 512),
        cost_estimate=cost(4 * spots * cells * wide, 2 * cells * (spots + 4 * wide)),
        name="forward",
    )(core, in_hbm(mapped), *arrays)


def stats_kernel(parts, core_ref, *refs):
    own_ref, other_ref, pred_ref, gene_ref, spot_ref = refs[parts:]
    pred = functools.reduce(jnp.add, [ref[...] for ref in refs[:parts]])
    pred_ref[...] = pred
    target = jnp.concatenate([own_ref[...], other_ref[...]], axis=1)
    terms = (pred * target, pred * pred, target * target)
    lane = lax.broadcasted_iota(jnp.int32, spot_ref.shape, 1)
    spot = jnp.zeros(spot_ref.shape, f32)
    for k, term in enumerate(terms):
        gene_ref[k : k + 1, :] = jnp.sum(term, axis=0, keepdims=True)
        spot = jnp.where(lane == k, jnp.sum(term, axis=1, keepdims=True), spot)
    spot_ref[...] = spot


def pred_stats(core, parts, target, column, wide):
    spots = parts[0].shape[0]
    whole = pl.BlockSpec((spots, 2 * wide), lambda i, core: (0, 0))
    return pl.pallas_call(
        functools.partial(stats_kernel, len(parts)),
        grid_spec=pltpu.PrefetchScalarGridSpec(
            num_scalar_prefetch=1,
            grid=(1,),
            in_specs=[whole] * len(parts)
            + [
                pl.BlockSpec((spots, wide), lambda i, core: (core[0], column)),
                pl.BlockSpec((spots, wide), lambda i, core: (2 + core[0], column)),
            ],
            out_specs=[
                whole,
                pl.BlockSpec((3, 2 * wide), lambda i, core: (0, 0)),
                pl.BlockSpec((spots, 4), lambda i, core: (0, 0)),
            ],
        ),
        out_shape=[
            jax.ShapeDtypeStruct((spots, 2 * wide), f32),
            jax.ShapeDtypeStruct((3, 2 * wide), f32),
            jax.ShapeDtypeStruct((spots, 4), f32),
        ],
        compiler_params=params(16),
        cost_estimate=cost(spots * wide * 20, spots * wide * 40),
        name="pred_stats",
    )(core, *parts, target, target)


def grad_pred_kernel(widths, genes_total, spots_total, core_ref, spot_ref, gene_ref, own_ref, other_ref, *refs):
    n = len(widths)
    pred_refs = refs[:n]
    turned_ref, inner_ref, sums_ref = refs[n:]
    spot = spot_ref[...]
    spot_pg, spot_pp, spot_gg = spot[:, 0:1], spot[:, 1:2], spot[:, 2:3]
    spot_scale = lax.rsqrt(spot_pp + epsilon) * lax.rsqrt(spot_gg + epsilon)
    spot_cos = spot_pg * spot_scale
    spot_back = spot_cos / (spot_pp + epsilon)
    gene = gene_ref[:, : 2 * sum(widths)]
    gene_scale = lax.rsqrt(gene[1:2, :] + epsilon) * lax.rsqrt(gene[2:3, :] + epsilon)
    gene_cos = gene[0:1, :] * gene_scale
    gene_back = gene_cos / (gene[1:2, :] + epsilon)
    folded = jnp.zeros((spot.shape[0], 128), f32)
    at = 0
    low = 0
    for q in range(n):
        wide = widths[q]
        pred = pred_refs[q][...]
        target = jnp.concatenate([own_ref[:, low : low + wide], other_ref[:, low : low + wide]], axis=1)
        cols = slice(at, at + 2 * wide)
        grad = -(target * gene_scale[:, cols] - gene_back[:, cols] * pred) / genes_total
        grad = grad - (target * spot_scale - spot_back * pred) / spots_total
        grad_low = grad.astype(bf16)
        turned_ref[at : at + 2 * wide, :] = grad_low.T
        prod = grad_low.astype(f32) * pred
        for k in range(0, 2 * wide, 128):
            folded = folded + prod[:, k : k + 128]
        at += 2 * wide
        low += wide
    inner_ref[...] = jnp.sum(folded.T, axis=0, keepdims=True)
    lane = lax.broadcasted_iota(jnp.int32, (1, 128), 1)
    gene_sum = jnp.sum(gene_cos, axis=1, keepdims=True)
    spot_sum = jnp.sum(spot_cos, axis=0, keepdims=True)
    sums_ref[...] = jnp.where(lane == 0, gene_sum, jnp.where(lane == 1, spot_sum, 0.0))


def grad_pred(core, widths, genes_total, spots_total, spot, gene, target, preds):
    spots = spot.shape[0]
    half = target.shape[1]
    genes = 2 * half
    return pl.pallas_call(
        functools.partial(grad_pred_kernel, widths, genes_total, spots_total),
        grid_spec=pltpu.PrefetchScalarGridSpec(
            num_scalar_prefetch=1,
            grid=(1,),
            in_specs=[VMEM] * 2
            + [
                pl.BlockSpec((spots, half), lambda i, core: (core[0], 0)),
                pl.BlockSpec((spots, half), lambda i, core: (2 + core[0], 0)),
            ]
            + [VMEM] * len(preds),
            out_specs=[VMEM] * 3,
        ),
        out_shape=[
            pltpu.VMEM((genes, spots), bf16),
            jax.ShapeDtypeStruct((1, spots), f32),
            jax.ShapeDtypeStruct((1, 128), f32),
        ],
        compiler_params=params(22),
        cost_estimate=cost(spots * genes * 14, spots * genes * 10),
        name="grad_pred",
    )(core, spot, gene, target, target, *preds)


def backward_kernel(widths, order_ref, logits_ref, enable_ref, retain_ref, col_ref, turned_ref, *refs):
    n = len(widths)
    panel_refs = refs[:n]
    grad_ref, row_ref = refs[n:]
    rows, spots = logits_ref.shape
    first = pl.multiple_of(pl.program_id(0) * rows, rows)
    enable = enable_ref[...].T
    retain = retain_ref[...].T
    shift, dens, inner = col_ref[0:1, :], col_ref[1:2, :], col_ref[2:3, :]
    part = rows // 2
    for h in range(2):
        here = pl.ds(first + h * part, part)
        panel = jnp.concatenate([ref[here, :] for ref in panel_refs], axis=1)
        grad_mapped = jnp.dot(panel, turned_ref[...], preferred_element_type=f32) + dens
        for k in range(part // 128):
            at = h * (part // 128) + k
            lines = slice(128 * at, 128 * (at + 1))
            block = jnp.where(enable[:, at : at + 1] > 0, logits_ref[lines, :], -1e30)
            mapping = jnp.exp(block - shift)
            grad = grad_mapped[128 * k : 128 * (k + 1), :]
            grad_ref[lines, :] = mapping * (retain[:, at : at + 1] * grad - inner)
            prod = grad * mapping
            folded = prod[:, 0:128]
            for c in range(128, spots, 128):
                folded = folded + prod[:, c : c + 128]
            row_ref[at : at + 1, :] = jnp.sum(folded.T, axis=0, keepdims=True)


def backward(order, logits, enable, retain, col, turned, panels):
    cells, spots = logits.shape
    genes = turned.shape[0]
    block = cells // PIECES
    widths = tuple(p.shape[1] for p in panels)
    cell = pl.BlockSpec((block // 128, 128), lambda i, order: (order[i], 0))
    return pl.pallas_call(
        functools.partial(backward_kernel, widths),
        grid_spec=pltpu.PrefetchScalarGridSpec(
            num_scalar_prefetch=1,
            grid=(PIECES,),
            in_specs=[
                pl.BlockSpec((block, spots), lambda i, order: (order[i], 0)),
                cell,
                cell,
                pl.BlockSpec((3, spots), lambda i, order: (0, 0)),
            ]
            + [VMEM] * (1 + len(panels)),
            out_specs=[pl.BlockSpec((block, spots), lambda i, order: (order[i], 0)), cell],
        ),
        out_shape=[
            jax.ShapeDtypeStruct((cells, spots), f32),
            jax.ShapeDtypeStruct((cells // 128, 128), f32),
        ],
        compiler_params=params(20),
        cost_estimate=cost(2 * cells * spots * genes, cells * 8 * spots, cells * spots),
        name="backward",
    )(order, logits, enable, retain, col, turned, *panels)


def join_kernel(*refs):
    at = 0
    for ref in refs[:-1]:
        refs[-1][at : at + ref.shape[0], :] = ref[...]
        at += ref.shape[0]


def join(*parts):
    rows = sum(p.shape[0] for p in parts)
    return pl.pallas_call(
        join_kernel,
        in_specs=[VMEM] * len(parts),
        out_specs=VMEM,
        out_shape=jax.ShapeDtypeStruct((rows, parts[0].shape[1]), bf16),
        compiler_params=params(12),
        cost_estimate=cost(0, 4 * rows * parts[0].shape[1]),
        name="join",
    )(*parts)


def select_kernel(inside_ref, middle_ref, end_ref, *out_refs):
    cut = out_refs[0].shape[1]
    for k, out in enumerate(out_refs):
        for flag, ref in ((1, middle_ref), (0, end_ref)):

            @pl.when(inside_ref[0] == flag)
            def _(out=out, ref=ref, k=k):
                out[...] = ref[:, k * cut : (k + 1) * cut]


def select(inside, middle, end, parts=1):
    rows, wide = middle.shape
    return pl.pallas_call(
        select_kernel,
        in_specs=[pl.BlockSpec(memory_space=pltpu.SMEM)] + [VMEM] * 2,
        out_specs=[VMEM] * parts,
        out_shape=[jax.ShapeDtypeStruct((rows, wide // parts), bf16)] * parts,
        compiler_params=params(12),
        cost_estimate=cost(0, 4 * rows * wide),
        name="select",
    )(inside, middle, end)


def lay_kernel(core_ref, theirs_ref, *refs):
    out_ref = refs[-1]
    mine = pl.program_id(0) == core_ref[0]

    @pl.when(mine)
    def _():
        at = 0
        for ref in refs[:-1]:
            out_ref[:, at : at + ref.shape[1]] = ref[...]
            at += ref.shape[1]

    @pl.when(jnp.logical_not(mine))
    def _():
        out_ref[...] = theirs_ref[...]


def lay(core, theirs, preds):
    spots, half = theirs.shape
    return pl.pallas_call(
        lay_kernel,
        grid_spec=pltpu.PrefetchScalarGridSpec(
            num_scalar_prefetch=1,
            grid=(2,),
            in_specs=[pl.BlockSpec((spots, half), lambda i, core: (0, 0))]
            + [pl.BlockSpec((spots, p.shape[1] // 2), lambda i, core: (0, core[0])) for p in preds],
            out_specs=pl.BlockSpec((spots, half), lambda i, core: (i, 0)),
        ),
        out_shape=jax.ShapeDtypeStruct((2 * spots, half), f32),
        compiler_params=params(20),
        cost_estimate=cost(0, spots * half * 16),
        name="lay",
    )(core, theirs, *preds)


def swap_cells(x):
    return lax.ppermute(x, "cells", [(0, 1), (1, 0)])


def swap_genes(x):
    return lax.ppermute(x, "genes", [(0, 1), (1, 0)])


def sum_spots_genes(x):
    if lax.axis_size("spots") != 8:
        return lax.psum(x, ("spots", "genes"))
    moved = [lax.ppermute(x, "spots", [(i, i ^ d) for i in range(8)]) for d in (2, 4, 6)]
    x = (x + moved[0]) + (moved[1] + moved[2])
    pairs = [lax.ppermute(x, ("spots", "genes"), [(i, i ^ d) for i in range(16)]) for d in (1, 2, 3)]
    return (x + pairs[0]) + (pairs[1] + pairs[2])


def both_genes(x):
    return lax.all_gather(x, "genes", axis=0, tiled=True)


class Step:
    def __init__(self, logits, filter_logits, expression, spot_expression, cell_mask):
        self.logits = pltpu.with_memory_space_constraint(logits, pltpu.HBM)
        self.expression = expression
        self.core = lax.axis_index("genes")
        self.enable = cell_mask.astype(f32).reshape(-1, 128)
        self.retain = jax.nn.sigmoid(filter_logits).reshape(-1, 128)
        self.spots = logits.shape[1]
        self.target = both_genes(spot_expression)
        self.core_flag = self.core.astype(jnp.int32).reshape(1)
        self.half = expression.shape[1]

    def local_stats(self):
        part = col_stats(self.logits, self.enable, self.retain)
        count = jnp.broadcast_to(jnp.sum(self.enable * self.retain), (1, self.spots))
        return jnp.concatenate([part, count], axis=0)

    def merge_stats(self, part, away):
        top = jnp.maximum(part[0], away[0])
        here, there = jnp.exp(part[0] - top), jnp.exp(away[0] - top)
        total = part[1] * here + away[1] * there
        self.density = (part[2] * here + away[2] * there) / total
        self.cell_count = part[3, 0] + away[3, 0]
        self.shift = (top + jnp.log(total))[None, :]

    def turned(self, order, shift, logits):
        return mapped_turned(order, logits, self.enable, self.retain, shift)

    def stats(self, parts, at, wide):
        return pred_stats(self.core_flag, parts, self.target, at // wide, wide)

    def gathered_whole(self):
        own = lax.all_gather(self.expression, "spots", axis=0, tiled=True)
        other = swap_genes(own)
        part = self.local_stats()
        self.merge_stats(part, swap_cells(part))
        order = jnp.arange(PIECES, dtype=jnp.int32)
        mapped = self.turned(order, self.shift, self.logits)
        wide = self.half // 4
        table = tuple((0, r) for r in range(PIECES))
        chunks = []
        for q in range(4):
            partial, panel = forward(self.core_flag, mapped, [(own, other)], table, [q], wide)
            chunks.append((wide, panel) + tuple(self.stats([lax.psum(partial, "cells")], q * wide, wide)))
        return order, chunks

    def gathered_line(self):
        near_pairs = [(2 * z + y, 2 * (z ^ 1) + y) for z in range(4) for y in range(2)]
        middle_pairs = [(2 * z + y, 2 * (3 - z) + y) for z in (1, 2) for y in range(2)]
        across_pairs = [(i, i ^ 1) for i in range(8)]

        def near(x):
            return lax.ppermute(x, "spots", near_pairs)

        def middle(x):
            return lax.ppermute(x, "spots", middle_pairs)

        def across(x):
            return lax.ppermute(x, "spots", across_pairs)

        spot = lax.axis_index("spots")
        z, y = spot // 2, spot % 2
        inside = (z == 1) | (z == 2)
        inside_flag = inside.astype(jnp.int32).reshape(1)
        column = jnp.stack([z, z ^ 1, jnp.where(z < 2, 2, 1), jnp.where(z < 2, 3, 0)])
        order = jnp.concatenate([2 * column + y, 2 * column + (1 - y)]).astype(jnp.int32)
        unit = self.half // 8
        expr = self.expression

        def cut(x, at, wide):
            return x[:, at * unit : (at + wide) * unit]

        def pick(middle, end, parts=1):
            return select(inside_flag, middle, end, parts)

        first = ((0, 0), (1, 0), (2, 0), (2, 1), (3, 0), (4, 0), (5, 0), (5, 1))
        second = ((0, 0), (1, 1), (2, 0), (2, 1), (3, 0), (4, 1), (5, 0), (5, 1))
        early = ((0, 0), (1, 0), (2, 0), (2, 2), (3, 0), (1, 1), (2, 1), (2, 3))
        core = self.core_flag
        s0, s1, sv, sf = cut(expr, 0, 2), cut(expr, 2, 2), cut(expr, 4, 3), cut(expr, 7, 1)
        expr_all = both_genes(expr)
        a0 = near(s0)
        bs01 = across(cut(expr, 0, 4))
        part = self.local_stats()
        a0, part, s0, s1 = hold(a0, part, s0, s1)
        a1 = near(s1)
        b0 = middle(join(s0, a0))
        away = swap_cells(part)
        a1, away, sv, logits, bs01, ev4 = hold(a1, away, sv, self.logits, bs01, cut(expr, 4, 4))
        bsv = across(ev4)
        av = near(sv)
        n01 = join(a0, a1)
        n01_all = both_genes(n01)
        self.merge_stats(part, away)
        mapped = self.turned(order, self.shift, logits)
        b0, a1, s1 = hold(b0, a1, s1)
        b1 = middle(join(s1, a1))
        av, b0, mapped = hold(av, b0, mapped)
        e0 = near(b0)
        av_all = both_genes(av)
        bsv, n01, sf, bs01 = hold(bsv, n01, sf, bs01)
        yn = across(n01)
        bs01_o = swap_genes(bs01)
        bsv_all = both_genes(bsv)
        sf = join(sf, cut(bsv, 3, 1))
        b1, sv, av = hold(b1, sv, av)
        bv = middle(join(sv, av))
        e0, b0, b1 = hold(e0, b0, b1)
        (mf0,) = pick(b0, e0)
        e1 = near(b1)
        mf0_o = swap_genes(mf0)
        yn, bs01_o, mf0 = hold(yn, bs01_o, mf0)
        ymf0 = across(mf0)
        yn_all = both_genes(yn)
        e1, mf0_o, sf, b1 = hold(e1, mf0_o, sf, b1)
        (mf1,) = pick(b1, e1)
        af = near(sf)
        mf1_o = swap_genes(mf1)
        ymf0, bv, mf1 = hold(ymf0, bv, mf1)
        ymf1 = across(mf1)
        ymf0_o = swap_genes(ymf0)
        af, bv, sf, mapped = hold(af, bv, sf, mapped)
        ev = near(bv)
        bf = middle(join(sf, af))
        af_all = both_genes(af)
        partial0, panel0 = forward(
            core,
            mapped,
            [expr_all, n01_all, (mf0, mf0_o), (bs01, bs01_o), yn_all, (ymf0, ymf0_o)],
            first,
            (0, 0, 0, 0, 0, 0),
            2 * unit,
        )
        away0 = swap_cells(partial0)
        ymf1, partial0, mf1_o, av, mapped = hold(ymf1, partial0, mf1_o, av, mapped)
        ynv = across(av)
        ymf1_o = swap_genes(ymf1)
        partial1, panel1 = forward(
            core,
            mapped,
            [expr_all, n01_all, (mf1, mf1_o), (bs01, bs01_o), yn_all, (ymf1, ymf1_o)],
            second,
            (1, 0, 0, 1, 0, 0),
            2 * unit,
        )
        away1 = swap_cells(partial1)
        ynv, ev, bv, partial1, bf = hold(ynv, ev, bv, partial1, bf)
        m2, m3, m4 = pick(bv, ev, 3)
        ym2 = across(m2)
        ef = near(bf)
        m2_o = swap_genes(m2)
        ynv_o = swap_genes(ynv)
        ym2, m2_o, ynv_o, away0, m3, mapped = hold(ym2, m2_o, ynv_o, away0, m3, mapped)
        ym3 = across(m3)
        ym2_o = swap_genes(ym2)
        m3_o = swap_genes(m3)
        partial2, panel2 = forward(
            core,
            mapped,
            [expr_all, av_all, (m2, m2_o), bsv_all, (ynv, ynv_o), (ym2, ym2_o)],
            first,
            (4, 0, 0, 0, 0, 0),
            unit,
        )
        away2 = swap_cells(partial2)
        ym3, ef, bf, partial2, m3_o, m4, mapped = hold(ym3, ef, bf, partial2, m3_o, m4, mapped)
        ym4 = across(m4)
        ym3_o = swap_genes(ym3)
        (mff,) = pick(bf, ef)
        mff_o = swap_genes(mff)
        m4_o = swap_genes(m4)
        partial3, panel3 = forward(
            core,
            mapped,
            [expr_all, av_all, (m3, m3_o), bsv_all, (ynv, ynv_o), (ym3, ym3_o)],
            first,
            (5, 1, 0, 1, 1, 0),
            unit,
        )
        away3 = swap_cells(partial3)
        ym4, partial3, away1, mff_o, mapped = hold(ym4, partial3, away1, mff_o, mapped)
        ym4_o = swap_genes(ym4)
        partialf, panelf = forward(
            core, mapped, [expr_all, af_all, (mff, mff_o), bsv_all], early, (7, 0, 0, 3), unit
        )
        awayf = swap_cells(partialf)
        ym4_o, partialf, m4_o, mapped = hold(ym4_o, partialf, m4_o, mapped)
        partial4, panel4 = forward(
            core,
            mapped,
            [expr_all, av_all, (m4, m4_o), bsv_all, (ynv, ynv_o), (ym4, ym4_o)],
            first,
            (6, 2, 0, 2, 2, 0),
            unit,
        )
        away4 = swap_cells(partial4)
        chunks = []
        rows = [
            ([partial0, away0], 0, 2, panel0),
            ([partial1, away1], 2, 2, panel1),
            ([partial2, away2], 4, 1, panel2),
            ([partial3, away3], 5, 1, panel3),
            ([partial4, away4], 6, 1, panel4),
            ([partialf, awayf], 7, 1, panelf),
        ]
        for parts, at, wide, panel in rows:
            chunks.append((wide * unit, panel) + tuple(self.stats(parts, at * unit, wide * unit)))
        return order, chunks


def body(logits, filter_logits, expression, spot_expression, cell_mask, spot_counts):
    cells_total = logits.shape[0] * lax.axis_size("cells")
    spots = logits.shape[1]
    spots_total = spots * lax.axis_size("spots") * lax.axis_size("genes")
    genes_total = expression.shape[1] * lax.axis_size("genes")
    step = Step(logits, filter_logits, expression, spot_expression, cell_mask)
    order, chunks = step.gathered_line() if lax.axis_size("spots") == 8 else step.gathered_whole()
    widths, panels, preds, gene_stats, spot_stats = zip(*chunks)
    density = step.density

    counts = spot_counts.astype(f32)
    kl_parts = jnp.stack([jnp.sum(density), jnp.sum(counts * (jnp.log(counts) - jnp.log(density))), jnp.sum(counts)])

    kl_block = jnp.broadcast_to(kl_parts[:, None], (3, 128))
    gene = sum_spots_genes(jnp.concatenate(gene_stats + (kl_block,), axis=1))
    dens_total, kl_part, count_total = gene[0, -1], gene[1, -1], gene[2, -1]
    kl_term = kl_part / count_total - jnp.log(count_total) + jnp.log(dens_total)
    offset = (step.cell_count - 0.5 * cells_total) / cells_total
    penalty = jnp.sqrt(offset * offset + 0.01)
    dens_grad = -counts / (count_total * density) + 1.0 / dens_total
    spot = functools.reduce(jnp.add, spot_stats)

    turned, inner, sums = grad_pred(
        step.core_flag, widths, genes_total, spots_total, spot, gene, step.target, preds
    )
    theirs = swap_genes(
        jnp.concatenate([jnp.where(step.core == 0, p[:, w:], p[:, :w]) for p, w in zip(preds, widths)], axis=1)
    )
    col = jnp.concatenate([step.shift, dens_grad[None], inner + (density * dens_grad)[None]], axis=0)
    grad_logits, row = backward(order, step.logits, step.enable, step.retain, col, turned, panels)

    row_sums = sum_spots_genes(jnp.concatenate([row, sums], axis=0))
    copies = lax.axis_size("spots") * lax.axis_size("genes")
    gene_sum, spot_sum = row_sums[-1, 0] / copies, row_sums[-1, 1]
    total_loss = -gene_sum / genes_total - spot_sum / spots_total + kl_term + penalty
    retain_grad = row_sums[:-1] + step.enable * offset / (penalty * cells_total)
    filter_grad = (retain_grad * step.retain * (1.0 - step.retain)).reshape(-1)

    predicted = lay(step.core_flag, theirs, preds)
    return (predicted, total_loss, grad_logits, filter_grad)


def solution(mesh):
    placed = (
        P("cells", ("spots", "genes")),
        P("cells"),
        P(("cells", "spots"), "genes"),
        P("spots", "genes"),
        P("cells"),
        P(("spots", "genes")),
    )
    return jax.shard_map(
        body,
        mesh=mesh,
        in_specs=placed,
        out_specs=(P("spots", "genes"), P(), P("cells", ("spots", "genes")), P("cells")),
        check_vma=False,
    )
```

time: 407 us -> 376 us (0.924)
  waiting for transfers between devices: 164 us -> 110 us
  Pallas kernels: 91.7 us -> 127 us
  local copies, waits for them, and re-layouts: 50.4 us -> 32.2 us
  between operations: 8.84 us -> 22.6 us
  starting transfers between devices: 82.6 us -> 71.5 us
    ppermute x7, waiting for transfers between devices: 46.9 us -> 10 us  [swap_cells(): return lax.ppermute(x, 'cells', [(0, 1), (1, 0)])]
    pallas_call x16 -> x22, Pallas kernels: 38.8 us -> 67.2 us  [the longest x6 53.2 us: forward(): pl.pallas_call(functools.partial(forward_kernel, table, [len(x) for x in...]
    ppermute x15 -> x8, waiting for transfers between devices: 86.3 us -> 68.5 us  [near(): return lax.ppermute(x, 'spots', near_pairs)]
    unnamed x121 -> x111, local copies, waits for them, and re-layouts: 39 us -> 23.2 us
    pallas_call x1, Pallas kernels: 11.1 us -> 15.9 us  [mapped_turned(): pl.pallas_call(mapped_kernel, grid_spec=pltpu.PrefetchScalarGridSpec(num_...]
    pallas_call x1, Pallas kernels: 6.45 us -> 10.9 us  [col_stats(): pl.pallas_call(col_stats_kernel, grid=(cells // block,), in_specs=[pl.Blo...]
    unnamed x1 -> x7, other arithmetic: 0.01 us -> 4.08 us
    ppermute x10 -> x4, starting transfers between devices: 8.58 us -> 5.07 us  [middle(): return lax.ppermute(x, 'spots', middle_pairs)]
  transfers between devices with their start and end apart: 74 -> 61, of which waited for: 25 -> 21; matrix products, arithmetic and copies ran while one was open for 5% -> 5% of each run, Pallas kernels for 21% -> 33%
where the time goes in v3:
time: 376 us; the launch traced here: 375 us
  Pallas kernels  127 us (34%)
  waiting for transfers between devices  110 us (29%)
  starting transfers between devices  71.5 us (19%)
  local copies, waits for them, and re-layouts  32.2 us (9%)
  between operations  22.6 us (6%)
  other arithmetic  11.6 us (3%)
    ppermute x8, waiting for transfers between devices, near(): return lax.ppermute(x, 'spots', near_pairs)  68.5 us
    pallas_call x6, Pallas kernels, forward(): pl.pallas_call(functools.partial(forward_kernel, table, [len(x) for x in...  53.2 us
    ppermute x8, starting transfers between devices, near(): return lax.ppermute(x, 'spots', near_pairs)  31.8 us
    pallas_call x1, Pallas kernels, backward(): pl.pallas_call(functools.partial(backward_kernel, widths), grid_spec=pltp...  26.8 us
    unnamed x111, local copies, waits for them, and re-layouts  23.2 us
    ppermute x9, waiting for transfers between devices, across(): return lax.ppermute(x, 'spots', across_pairs)  19.5 us
    pallas_call x1, Pallas kernels, mapped_turned(): pl.pallas_call(mapped_kernel, grid_spec=pltpu.PrefetchScalarGridSpec(num_...  15.9 us
    pallas_call x1, Pallas kernels, col_stats(): pl.pallas_call(col_stats_kernel, grid=(cells // block,), in_specs=[pl.Blo...  10.9 us
  transfers between devices with their start and end apart: 61, of which 21 were waited for; matrix products, arithmetic and copies ran while one was open for 5% of the time, Pallas kernels for 33%

profile of v3, /device:TPU:0, one launch (start us, length us, event | category | flops | bytes accessed | tf_op | source)
XLA Modules:
  0.0 374.8 jit_solution(4955299255532777057)
XLA Ops:
  8.7 3.1 collective-permute-start
  15.1 10.9 %col_stats.1 = f32[3,512]{1,0:T(4,128)S(1)} custom-call(f32[8192,512]{1,0:T(8,128)} %logits_ref.4, f32[64,128]{1,0:T(8,128)S(1)} %convert_bitcast_fusion.enable_ref, f32[64,128]{1,0:T(8,128)S(1)} %get-tuple-element.242.retain_ref), custom_call_target="tpu_custom_call" | custom-call | flops 1 | bytes 1 | tf_op jit(solution)/shard_map/col_stats/pallas_call | solution.py:76
  30.8 9.0 %collective-permute-done.1.refs_1_ = bf16[1024,256]{1,0:T(8,128)(2,1)S(1)} collective-permute-done((bf16[1024,256]{1,0:T(8,128)(2,1)S(1)}, bf16[1024,256]{1,0:T(8,128)(2,1)S(1)}, u32[]{:S(2)}, u32[]{:S(2)}) %collective-permute-start.1) | collective-permute-done | bytes 524320 | tf_op jit(solution)/shard_map/ppermute | solution.py:517
  44.9 3.5 collective-permute-start.7
  48.5 15.9 %mapped_turned.1.mapped_ref = bf16[512,8192]{1,0:T(8,128)(2,1)} custom-call(s32[8]{0:T(128)S(1)} %pad_add_fusion.order_ref, f32[8192,512]{1,0:T(8,128)} %logits_ref.4, f32[64,128]{1,0:T(8,128)S(1)} %convert_bitcast_fusion.enable_ref, f32[64,128]{1,0:T(8,128)S(1)} %get-tuple-element.242.retain_ref, f32[1,512]{1,0:T(1,128)S(1)} %get-tuple-element.244.shift_ref), custom_call_target="tpu_custom_call" | custom-call | flops 1 | bytes 1 | tf_op jit(solution)/shard_map/mapped_turned/pallas_call | solution.py:104
  66.3 8.3 %collective-permute-start.9 = (bf16[2048,256]{1,0:T(8,128)(2,1)}, bf16[2048,256]{1,0:T(8,128)(2,1)}, u32[]{:S(2)}, u32[]{:S(2)}) collective-permute-start(bf16[2048,256]{1,0:T(8,128)(2,1)} %collective-permute-done.8.middle_ref), channel_id=1, source_target_pairs={{0,4},{2,6},{4,0},{6,2},{8,12},{10,14},{12,8},{14,10},{1,5},{3,7},... | collective-permute-start | bytes 3145736 | tf_op jit(solution)/shard_map/ppermute | solution.py:517
  76.3 19.0 %collective-permute-done.9.end_ref = bf16[2048,256]{1,0:T(8,128)(2,1)} collective-permute-done((bf16[2048,256]{1,0:T(8,128)(2,1)}, bf16[2048,256]{1,0:T(8,128)(2,1)}, u32[]{:S(2)}, u32[]{:S(2)}) %collective-permute-start.9) | collective-permute-done | bytes 1048608 | tf_op jit(solution)/shard_map/ppermute | solution.py:517
  96.9 4.5 %collective-permute-done.5 = bf16[2048,256]{1,0:T(8,128)(2,1)} collective-permute-done((bf16[2048,256]{1,0:T(8,128)(2,1)}, bf16[2048,256]{1,0:T(8,128)(2,1)}, u32[]{:S(2)}, u32[]{:S(2)}) %collective-permute-start.5) | collective-permute-done | bytes 1048608 | tf_op jit(solution)/shard_map/ppermute | solution.py:523
  108.6 22.9 %collective-permute-done.13.end_ref = bf16[2048,256]{1,0:T(8,128)(2,1)S(1)} collective-permute-done((bf16[2048,256]{1,0:T(8,128)(2,1)S(1)}, bf16[2048,256]{1,0:T(8,128)(2,1)S(1)}, u32[]{:S(2)}, u32[]{:S(2)}) %collective-permute-start.13) | collective-permute-done | bytes 1048608 | tf_op jit(solution)/shard_map/ppermute | solution.py:517
  133.1 10.3 %collective-permute-start.16 = (bf16[2048,128]{1,0:T(8,128)(2,1)S(1)}, bf16[2048,128]{1,0:T(8,128)(2,1)S(1)}, u32[]{:S(2)}, u32[]{:S(2)}) collective-permute-start(bf16[2048,128]{1,0:T(8,128)(2,1)S(1)} %join.10.refs_0_), channel_id=1, source_target_pairs={{0,4},{2,6},{4,0},{6,2},{8,12},{10,14},{12,8},{14,10},{1,5},{3,7},... | collective-permute-start | bytes 1572872 | tf_op jit(solution)/shard_map/ppermute | solution.py:517
  143.4 11.8 %collective-permute-done.16.refs_1_ = bf16[2048,128]{1,0:T(8,128)(2,1)S(1)} collective-permute-done((bf16[2048,128]{1,0:T(8,128)(2,1)S(1)}, bf16[2048,128]{1,0:T(8,128)(2,1)S(1)}, u32[]{:S(2)}, u32[]{:S(2)}) %collective-permute-start.16) | collective-permute-done | bytes 524320 | tf_op jit(solution)/shard_map/ppermute | solution.py:517
  157.0 9.4 %forward.6 = (f32[512,512]{1,0:T(8,128)S(1)}, bf16[8192,512]{1,0:T(8,128)(2,1)}) custom-call(s32[1]{0:T(128)} %bitcast.core_ref, bf16[512,8192]{1,0:T(8,128)(2,1)} %mapped_turned.1.mapped_ref, bf16[2048,1024]{1,0:T(8,128)(2,1)} %all-gather.8.cloned.1.call-done.refs_0_, bf16[4096,256]{1,0:T(8,128)(2,1)} %all-gather.10.cloned.1.call-done.refs_1_, ...), custom_call_target="tpu_custom_call" | custom-call | flops 1 | bytes 1 | tf_op jit(solution)/shard_map/forward/pallas_call | solution.py:184
  171.3 10.3 %forward.7 = (f32[512,512]{1,0:T(8,128)}, bf16[8192,512]{1,0:T(8,128)(2,1)}) custom-call(s32[1]{0:T(128)} %bitcast.core_ref, bf16[512,8192]{1,0:T(8,128)(2,1)} %mapped_turned.1.mapped_ref, bf16[2048,1024]{1,0:T(8,128)(2,1)} %all-gather.8.cloned.1.call-done.refs_0_, bf16[4096,256]{1,0:T(8,128)(2,1)} %all-gather.10.cloned.1.call-done.refs_1_, ...), custom_call_target="tpu_custom_call" | custom-call | flops 1 | bytes 1 | tf_op jit(solution)/shard_map/forward/pallas_call | solution.py:184
  181.6 5.7 %collective-permute-done.19.refs_5_ = bf16[1024,384]{1,0:T(8,128)(2,1)S(1)} collective-permute-done((bf16[1024,384]{1,0:T(8,128)(2,1)S(1)}, bf16[1024,384]{1,0:T(8,128)(2,1)S(1)}, u32[]{:S(2)}, u32[]{:S(2)}) %collective-permute-start.19) | collective-permute-done | bytes 786464 | tf_op jit(solution)/shard_map/ppermute | solution.py:523
  187.3 3.8 %collective-permute-done.20.end_ref = bf16[2048,384]{1,0:T(8,128)(2,1)} collective-permute-done((bf16[2048,384]{1,0:T(8,128)(2,1)}, bf16[2048,384]{1,0:T(8,128)(2,1)}, u32[]{:S(2)}, u32[]{:S(2)}) %collective-permute-start.20) | collective-permute-done | bytes 1572896 | tf_op jit(solution)/shard_map/ppermute | solution.py:517
  191.1 3.1 select.13
  196.7 3.7 collective-permute-start.28
  201.4 8.1 %collective-permute-done.23.refs_7_ = bf16[2048,128]{1,0:T(8,128)(2,1)} collective-permute-done((bf16[2048,128]{1,0:T(8,128)(2,1)S(1)}, bf16[2048,128]{1,0:T(8,128)(2,1)}, u32[]{:S(2)}, u32[]{:S(2)}) %collective-permute-start.23) | collective-permute-done | bytes 524320 | tf_op jit(solution)/shard_map/ppermute | solution.py:523
  213.4 8.0 %forward.8 = (f32[512,256]{1,0:T(8,128)S(1)}, bf16[8192,256]{1,0:T(8,128)(2,1)}) custom-call(s32[1]{0:T(128)} %bitcast.core_ref, bf16[512,8192]{1,0:T(8,128)(2,1)} %mapped_turned.1.mapped_ref, bf16[2048,1024]{1,0:T(8,128)(2,1)} %all-gather.8.cloned.1.call-done.refs_0_, bf16[2048,384]{1,0:T(8,128)(2,1)} %all-gather.16.cloned.1.call-done.refs_1_, ...), custom_call_target="tpu_custom_call" | custom-call | flops 1 | bytes 1 | tf_op jit(solution)/shard_map/forward/pallas_call | solution.py:184
  229.9 2.5 pad_maximum_fusion.1
  233.2 9.0 %forward.9 = (f32[512,256]{1,0:T(8,128)}, bf16[8192,256]{1,0:T(8,128)(2,1)}) custom-call(s32[1]{0:T(128)} %bitcast.core_ref, bf16[512,8192]{1,0:T(8,128)(2,1)} %mapped_turned.1.mapped_ref, bf16[2048,1024]{1,0:T(8,128)(2,1)} %all-gather.8.cloned.1.call-done.refs_0_, bf16[2048,384]{1,0:T(8,128)(2,1)} %all-gather.16.cloned.1.call-done.refs_1_, ...), custom_call_target="tpu_custom_call" | custom-call | flops 1 | bytes 1 | tf_op jit(solution)/shard_map/forward/pallas_call | solution.py:184
  242.3 3.4 copy-done
  252.6 8.0 %forward.10 = (f32[512,256]{1,0:T(8,128)S(1)}, bf16[8192,256]{1,0:T(8,128)(2,1)}) custom-call(s32[1]{0:T(128)} %bitcast.core_ref, bf16[512,8192]{1,0:T(8,128)(2,1)} %mapped_turned.1.mapped_ref, bf16[2048,1024]{1,0:T(8,128)(2,1)} %all-gather.8.cloned.1.call-done.refs_0_, bf16[4096,128]{1,0:T(8,128)(2,1)} %all-gather.20.cloned.1.call-done.refs_1_, ...), custom_call_target="tpu_custom_call" | custom-call | flops 1 | bytes 1 | tf_op jit(solution)/shard_map/forward/pallas_call | solution.py:184
  261.2 3.4 copy-done.2
  268.2 8.5 %forward.11 = (f32[512,256]{1,0:T(8,128)S(1)}, bf16[8192,256]{1,0:T(8,128)(2,1)}) custom-call(s32[1]{0:T(128)} %bitcast.core_ref, bf16[512,8192]{1,0:T(8,128)(2,1)} %mapped_turned.1.mapped_ref, bf16[2048,1024]{1,0:T(8,128)(2,1)} %all-gather.8.cloned.1.call-done.refs_0_, bf16[2048,384]{1,0:T(8,128)(2,1)} %all-gather.16.cloned.1.call-done.refs_1_, ...), custom_call_target="tpu_custom_call" | custom-call | flops 1 | bytes 1 | tf_op jit(solution)/shard_map/forward/pallas_call | solution.py:184
  282.6 7.9 %collective-permute-done.39.refs_1_ = f32[512,256]{1,0:T(8,128)S(1)} collective-permute-done((f32[512,256]{1,0:T(8,128)S(1)}, f32[512,256]{1,0:T(8,128)S(1)}, u32[]{:S(2)}, u32[]{:S(2)}) %collective-permute-start.39) | collective-permute-done | bytes 524320 | tf_op jit(solution)/shard_map/ppermute | solution.py:445
  291.0 3.5 collective-permute-start.42
  305.2 2.5 grad_pred.1
  314.5 26.8 %backward.1 = (f32[8192,512]{1,0:T(8,128)}, f32[64,128]{1,0:T(8,128)S(1)}) custom-call(s32[8]{0:T(128)S(1)} %pad_add_fusion.order_ref, f32[8192,512]{1,0:T(8,128)} %logits_ref.4, f32[64,128]{1,0:T(8,128)S(1)} %convert_bitcast_fusion.enable_ref, f32[64,128]{1,0:T(8,128)S(1)} %get-tuple-element.242.retain_ref, f32[3,512]{1,0:T(4,128)S(1)} %pad_maximum_fusion.col_ref, ...), custom_call_target="tpu_custom_call" | custom-call | flops 1 | bytes 1 | tf_op jit(solution)/shard_map/backward/pallas_call | solution.py:343
  341.5 2.9 collective-permute-start.49
  346.8 3.4 collective-permute-done.50
  363.0 3.8 %lay.1 = f32[1024,1024]{1,0:T(8,128)} custom-call(s32[1]{0:T(128)} %bitcast.core_ref, f32[512,1024]{1,0:T(8,128)} %collective-permute-done.41.theirs_ref, f32[512,512]{1,0:T(8,128)S(1)} %get-tuple-element.167.refs_0_, f32[512,512]{1,0:T(8,128)S(1)} %get-tuple-element.185.refs_1_, f32[512,256]{1,0:T(8,128)S(1)} %get-tuple-element.187.refs_2_, ...), custom_call_target="tpu_custom_call" | custom-call | flops 1 | bytes 1 | tf_op jit(solution)/shard_map/lay/pallas_call | solution.py:428
  (272 shorter events, 95.4 us)
Async XLA Ops:
  7.2 149.8 %all-gather.10.cloned.1.call-start = ((), (), s32[]{:S(2)}) async-start(), calls=%async_computation.1 | async-start | bytes 3145728 | tf_op jit(solution)/shard_map/all_gather | solution.py:462
  12.9 26.9 %collective-permute-start.3 = (bf16[1024,512]{1,0:T(8,128)(2,1)S(1)}, bf16[1024,512]{1,0:T(8,128)(2,1)}, u32[]{:S(2)}, u32[]{:S(2)}) collective-permute-start(bf16[1024,512]{1,0:T(8,128)(2,1)S(1)} %get-tuple-element.233), channel_id=1, source_target_pairs={{0,2},{2,0},{4,6},{6,4},{8,10},{10,8},{12,14},{14,12},{1,3},{3,1},... | collective-permute-start | bytes 3145736 | tf_op jit(solution)/shard_map/ppermute | solution.py:523
  40.9 116.1 %all-gather.8.cloned.1.call-start = ((), (), s32[]{:S(2)}) async-start(), calls=%async_computation | async-start | bytes 6291456 | tf_op jit(solution)/shard_map/all_gather | solution.py:462
  41.6 115.4 %all-gather.12.cloned.1.call-start = ((), (), s32[]{:S(2)}) async-start(), calls=%async_computation.2 | async-start | bytes 3145728 | tf_op jit(solution)/shard_map/all_gather | solution.py:462
  42.7 21.7 %collective-permute-start.8 = (bf16[2048,256]{1,0:T(8,128)(2,1)}, bf16[2048,256]{1,0:T(8,128)(2,1)}, u32[]{:S(2)}, u32[]{:S(2)}) collective-permute-start(bf16[2048,256]{1,0:T(8,128)(2,1)} %join.7), channel_id=1, source_target_pairs={{4,8},{6,10},{8,4},{10,6},{5,9},{7,11},{9,5},{11,7},{20,24},{22,26... | collective-permute-start | bytes 3145736 | tf_op jit(solution)/shard_map/ppermute | solution.py:520
  44.4 31.1 %collective-permute-start.4 = (bf16[1024,512]{1,0:T(8,128)(2,1)}, bf16[1024,512]{1,0:T(8,128)(2,1)}, u32[]{:S(2)}, u32[]{:S(2)}) collective-permute-start(bf16[1024,512]{1,0:T(8,128)(2,1)} %get-tuple-element.116), channel_id=1, source_target_pairs={{0,2},{2,0},{4,6},{6,4},{8,10},{10,8},{12,14},{14,12},{1,3},{3,1},... | collective-permute-start | bytes 3145736 | tf_op jit(solution)/shard_map/ppermute | solution.py:523
  44.9 21.4 %collective-permute-start.7 = (bf16[1024,384]{1,0:T(8,128)(2,1)S(1)}, bf16[1024,384]{1,0:T(8,128)(2,1)S(1)}, u32[]{:S(2)}, u32[]{:S(2)}) collective-permute-start(bf16[1024,384]{1,0:T(8,128)(2,1)S(1)} %slice.103.refs_0_), channel_id=1, source_target_pairs={{0,4},{2,6},{4,0},{6,2},{8,12},{10,14},{12,8},{14,10},{1,5},{3,7},... | collective-permute-start | bytes 2359304 | tf_op jit(solution)/shard_map/ppermute | solution.py:517
  66.3 29.1 %collective-permute-start.9 = (bf16[2048,256]{1,0:T(8,128)(2,1)}, bf16[2048,256]{1,0:T(8,128)(2,1)}, u32[]{:S(2)}, u32[]{:S(2)}) collective-permute-start(bf16[2048,256]{1,0:T(8,128)(2,1)} %collective-permute-done.8.middle_ref), channel_id=1, source_target_pairs={{0,4},{2,6},{4,0},{6,2},{8,12},{10,14},{12,8},{14,10},{1,5},{3,7},... | collective-permute-start | bytes 3145736 | tf_op jit(solution)/shard_map/ppermute | solution.py:517
  75.5 21.4 %collective-permute-start.6 = (bf16[1024,512]{1,0:T(8,128)(2,1)}, bf16[1024,512]{1,0:T(8,128)(2,1)}, u32[]{:S(2)}, u32[]{:S(2)}) collective-permute-start(bf16[1024,512]{1,0:T(8,128)(2,1)} %collective-permute-done.3.refs_4_), channel_id=1, source_target_pairs={{0,1},{1,0},{2,3},{3,2},{4,5},{5,4},{6,7},{7,6},{8,9},{9,8},{10,11... | collective-permute-start | bytes 3145736 | tf_op jit(solution)/shard_map/ppermute | solution.py:449
  75.6 25.9 %collective-permute-start.5 = (bf16[2048,256]{1,0:T(8,128)(2,1)}, bf16[2048,256]{1,0:T(8,128)(2,1)}, u32[]{:S(2)}, u32[]{:S(2)}) collective-permute-start(bf16[2048,256]{1,0:T(8,128)(2,1)} %join.6), channel_id=1, source_target_pairs={{0,2},{2,0},{4,6},{6,4},{8,10},{10,8},{12,14},{14,12},{1,3},{3,1},... | collective-permute-start | bytes 3145736 | tf_op jit(solution)/shard_map/ppermute | solution.py:523
  101.5 111.9 %all-gather.16.cloned.1.call-start = ((), (), s32[]{:S(2)}) async-start(), calls=%async_computation.4 | async-start | bytes 2359296 | tf_op jit(solution)/shard_map/all_gather | solution.py:462
  102.1 111.4 %all-gather.18.cloned.1.call-start = ((), (), s32[]{:S(2)}) async-start(), calls=%async_computation.5 | async-start | bytes 3145728 | tf_op jit(solution)/shard_map/all_gather | solution.py:462
  102.7 139.5 %all-gather.14.cloned.1.call-start = ((), (), s32[]{:S(2)}) async-start(), calls=%async_computation.3 | async-start | bytes 12582912 | tf_op jit(solution)/shard_map/all_gather | solution.py:462
  103.3 149.3 %all-gather.20.cloned.1.call-start = ((), (), s32[]{:S(2)}) async-start(), calls=%async_computation.6 | async-start | bytes 1572864 | tf_op jit(solution)/shard_map/all_gather | solution.py:462
  104.0 27.6 %collective-permute-start.12 = (bf16[2048,384]{1,0:T(8,128)(2,1)S(1)}, bf16[2048,384]{1,0:T(8,128)(2,1)}, u32[]{:S(2)}, u32[]{:S(2)}) collective-permute-start(bf16[2048,384]{1,0:T(8,128)(2,1)S(1)} %join.9), channel_id=1, source_target_pairs={{4,8},{6,10},{8,4},{10,6},{5,9},{7,11},{9,5},{11,7},{20,24},{22,26... | collective-permute-start | bytes 4718600 | tf_op jit(solution)/shard_map/ppermute | solution.py:520
  105.9 25.6 %collective-permute-start.13 = (bf16[2048,256]{1,0:T(8,128)(2,1)S(1)}, bf16[2048,256]{1,0:T(8,128)(2,1)S(1)}, u32[]{:S(2)}, u32[]{:S(2)}) collective-permute-start(bf16[2048,256]{1,0:T(8,128)(2,1)S(1)} %copy-done.20), channel_id=1, source_target_pairs={{0,4},{2,6},{4,0},{6,2},{8,12},{10,14},{12,8},{14,10},{1,5},{3,7},... | collective-permute-start | bytes 3145736 | tf_op jit(solution)/shard_map/ppermute | solution.py:517
  106.7 25.3 %collective-permute-start.11 = (bf16[2048,256]{1,0:T(8,128)(2,1)S(1)}, bf16[2048,256]{1,0:T(8,128)(2,1)}, u32[]{:S(2)}, u32[]{:S(2)}) collective-permute-start(bf16[2048,256]{1,0:T(8,128)(2,1)S(1)} %select.11.refs_2_), channel_id=1, source_target_pairs={{0,2},{2,0},{4,6},{6,4},{8,10},{10,8},{12,14},{14,12},{1,3},{3,1},... | collective-permute-start | bytes 3145736 | tf_op jit(solution)/shard_map/ppermute | solution.py:523
  132.0 25.0 %collective-permute-start.17 = (bf16[2048,256]{1,0:T(8,128)(2,1)}, bf16[2048,256]{1,0:T(8,128)(2,1)}, u32[]{:S(2)}, u32[]{:S(2)}) collective-permute-start(bf16[2048,256]{1,0:T(8,128)(2,1)} %collective-permute-done.11.refs_7_), channel_id=1, source_target_pairs={{0,1},{1,0},{2,3},{3,2},{4,5},{5,4},{6,7},{7,6},{8,9},{9,8},{10,11... | collective-permute-start | bytes 3145736 | tf_op jit(solution)/shard_map/ppermute | solution.py:449
  132.0 34.4 %collective-permute-start.18 = (bf16[2048,256]{1,0:T(8,128)(2,1)S(1)}, bf16[2048,256]{1,0:T(8,128)(2,1)}, u32[]{:S(2)}, u32[]{:S(2)}) collective-permute-start(bf16[2048,256]{1,0:T(8,128)(2,1)S(1)} %select.12.refs_2_), channel_id=1, source_target_pairs={{0,1},{1,0},{2,3},{3,2},{4,5},{5,4},{6,7},{7,6},{8,9},{9,8},{10,11... | collective-permute-start | bytes 3145736 | tf_op jit(solution)/shard_map/ppermute | solution.py:449
  132.5 33.9 %collective-permute-start.15 = (bf16[2048,256]{1,0:T(8,128)(2,1)S(1)}, bf16[2048,256]{1,0:T(8,128)(2,1)}, u32[]{:S(2)}, u32[]{:S(2)}) collective-permute-start(bf16[2048,256]{1,0:T(8,128)(2,1)S(1)} %select.12.refs_2_), channel_id=1, source_target_pairs={{0,2},{2,0},{4,6},{6,4},{8,10},{10,8},{12,14},{14,12},{1,3},{3,1},... | collective-permute-start | bytes 3145736 | tf_op jit(solution)/shard_map/ppermute | solution.py:523
  133.1 22.1 %collective-permute-start.16 = (bf16[2048,128]{1,0:T(8,128)(2,1)S(1)}, bf16[2048,128]{1,0:T(8,128)(2,1)S(1)}, u32[]{:S(2)}, u32[]{:S(2)}) collective-permute-start(bf16[2048,128]{1,0:T(8,128)(2,1)S(1)} %join.10.refs_0_), channel_id=1, source_target_pairs={{0,4},{2,6},{4,0},{6,2},{8,12},{10,14},{12,8},{14,10},{1,5},{3,7},... | collective-permute-start | bytes 1572872 | tf_op jit(solution)/shard_map/ppermute | solution.py:517
  155.2 35.9 %collective-permute-start.20 = (bf16[2048,384]{1,0:T(8,128)(2,1)}, bf16[2048,384]{1,0:T(8,128)(2,1)}, u32[]{:S(2)}, u32[]{:S(2)}) collective-permute-start(bf16[2048,384]{1,0:T(8,128)(2,1)} %collective-permute-done.12.middle_ref), channel_id=1, source_target_pairs={{0,4},{2,6},{4,0},{6,2},{8,12},{10,14},{12,8},{14,10},{1,5},{3,7},... | collective-permute-start | bytes 4718600 | tf_op jit(solution)/shard_map/ppermute | solution.py:517
  168.8 31.6 %collective-permute-start.26 = (f32[512,512]{1,0:T(8,128)S(1)}, f32[512,512]{1,0:T(8,128)S(1)}, u32[]{:S(2)}, u32[]{:S(2)}) collective-permute-start(f32[512,512]{1,0:T(8,128)S(1)} %get-tuple-element.152.refs_0_), channel_id=1, source_target_pairs={{0,16},{16,0},{1,17},{17,1},{2,18},{18,2},{3,19},{19,3},{4,20},{20... | collective-permute-start | bytes 3145736 | tf_op jit(solution)/shard_map/ppermute | solution.py:445
  196.7 27.5 %collective-permute-start.28 = (bf16[4096,128]{1,0:T(8,128)(2,1)S(1)}, bf16[4096,128]{1,0:T(8,128)(2,1)S(1)}, u32[]{:S(2)}, u32[]{:S(2)}) collective-permute-start(bf16[4096,128]{1,0:T(8,128)(2,1)S(1)} %collective-permute-done.22.middle_ref), channel_id=1, source_target_pairs={{0,4},{2,6},{4,0},{6,2},{8,12},{10,14},{12,8},{14,10},{1,5},{3,7},... | collective-permute-start | bytes 3145736 | tf_op jit(solution)/shard_map/ppermute | solution.py:517
  211.9 36.3 %collective-permute-start.33 = (f32[512,512]{1,0:T(8,128)}, f32[512,512]{1,0:T(8,128)}, u32[]{:S(2)}, u32[]{:S(2)}) collective-permute-start(f32[512,512]{1,0:T(8,128)} %get-tuple-element.168.refs_0_), channel_id=1, source_target_pairs={{0,16},{16,0},{1,17},{17,1},{2,18},{18,2},{3,19},{19,3},{4,20},{20... | collective-permute-start | bytes 3145736 | tf_op jit(solution)/shard_map/ppermute | solution.py:445
  225.0 23.8 %collective-permute-start.34 = (bf16[4096,128]{1,0:T(8,128)(2,1)S(1)}, bf16[4096,128]{1,0:T(8,128)(2,1)}, u32[]{:S(2)}, u32[]{:S(2)}) collective-permute-start(bf16[4096,128]{1,0:T(8,128)(2,1)S(1)} %select.14.refs_2_), channel_id=1, source_target_pairs={{0,1},{1,0},{2,3},{3,2},{4,5},{5,4},{6,7},{7,6},{8,9},{9,8},{10,11... | collective-permute-start | bytes 3145736 | tf_op jit(solution)/shard_map/ppermute | solution.py:449
  225.7 23.8 %collective-permute-start.35 = (f32[512,256]{1,0:T(8,128)}, f32[512,256]{1,0:T(8,128)}, u32[]{:S(2)}, u32[]{:S(2)}) collective-permute-start(f32[512,256]{1,0:T(8,128)} %copy-done.26), channel_id=1, source_target_pairs={{0,16},{16,0},{1,17},{17,1},{2,18},{18,2},{3,19},{19,3},{4,20},{20... | collective-permute-start | bytes 1572872 | tf_op jit(solution)/shard_map/ppermute | solution.py:445
  227.2 21.7 %collective-permute-start.31 = (bf16[2048,128]{1,0:T(8,128)(2,1)}, bf16[2048,128]{1,0:T(8,128)(2,1)}, u32[]{:S(2)}, u32[]{:S(2)}) collective-permute-start(bf16[2048,128]{1,0:T(8,128)(2,1)} %copy-done.25), channel_id=1, source_target_pairs={{0,2},{2,0},{4,6},{6,4},{8,10},{10,8},{12,14},{14,12},{1,3},{3,1},... | collective-permute-start | bytes 1572872 | tf_op jit(solution)/shard_map/ppermute | solution.py:523
  232.4 35.9 %collective-permute-start.38 = (bf16[2048,128]{1,0:T(8,128)(2,1)}, bf16[2048,128]{1,0:T(8,128)(2,1)}, u32[]{:S(2)}, u32[]{:S(2)}) collective-permute-start(bf16[2048,128]{1,0:T(8,128)(2,1)} %copy-done.25), channel_id=1, source_target_pairs={{0,1},{1,0},{2,3},{3,2},{4,5},{5,4},{6,7},{7,6},{8,9},{9,8},{10,11... | collective-permute-start | bytes 1572872 | tf_op jit(solution)/shard_map/ppermute | solution.py:449
  248.2 30.0 %collective-permute-start.36 = (f32[512,256]{1,0:T(8,128)}, f32[512,256]{1,0:T(8,128)S(1)}, u32[]{:S(2)}, u32[]{:S(2)}) collective-permute-start(f32[512,256]{1,0:T(8,128)} %get-tuple-element.188.refs_0_), channel_id=1, source_target_pairs={{0,16},{16,0},{1,17},{17,1},{2,18},{18,2},{3,19},{19,3},{4,20},{20... | collective-permute-start | bytes 1572872 | tf_op jit(solution)/shard_map/ppermute | solution.py:445
  260.6 21.7 %collective-permute-start.40 = (f32[512,256]{1,0:T(8,128)S(1)}, f32[512,256]{1,0:T(8,128)S(1)}, u32[]{:S(2)}, u32[]{:S(2)}) collective-permute-start(f32[512,256]{1,0:T(8,128)S(1)} %get-tuple-element.199.refs_0_), channel_id=1, source_target_pairs={{0,16},{16,0},{1,17},{17,1},{2,18},{18,2},{3,19},{19,3},{4,20},{20... | collective-permute-start | bytes 1572872 | tf_op jit(solution)/shard_map/ppermute | solution.py:445
  298.4 62.6 %collective-permute-start.41 = (f32[512,1024]{1,0:T(8,128)}, f32[512,1024]{1,0:T(8,128)}, u32[]{:S(2)}, u32[]{:S(2)}) collective-permute-start(f32[512,1024]{1,0:T(8,128)} %select_dynamic-update-slice_fusion.2), channel_id=1, source_target_pairs={{0,1},{1,0},{2,3},{3,2},{4,5},{5,4},{6,7},{7,6},{8,9},{9,8},{10,11... | collective-permute-start | bytes 6291464 | tf_op jit(solution)/shard_map/ppermute | solution.py:449
  (81 other events, 751.6 us)
Sparse Core Ops, SparseCore 0:
  41.0 9.9 all-gather.9
  52.5 14.8 all-gather.7
  101.6 8.5 all-gather.11
  111.6 10.8 all-gather.15
  124.0 13.8 all-gather.17
  139.2 19.2 all-gather.13
  225.3 10.4 all-gather.19

commit v4 on v3

v4 whole, which is shorter than its diff:
```python
import functools

import jax
import jax.numpy as jnp
from jax import lax
from jax.experimental import pallas as pl
from jax.experimental.pallas import tpu as pltpu
from jax.sharding import PartitionSpec as P

epsilon = 1e-06
bf16 = jnp.bfloat16
f32 = jnp.float32
PIECES = 8
MIB = 1024 * 1024
VMEM = pl.BlockSpec(memory_space=pltpu.VMEM)


def params(limit):
    return pltpu.CompilerParams(vmem_limit_bytes=limit * MIB)


def cost(flops=0, bytes_accessed=0, transcendentals=0):
    return pl.CostEstimate(flops=1, bytes_accessed=1, transcendentals=0)


def in_hbm(x):
    return pltpu.with_memory_space_constraint(x, pltpu.HBM)


def hold(*values):
    return lax.optimization_barrier(values)


def col_stats_kernel(logits_ref, enable_ref, retain_ref, out_ref, top, total, dens):
    step = pl.program_id(0)

    @pl.when(step == 0)
    def _():
        top[...] = jnp.full_like(top, -1e29)
        total[...] = jnp.zeros_like(total)
        dens[...] = jnp.zeros_like(dens)

    rows, spots = logits_ref.shape
    enable = enable_ref[...].T
    retain = retain_ref[...].T
    blocks = []
    new = top[...]
    for k in range(rows // 128):
        block = jnp.where(enable[:, k : k + 1] > 0, logits_ref[128 * k : 128 * (k + 1), :], -1e30)
        blocks.append(block.reshape(16, 8, spots))
        new = jnp.maximum(new, jnp.max(blocks[-1], axis=0))
    shrink = jnp.exp(top[...] - new)
    top[...] = new
    sums = total[...] * shrink
    kept = dens[...] * shrink
    for k in range(rows // 128):
        part = jnp.exp(blocks[k] - new[None])
        share = jnp.broadcast_to(retain[:, k : k + 1], (128, spots)).reshape(16, 8, spots)
        sums = sums + jnp.sum(part, axis=0)
        kept = kept + jnp.sum(part * share, axis=0)
    total[...] = sums
    dens[...] = kept

    @pl.when(step == pl.num_programs(0) - 1)
    def _():
        best = jnp.max(new, axis=0, keepdims=True)
        scale = jnp.exp(new - best)
        out_ref[0:1, :] = best
        out_ref[1:2, :] = jnp.sum(sums * scale, axis=0, keepdims=True)
        out_ref[2:3, :] = jnp.sum(kept * scale, axis=0, keepdims=True)


def col_stats(logits, enable, retain, block=1024):
    cells, spots = logits.shape
    cell = pl.BlockSpec((block // 128, 128), lambda i: (i, 0))
    return pl.pallas_call(
        col_stats_kernel,
        grid=(cells // block,),
        in_specs=[pl.BlockSpec((block, spots), lambda i: (i, 0)), cell, cell],
        out_specs=pl.BlockSpec((3, spots), lambda i: (0, 0)),
        out_shape=jax.ShapeDtypeStruct((3, spots), f32),
        scratch_shapes=[pltpu.VMEM((8, spots), f32)] * 3,
        compiler_params=params(20),
        cost_estimate=cost(cells * spots * 8, cells * spots * 4, cells * spots),
        name="col_stats",
    )(logits, enable, retain)


def mapped_kernel(order_ref, logits_ref, enable_ref, retain_ref, shift_ref, out_ref):
    rows, spots = logits_ref.shape
    enable = enable_ref[...].T
    retain = retain_ref[...].T
    shift = shift_ref[...]
    for k in range(rows // 128):
        block = jnp.where(enable[:, k : k + 1] > 0, logits_ref[128 * k : 128 * (k + 1), :], -1e30)
        mapped = retain[:, k : k + 1] * jnp.exp(block - shift)
        out_ref[:, 128 * k : 128 * (k + 1)] = mapped.astype(bf16).T


def mapped_turned(order, logits, enable, retain, shift):
    cells, spots = logits.shape
    block = cells // PIECES
    cell = pl.BlockSpec((block // 128, 128), lambda i, order: (order[i], 0))
    return pl.pallas_call(
        mapped_kernel,
        grid_spec=pltpu.PrefetchScalarGridSpec(
            num_scalar_prefetch=1,
            grid=(PIECES,),
            in_specs=[
                pl.BlockSpec((block, spots), lambda i, order: (order[i], 0)),
                cell,
                cell,
                pl.BlockSpec((1, spots), lambda i, order: (0, 0)),
            ],
            out_specs=pl.BlockSpec((spots, block), lambda i, order: (0, i)),
        ),
        out_shape=pltpu.HBM((spots, cells), bf16),
        compiler_params=params(20),
        cost_estimate=cost(cells * spots * 6, cells * spots * 6, cells * spots),
        name="mapped_turned",
    )(order, logits, enable, retain, shift)


def forward_kernel(pieces, table, columns, rows, wide, more, core_ref, mapped_ref, *refs):
    n = len(columns)
    sources = (refs[:n], refs[n : 2 * n])
    refs = refs[2 * n :]
    base = refs[0][...] if more else None
    pred_ref, panel_ref, held, turned, own_sems, other_sems, mapped_sems, panel_sems = refs[2 if more else 0 :]

    def piece(r, which, column):
        source, block = table[r]
        part = sources[which][source].at[pl.ds(block * rows, rows), pl.ds(columns[source] * wide, wide)]
        target = held.at[pl.ds(r * rows, rows), pl.ds(column, wide)]
        return pltpu.make_async_copy(part, target, (own_sems, other_sems)[which].at[r])

    def load(r):
        cols = pl.ds(r * rows, rows)
        return pltpu.make_async_copy(mapped_ref.at[:, cols], turned.at[:, cols], mapped_sems.at[r])

    def save(r):
        here = pl.ds(r * rows, rows)
        return pltpu.make_async_copy(held.at[here, :], panel_ref.at[here, :], panel_sems.at[r])

    for r in pieces:
        for core in range(2):

            @pl.when(core_ref[0] == core)
            def _(core=core, r=r):
                piece(r, 0, core * wide).start()
                piece(r, 1, (1 - core) * wide).start()

        load(r).start()
    total = base
    for r in pieces:
        piece(r, 0, 0).wait()
        piece(r, 1, 0).wait()
        save(r).start()
        load(r).wait()
        here = slice(r * rows, (r + 1) * rows)
        part = jnp.dot(turned[:, here], held[here, :], preferred_element_type=f32)
        total = part if total is None else total + part
    pred_ref[...] = total
    for r in pieces:
        save(r).wait()


def forward(core, mapped, sources, table, columns, wide, pieces=tuple(range(PIECES)), begun=None):
    spots, cells = mapped.shape
    rows = cells // PIECES
    own, other = zip(*sources)
    hbm = pl.BlockSpec(memory_space=pltpu.HBM)
    n = 2 + 2 * len(own)
    return pl.pallas_call(
        functools.partial(forward_kernel, pieces, table, columns, rows, wide, begun is not None),
        in_specs=[pl.BlockSpec(memory_space=pltpu.SMEM), hbm] + [hbm] * (n - 2) + ([VMEM, hbm] if begun else []),
        out_specs=[VMEM, hbm],
        out_shape=[
            jax.ShapeDtypeStruct((spots, 2 * wide), f32),
            pltpu.HBM((cells, 2 * wide), bf16),
        ],
        scratch_shapes=[pltpu.VMEM((cells, 2 * wide), bf16), pltpu.VMEM((spots, cells), bf16)]
        + [pltpu.SemaphoreType.DMA((PIECES,))] * 4,
        input_output_aliases={n + 1: 1} if begun else {},
        compiler_params=params(14 + 16 * wide // 512),
        cost_estimate=cost(4 * spots * cells * wide, 2 * cells * (spots + 4 * wide)),
        name="forward",
    )(core, in_hbm(mapped), *[in_hbm(x) for x in own + other], *(begun or ()))


def in_order(core, own, other):
    first = core == 0
    return jnp.concatenate([jnp.where(first, own, other), jnp.where(first, other, own)], axis=1)


def stats_kernel(parts, core_ref, *refs):
    own_ref, other_ref, pred_ref, gene_ref, spot_ref, sent_ref = refs[parts:]
    wide = own_ref.shape[1]
    pred = functools.reduce(jnp.add, [ref[...] for ref in refs[:parts]])
    pred_ref[...] = pred
    sent_ref[...] = jnp.where(core_ref[0] == 0, pred[:, wide:], pred[:, :wide])
    target = in_order(core_ref[0], own_ref[...], other_ref[...])
    terms = (pred * target, pred * pred, target * target)
    lane = lax.broadcasted_iota(jnp.int32, spot_ref.shape, 1)
    spot = jnp.zeros(spot_ref.shape, f32)
    for k, term in enumerate(terms):
        gene_ref[k : k + 1, :] = jnp.sum(term, axis=0, keepdims=True)
        spot = jnp.where(lane == k, jnp.sum(term, axis=1, keepdims=True), spot)
    spot_ref[...] = spot


def pred_stats(core, parts, target, other, column, other_column, wide):
    spots = parts[0].shape[0]
    whole = pl.BlockSpec((spots, 2 * wide), lambda i, core: (0, 0))
    return pl.pallas_call(
        functools.partial(stats_kernel, len(parts)),
        grid_spec=pltpu.PrefetchScalarGridSpec(
            num_scalar_prefetch=1,
            grid=(1,),
            in_specs=[whole] * len(parts)
            + [
                pl.BlockSpec((spots, wide), lambda i, core: (core[0], column)),
                pl.BlockSpec((spots, wide), lambda i, core: (0, other_column)),
            ],
            out_specs=[
                whole,
                pl.BlockSpec((3, 2 * wide), lambda i, core: (0, 0)),
                pl.BlockSpec((spots, 4), lambda i, core: (0, 0)),
                pl.BlockSpec((spots, wide), lambda i, core: (0, 0)),
            ],
        ),
        out_shape=[
            jax.ShapeDtypeStruct((spots, 2 * wide), f32),
            jax.ShapeDtypeStruct((3, 2 * wide), f32),
            jax.ShapeDtypeStruct((spots, 4), f32),
            jax.ShapeDtypeStruct((spots, wide), f32),
        ],
        compiler_params=params(16),
        cost_estimate=cost(spots * wide * 20, spots * wide * 40),
        name="pred_stats",
    )(core, *parts, target, other)


def grad_pred_kernel(widths, genes_total, spots_total, core_ref, spot_ref, gene_ref, own_ref, *refs):
    n = len(widths)
    other_refs, pred_refs = refs[:3], refs[3 : 3 + n]
    refs = refs[3:]
    quarter = other_refs[0].shape[1]
    turned_ref, inner_ref, sums_ref = refs[n:]
    spot = spot_ref[...]
    spot_pg, spot_pp, spot_gg = spot[:, 0:1], spot[:, 1:2], spot[:, 2:3]
    spot_scale = lax.rsqrt(spot_pp + epsilon) * lax.rsqrt(spot_gg + epsilon)
    spot_cos = spot_pg * spot_scale
    spot_back = spot_cos / (spot_pp + epsilon)
    gene = gene_ref[:, : 2 * sum(widths)]
    gene_scale = lax.rsqrt(gene[1:2, :] + epsilon) * lax.rsqrt(gene[2:3, :] + epsilon)
    gene_cos = gene[0:1, :] * gene_scale
    gene_back = gene_cos / (gene[1:2, :] + epsilon)
    folded = jnp.zeros((spot.shape[0], 128), f32)
    at = 0
    low = 0
    for q in range(n):
        wide = widths[q]
        pred = pred_refs[q][...]
        other = other_refs[min(low // quarter, 2)]
        other_low = low - min(low // quarter, 2) * quarter
        target = in_order(core_ref[0], own_ref[:, low : low + wide], other[:, other_low : other_low + wide])
        cols = slice(at, at + 2 * wide)
        grad = -(target * gene_scale[:, cols] - gene_back[:, cols] * pred) / genes_total
        grad = grad - (target * spot_scale - spot_back * pred) / spots_total
        grad_low = grad.astype(bf16)
        turned_ref[at : at + 2 * wide, :] = grad_low.T
        prod = grad_low.astype(f32) * pred
        for k in range(0, 2 * wide, 128):
            folded = folded + prod[:, k : k + 128]
        at += 2 * wide
        low += wide
    inner_ref[...] = jnp.sum(folded.T, axis=0, keepdims=True)
    lane = lax.broadcasted_iota(jnp.int32, (1, 128), 1)
    gene_sum = jnp.sum(gene_cos, axis=1, keepdims=True)
    spot_sum = jnp.sum(spot_cos, axis=0, keepdims=True)
    sums_ref[...] = jnp.where(lane == 0, gene_sum, jnp.where(lane == 1, spot_sum, 0.0))


def grad_pred(core, widths, genes_total, spots_total, spot, gene, target, others, preds):
    half = target.shape[1]
    spots = spot.shape[0]
    genes = 2 * half
    return pl.pallas_call(
        functools.partial(grad_pred_kernel, widths, genes_total, spots_total),
        grid_spec=pltpu.PrefetchScalarGridSpec(
            num_scalar_prefetch=1,
            grid=(1,),
            in_specs=[VMEM] * 2
            + [pl.BlockSpec((spots, half), lambda i, core: (core[0], 0))]
            + [VMEM] * (3 + len(preds)),
            out_specs=[VMEM] * 3,
        ),
        out_shape=[
            pltpu.VMEM((genes, spots), bf16),
            jax.ShapeDtypeStruct((1, spots), f32),
            jax.ShapeDtypeStruct((1, 128), f32),
        ],
        compiler_params=params(20),
        cost_estimate=cost(spots * genes * 14, spots * genes * 10),
        name="grad_pred",
    )(core, spot, gene, target, *others, *preds)


def backward_kernel(widths, order_ref, logits_ref, enable_ref, retain_ref, col_ref, turned_ref, *refs):
    n = len(widths)
    panel_refs = refs[:n]
    grad_ref, row_ref = refs[n:]
    rows, spots = logits_ref.shape
    first = pl.multiple_of(pl.program_id(0) * rows, rows)
    enable = enable_ref[...].T
    retain = retain_ref[...].T
    shift, dens, inner = col_ref[0:1, :], col_ref[1:2, :], col_ref[2:3, :]
    part = rows // 2
    for h in range(2):
        here = pl.ds(first + h * part, part)
        near = slice(h * part, (h + 1) * part)
        panel = jnp.concatenate([ref[near if ref.shape[0] == rows else here, :] for ref in panel_refs], axis=1)
        grad_mapped = jnp.dot(panel, turned_ref[...], preferred_element_type=f32) + dens
        for k in range(part // 128):
            at = h * (part // 128) + k
            lines = slice(128 * at, 128 * (at + 1))
            block = jnp.where(enable[:, at : at + 1] > 0, logits_ref[lines, :], -1e30)
            mapping = jnp.exp(block - shift)
            grad = grad_mapped[128 * k : 128 * (k + 1), :]
            grad_ref[lines, :] = mapping * (retain[:, at : at + 1] * grad - inner)
            prod = grad * mapping
            folded = prod[:, 0:128]
            for c in range(128, spots, 128):
                folded = folded + prod[:, c : c + 128]
            row_ref[at : at + 1, :] = jnp.sum(folded.T, axis=0, keepdims=True)


def backward(order, logits, enable, retain, col, turned, panels):
    cells, spots = logits.shape
    genes = turned.shape[0]
    block = cells // PIECES
    widths = tuple(p.shape[1] for p in panels)
    streamed = (0,) + tuple(range(len(panels) - 2, len(panels)))
    cell = pl.BlockSpec((block // 128, 128), lambda i, order: (order[i], 0))
    return pl.pallas_call(
        functools.partial(backward_kernel, widths),
        grid_spec=pltpu.PrefetchScalarGridSpec(
            num_scalar_prefetch=1,
            grid=(PIECES,),
            in_specs=[
                pl.BlockSpec((block, spots), lambda i, order: (order[i], 0)),
                cell,
                cell,
                pl.BlockSpec((3, spots), lambda i, order: (0, 0)),
            ]
            + [VMEM]
            + [pl.BlockSpec((block, w), lambda i, order: (i, 0)) if q in streamed else VMEM for q, w in enumerate(widths)],
            out_specs=[pl.BlockSpec((block, spots), lambda i, order: (order[i], 0)), cell],
        ),
        out_shape=[
            jax.ShapeDtypeStruct((cells, spots), f32),
            jax.ShapeDtypeStruct((cells // 128, 128), f32),
        ],
        compiler_params=params(26),
        cost_estimate=cost(2 * cells * spots * genes, cells * 8 * spots, cells * spots),
        name="backward",
    )(order, logits, enable, retain, col, turned, *[in_hbm(p) if q in streamed else p for q, p in enumerate(panels)])


def join_kernel(*refs):
    at = 0
    for ref in refs[:-1]:
        refs[-1][at : at + ref.shape[0], :] = ref[...]
        at += ref.shape[0]


def join(*parts):
    rows = sum(p.shape[0] for p in parts)
    return pl.pallas_call(
        join_kernel,
        in_specs=[VMEM] * len(parts),
        out_specs=VMEM,
        out_shape=jax.ShapeDtypeStruct((rows, parts[0].shape[1]), bf16),
        compiler_params=params(12),
        cost_estimate=cost(0, 4 * rows * parts[0].shape[1]),
        name="join",
    )(*parts)


def select_kernel(inside_ref, b_ref, e_ref, c_ref, f_ref, *out_refs):
    rows = b_ref.shape[0]
    cut = out_refs[0].shape[1]
    for k, out in enumerate(out_refs):
        cols = slice(k * cut, (k + 1) * cut)
        for flag, refs in ((1, (b_ref, c_ref)), (0, (e_ref, f_ref))):

            @pl.when(inside_ref[0] == flag)
            def _(out=out, refs=refs, cols=cols):
                out[0:rows, :] = refs[0][:, cols]
                out[rows : 2 * rows, :] = refs[1][:, cols]


def select(inside, b, e, c, f, parts=1):
    rows, wide = b.shape
    return pl.pallas_call(
        select_kernel,
        in_specs=[pl.BlockSpec(memory_space=pltpu.SMEM)] + [VMEM] * 4,
        out_specs=[VMEM] * parts,
        out_shape=[jax.ShapeDtypeStruct((2 * rows, wide // parts), bf16)] * parts,
        compiler_params=params(12),
        cost_estimate=cost(0, 8 * rows * wide),
        name="select",
    )(inside, b, e, c, f)


def lay_kernel(core_ref, *refs):
    out_ref = refs[-1]
    n = (len(refs) - 1) // 2
    for mine, parts in ((True, refs[:n]), (False, refs[n : 2 * n])):

        @pl.when((pl.program_id(0) == core_ref[0]) == mine)
        def _(parts=parts):
            at = 0
            for ref in parts:
                out_ref[:, at : at + ref.shape[1]] = ref[...]
                at += ref.shape[1]


def lay(core, preds, theirs, half, column, begun=None):
    spots = preds[0].shape[0]
    wide = sum(p.shape[1] for p in theirs)
    return pl.pallas_call(
        lay_kernel,
        grid_spec=pltpu.PrefetchScalarGridSpec(
            num_scalar_prefetch=1,
            grid=(2,),
            in_specs=[pl.BlockSpec((spots, p.shape[1]), lambda i, core: (0, core[0])) for p in theirs]
            + [pl.BlockSpec((spots, p.shape[1]), lambda i, core: (0, 0)) for p in theirs]
            + ([] if begun is None else [pl.BlockSpec(memory_space=pl.ANY)]),
            out_specs=pl.BlockSpec((spots, wide), lambda i, core: (i, column)),
        ),
        out_shape=jax.ShapeDtypeStruct((2 * spots, half), f32),
        input_output_aliases={} if begun is None else {1 + 2 * len(preds): 0},
        compiler_params=params(24),
        cost_estimate=cost(0, spots * half * 16),
        name="lay",
    )(core, *[in_hbm(x) for x in (*preds, *theirs)], *(() if begun is None else (begun,)))


def swap_cells(x):
    return lax.ppermute(x, "cells", [(0, 1), (1, 0)])


def swap_genes(x):
    return lax.ppermute(x, "genes", [(0, 1), (1, 0)])


def sum_spots_genes(x, meanwhile=()):
    if lax.axis_size("spots") != 8:
        return lax.psum(x, ("spots", "genes")), meanwhile
    moved = [lax.ppermute(x, "spots", [(i, i ^ d) for i in range(8)]) for d in (2, 4, 6)]
    moved[0], moved[1], moved[2], *meanwhile = hold(*moved, *meanwhile)
    x = (x + moved[0]) + (moved[1] + moved[2])
    pairs = [lax.ppermute(x, ("spots", "genes"), [(i, i ^ d) for i in range(16)]) for d in (1, 2, 3)]
    return (x + pairs[0]) + (pairs[1] + pairs[2]), meanwhile


class Step:
    def __init__(self, logits, filter_logits, expression, spot_expression, cell_mask):
        self.logits = pltpu.with_memory_space_constraint(logits, pltpu.HBM)
        self.expression = expression
        self.core = lax.axis_index("genes")
        self.enable = cell_mask.astype(f32).reshape(-1, 128)
        self.retain = jax.nn.sigmoid(filter_logits).reshape(-1, 128)
        self.spots = logits.shape[1]
        self.core_flag = self.core.astype(jnp.int32).reshape(1)
        self.half = expression.shape[1]
        self.target = spot_expression
        sent = lax.dynamic_slice_in_dim(spot_expression, (1 - self.core) * self.spots, self.spots, 0)
        quarter = self.half // 4
        self.target_sent = [sent[:, :quarter], sent[:, quarter : 2 * quarter], sent[:, 2 * quarter :]]

    def local_stats(self):
        part = col_stats(self.logits, self.enable, self.retain)
        count = jnp.broadcast_to(jnp.sum(self.enable * self.retain), (1, self.spots))
        return jnp.concatenate([part, count], axis=0)

    def merge_stats(self, part, away):
        top = jnp.maximum(part[0], away[0])
        here, there = jnp.exp(part[0] - top), jnp.exp(away[0] - top)
        total = part[1] * here + away[1] * there
        self.density = (part[2] * here + away[2] * there) / total
        self.cell_count = part[3, 0] + away[3, 0]
        self.shift = (top + jnp.log(total))[None, :]

    def turned(self, order, shift, logits):
        return mapped_turned(order, logits, self.enable, self.retain, shift)

    def stats(self, parts, other, at, wide):
        begin = self.half - other.shape[1] if other.shape[1] > self.half // 4 else at // (self.half // 4) * (self.half // 4)
        return pred_stats(self.core_flag, parts, self.target, other, at // wide, (at - begin) // wide, wide)

    def gathered_whole(self):
        own = lax.all_gather(self.expression, "spots", axis=0, tiled=True)
        other = swap_genes(own)
        part = self.local_stats()
        self.target_other = [swap_genes(x) for x in self.target_sent]
        self.merge_stats(part, swap_cells(part))
        order = jnp.arange(PIECES, dtype=jnp.int32)
        mapped = self.turned(order, self.shift, self.logits)
        wide = self.half // 4
        table = tuple((0, r) for r in range(PIECES))
        chunks = []
        for q in range(4):
            partial, panel = forward(self.core_flag, mapped, [(own, other)], table, [q], wide)
            chunks.append((wide, panel) + tuple(self.stats([lax.psum(partial, "cells")], self.target_other[min(q, 2)], q * wide, wide)))
        return order, chunks

    def gathered_line(self):
        near_pairs = [(2 * z + y, 2 * (z ^ 1) + y) for z in range(4) for y in range(2)]
        middle_pairs = [(2 * z + y, 2 * (3 - z) + y) for z in (1, 2) for y in range(2)]
        across_pairs = [(i, i ^ 1) for i in range(8)]

        def near(x):
            return lax.ppermute(x, "spots", near_pairs)

        def middle(x):
            return lax.ppermute(x, "spots", middle_pairs)

        def across(x):
            return lax.ppermute(x, "spots", across_pairs)

        spot = lax.axis_index("spots")
        z, y = spot // 2, spot % 2
        inside = (z == 1) | (z == 2)
        inside_flag = inside.astype(jnp.int32).reshape(1)
        column = jnp.stack([z, z ^ 1, jnp.where(z < 2, 2, 1), jnp.where(z < 2, 3, 0)])
        order = jnp.concatenate([2 * column + y, 2 * column + (1 - y)]).astype(jnp.int32)
        unit = self.half // 8
        expr = self.expression

        def cut(x, at, wide):
            return x[:, at * unit : (at + wide) * unit]

        def pick(b, e, c, f, parts=1):
            return select(inside_flag, b, e, c, f, parts)

        first = ((0, 0), (1, 0), (2, 0), (2, 1), (3, 0), (4, 0), (5, 0), (5, 1))
        early = ((0, 0), (1, 0), (2, 0), (2, 2), (3, 0), (1, 1), (2, 1), (2, 3))
        core = self.core_flag

        def run(sources, table, columns, wide):
            return forward(core, mapped, sources, table, columns, wide * unit)

        s01 = cut(expr, 0, 4)
        beside = across(expr)
        a01 = near(s01)
        b01 = middle(s01)
        expr_o = swap_genes(expr)
        target_0 = swap_genes(self.target_sent[0])
        part = self.local_stats()
        a01, b01, part, target_0, sv, target_1 = hold(
            a01, b01, part, target_0, cut(expr, 4, 3), self.target_sent[1]
        )
        c01 = middle(a01)
        e01 = near(b01)
        away = swap_cells(part)
        target_1 = swap_genes(target_1)
        self.merge_stats(part, away)
        mapped = self.turned(order, self.shift, self.logits)
        beside, e01, c01, expr_o, mapped, a01, sv, target_1 = hold(
            beside, e01, c01, expr_o, mapped, a01, sv, target_1
        )
        yn = across(a01)
        f01 = near(c01)
        beside_o = swap_genes(beside)
        a01_o = swap_genes(a01)
        bv = middle(sv)
        yn, f01, a01_o, sv, beside = hold(yn, f01, a01_o, sv, beside)
        mf0, mf1 = pick(b01, e01, c01, f01, 2)
        ymf0 = across(mf0)
        av = near(sv)
        mf0_o, yn_o = swap_genes(mf0), swap_genes(yn)
        sf = join(cut(expr, 7, 1), cut(beside, 7, 1))
        ymf0, av, mf0_o, yn_o, beside_o, mf1, bv, mapped = hold(ymf0, av, mf0_o, yn_o, beside_o, mf1, bv, mapped)
        ymf1 = across(mf1)
        ev = near(bv)
        cv = middle(av)
        ymf0_o, mf1_o = swap_genes(ymf0), swap_genes(mf1)
        expr_2, a01_2, beside_2, yn_2 = (expr, expr_o), (a01, a01_o), (beside, beside_o), (yn, yn_o)
        partial0, panel0 = run(
            [expr_2, a01_2, (mf0, mf0_o), beside_2, yn_2, (ymf0, ymf0_o)], first, (0, 0, 0, 0, 0, 0), 2
        )
        ymf1, ev, cv, partial0, mf1_o, av, mapped = hold(ymf1, ev, cv, partial0, mf1_o, av, mapped)
        ynv = across(av)
        fv = near(cv)
        ymf1_o = swap_genes(ymf1)
        away0 = swap_cells(partial0)
        av_o = swap_genes(av)
        partial1, panel1 = run(
            [expr_2, a01_2, (mf1, mf1_o), beside_2, yn_2, (ymf1, ymf1_o)], first, (1, 1, 0, 1, 1, 0), 2
        )
        ynv, fv, partial1, av_o, sf = hold(ynv, fv, partial1, av_o, sf)
        m2, m3, m4 = pick(bv, ev, cv, fv, 3)
        ym2 = across(m2)
        af = near(sf)
        away1 = swap_cells(partial1)
        ynv_o = swap_genes(ynv)
        ym2, af, ynv_o, away0, m2, m3, sf, mapped = hold(ym2, af, ynv_o, away0, m2, m3, sf, mapped)
        ym3 = across(m3)
        bf = middle(sf)
        ym2_o, m2_o = swap_genes(ym2), swap_genes(m2)
        av_2, ynv_2 = (av, av_o), (ynv, ynv_o)
        partial2, panel2 = run([expr_2, av_2, (m2, m2_o), beside_2, ynv_2, (ym2, ym2_o)], first, (4, 0, 0, 4, 0, 0), 1)
        stats0 = self.stats([partial0, away0], target_0, 0, 2 * unit)
        ym3, bf, partial2, away1, m3, m4, af, mapped, *stats0 = hold(
            ym3, bf, partial2, away1, m3, m4, af, mapped, *stats0
        )
        ym4 = across(m4)
        ef, cf = near(bf), middle(af)
        ym3_o, m3_o = swap_genes(ym3), swap_genes(m3)
        partial3, panel3 = run([expr_2, av_2, (m3, m3_o), beside_2, ynv_2, (ym3, ym3_o)], first, (5, 1, 0, 5, 1, 0), 1)
        stats1 = self.stats([partial1, away1], target_1, 2 * unit, 2 * unit)
        ym4, ef, cf, partial3, partial2, m4, mapped, *stats1 = hold(
            ym4, ef, cf, partial3, partial2, m4, mapped, *stats1
        )
        ff = near(cf)
        ym4_o, m4_o = swap_genes(ym4), swap_genes(m4)
        away2 = swap_cells(partial2)
        away3 = swap_cells(partial3)
        partial4, panel4 = run([expr_2, av_2, (m4, m4_o), beside_2, ynv_2, (ym4, ym4_o)], first, (6, 2, 0, 6, 2, 0), 1)
        ff, partial4, away2, af, mapped, target_2 = hold(ff, partial4, away2, af, mapped, self.target_sent[2])
        away4 = swap_cells(partial4)
        (mff,) = pick(bf, ef, cf, ff)
        mff_o, af_o = swap_genes(mff), swap_genes(af)
        target_2 = swap_genes(target_2)
        self.target_other = (target_0, target_1, target_2)
        partialf, panelf = run([expr_2, (af, af_o), (mff, mff_o), beside_2], early, (7, 0, 0, 7), 1)
        stats2 = self.stats([partial2, away2], target_2, 4 * unit, unit)
        partialf, away3, *stats2 = hold(partialf, away3, *stats2)
        stats3 = self.stats([partial3, away3], target_2, 5 * unit, unit)
        awayf = swap_cells(partialf)
        stats4 = self.stats([partial4, away4], target_2, 6 * unit, unit)
        statsf = self.stats([partialf, awayf], target_2, 7 * unit, unit)
        return order, [
            (2 * unit, panel0, *stats0),
            (2 * unit, panel1, *stats1),
            (unit, panel2, *stats2),
            (unit, panel3, *stats3),
            (unit, panel4, *stats4),
            (unit, panelf, *statsf),
        ]


def body(logits, filter_logits, expression, spot_expression, cell_mask, spot_counts):
    cells_total = logits.shape[0] * lax.axis_size("cells")
    spots = logits.shape[1]
    spots_total = spots * lax.axis_size("spots") * lax.axis_size("genes")
    genes_total = expression.shape[1] * lax.axis_size("genes")
    step = Step(logits, filter_logits, expression, spot_expression, cell_mask)
    order, chunks = step.gathered_line() if lax.axis_size("spots") == 8 else step.gathered_whole()
    widths, panels, preds, gene_stats, spot_stats, sent = zip(*chunks)
    density = step.density

    counts = spot_counts.astype(f32)
    kl_parts = jnp.stack([jnp.sum(density), jnp.sum(counts * (jnp.log(counts) - jnp.log(density))), jnp.sum(counts)])

    kl_block = jnp.broadcast_to(kl_parts[:, None], (3, 128))
    theirs = [swap_genes(x) for x in sent]
    half = expression.shape[1]
    split = len(widths) - 2
    predicted = lay(step.core_flag, preds[:split], theirs[:split], half, 0)
    gene, (predicted,) = sum_spots_genes(jnp.concatenate(gene_stats + (kl_block,), axis=1), (predicted,))
    dens_total, kl_part, count_total = gene[0, -1], gene[1, -1], gene[2, -1]
    kl_term = kl_part / count_total - jnp.log(count_total) + jnp.log(dens_total)
    offset = (step.cell_count - 0.5 * cells_total) / cells_total
    penalty = jnp.sqrt(offset * offset + 0.01)
    dens_grad = -counts / (count_total * density) + 1.0 / dens_total
    spot = functools.reduce(jnp.add, spot_stats)

    turned, inner, sums = grad_pred(
        step.core_flag, widths, genes_total, spots_total, spot, gene, step.target, step.target_other, preds
    )
    col = jnp.concatenate([step.shift, dens_grad[None], inner + (density * dens_grad)[None]], axis=0)
    grad_logits, row = backward(order, step.logits, step.enable, step.retain, col, turned, panels)

    row, core = hold(row, step.core_flag)
    late = sum(widths[split:])
    predicted = lay(core, preds[split:], theirs[split:], half, (half - late) // late, predicted)
    row_sums, (predicted,) = sum_spots_genes(jnp.concatenate([row, sums], axis=0), (predicted,))
    copies = lax.axis_size("spots") * lax.axis_size("genes")
    gene_sum, spot_sum = row_sums[-1, 0] / copies, row_sums[-1, 1]
    total_loss = -gene_sum / genes_total - spot_sum / spots_total + kl_term + penalty
    retain_grad = row_sums[:-1] + step.enable * offset / (penalty * cells_total)
    filter_grad = (retain_grad * step.retain * (1.0 - step.retain)).reshape(-1)

    return (predicted, total_loss, grad_logits, filter_grad)


def solution(mesh):
    placed = (
        P("cells", ("spots", "genes")),
        P("cells"),
        P(("cells", "spots"), "genes"),
        P("spots", "genes"),
        P("cells"),
        P(("spots", "genes")),
    )
    return jax.shard_map(
        body,
        mesh=mesh,
        in_specs=placed,
        out_specs=(P("spots", "genes"), P(), P("cells", ("spots", "genes")), P("cells")),
        check_vma=False,
    )
```

time: 376 us -> 325 us (0.86)
  between operations: 22.6 us -> 8.96 us
  waiting for transfers between devices: 110 us -> 98.8 us
  local copies, waits for them, and re-layouts: 32.2 us -> 23.1 us
  Pallas kernels: 127 us -> 120 us
  other arithmetic: 11.6 us -> 5.51 us
  starting transfers between devices: 71.5 us -> 67.6 us
    ppermute x8 -> x9, waiting for transfers between devices: 68.5 us -> 35.8 us  [near(): return lax.ppermute(x, 'spots', near_pairs)]
    ppermute x9 -> x8, waiting for transfers between devices: 19.5 us -> 36.7 us  [across(): return lax.ppermute(x, 'spots', across_pairs)]
    ppermute x7, waiting for transfers between devices: 10 us -> 23.1 us  [swap_cells(): return lax.ppermute(x, 'cells', [(0, 1), (1, 0)])]
    unnamed x111 -> x139, local copies, waits for them, and re-layouts: 23.2 us -> 10.7 us
    ppermute x8 -> x9, starting transfers between devices: 31.8 us -> 22.3 us  [near(): return lax.ppermute(x, 'spots', near_pairs)]
    ppermute x6, waiting for transfers between devices: 6.2 us -> 0.96 us  [sum_spots_genes(): lax.ppermute(x, 'spots', [(i, i ^ d) for i in range(8)])]
    unnamed x7 -> x1, other arithmetic: 4.08 us -> 0.01 us
    ppermute x9 -> x8, starting transfers between devices: 9.65 us -> 10.5 us  [across(): return lax.ppermute(x, 'spots', across_pairs)]
  transfers between devices with their start and end apart: 61 -> 69, of which waited for: 21 -> 23; matrix products, arithmetic and copies ran while one was open for 5% -> 5% of each run, Pallas kernels for 33% -> 37%
where the time goes in v4:
time: 325 us; the launch traced here: 324 us
  Pallas kernels  120 us (37%)
  waiting for transfers between devices  98.8 us (30%)
  starting transfers between devices  67.6 us (21%)
  local copies, waits for them, and re-layouts  23.1 us (7%)
  between operations  8.96 us (3%)
  other arithmetic  5.51 us (2%)
    pallas_call x6, Pallas kernels, forward(): pl.pallas_call(functools.partial(forward_kernel, pieces, table, columns,...  51 us
    ppermute x8, waiting for transfers between devices, across(): return lax.ppermute(x, 'spots', across_pairs)  36.7 us
    ppermute x9, waiting for transfers between devices, near(): return lax.ppermute(x, 'spots', near_pairs)  35.8 us
    pallas_call x1, Pallas kernels, backward(): pl.pallas_call(functools.partial(backward_kernel, widths), grid_spec=pltp...  25.6 us
    ppermute x7, waiting for transfers between devices, swap_cells(): return lax.ppermute(x, 'cells', [(0, 1), (1, 0)])  23.1 us
    ppermute x9, starting transfers between devices, near(): return lax.ppermute(x, 'spots', near_pairs)  22.3 us
    pallas_call x1, Pallas kernels, mapped_turned(): pl.pallas_call(mapped_kernel, grid_spec=pltpu.PrefetchScalarGridSpec(num_...  15.6 us
    pallas_call x1, Pallas kernels, col_stats(): pl.pallas_call(col_stats_kernel, grid=(cells // block,), in_specs=[pl.Blo...  10.9 us
  transfers between devices with their start and end apart: 69, of which 23 were waited for; matrix products, arithmetic and copies ran while one was open for 5% of the time, Pallas kernels for 37%

profile of v4, /device:TPU:0, one launch (start us, length us, event | category | flops | bytes accessed | tf_op | source)
XLA Modules:
  0.0 324.5 jit_solution(16194379155242205923)
XLA Ops:
  2.0 3.1 collective-permute-start
  7.4 2.1 fusion.12
  10.6 10.9 %col_stats.1 = f32[3,512]{1,0:T(4,128)S(1)} custom-call(f32[8192,512]{1,0:T(8,128)} %logits_ref.5, f32[64,128]{1,0:T(8,128)S(1)} %convert_bitcast_fusion.enable_ref, f32[64,128]{1,0:T(8,128)S(1)} %get-tuple-element.296.retain_ref), custom_call_target="tpu_custom_call" | custom-call | flops 1 | bytes 1 | tf_op jit(solution)/shard_map/col_stats/pallas_call | solution.py:76
  21.4 2.2 slice.67
  24.2 4.1 %collective-permute-done.refs_1_ = bf16[1024,512]{1,0:T(8,128)(2,1)} collective-permute-done((bf16[1024,512]{1,0:T(8,128)(2,1)S(1)}, bf16[1024,512]{1,0:T(8,128)(2,1)}, u32[]{:S(2)}, u32[]{:S(2)}) %collective-permute-start) | collective-permute-done | bytes 1048608 | tf_op jit(solution)/shard_map/ppermute | solution.py:526
  28.3 4.7 %collective-permute-start.5 = (bf16[1024,512]{1,0:T(8,128)(2,1)S(1)}, bf16[1024,512]{1,0:T(8,128)(2,1)S(1)}, u32[]{:S(2)}, u32[]{:S(2)}) collective-permute-start(bf16[1024,512]{1,0:T(8,128)(2,1)S(1)} %collective-permute-done.1.b_ref), channel_id=1, source_target_pairs={{0,4},{2,6},{4,0},{6,2},{8,12},{10,14},{12,8},{14,10},{1,5},{3,7},... | collective-permute-start | bytes 3145736 | tf_op jit(solution)/shard_map/ppermute | solution.py:526
  36.2 2.1 collective-permute-done.3
  39.0 15.6 %mapped_turned.1.mapped_ref = bf16[512,8192]{1,0:T(8,128)(2,1)} custom-call(s32[8]{0:T(128)S(1)} %pad_add_fusion.order_ref, f32[8192,512]{1,0:T(8,128)} %logits_ref.5, f32[64,128]{1,0:T(8,128)S(1)} %convert_bitcast_fusion.enable_ref, f32[64,128]{1,0:T(8,128)S(1)} %get-tuple-element.296.retain_ref, f32[1,512]{1,0:T(1,128)S(1)} %get-tuple-element.298.shift_ref), custom_call_target="tpu_custom_call" | custom-call | flops 1 | bytes 1 | tf_op jit(solution)/shard_map/mapped_turned/pallas_call | solution.py:104
  56.9 3.9 %collective-permute-start.10 = (bf16[1024,512]{1,0:T(8,128)(2,1)}, bf16[1024,512]{1,0:T(8,128)(2,1)}, u32[]{:S(2)}, u32[]{:S(2)}) collective-permute-start(bf16[1024,512]{1,0:T(8,128)(2,1)} %collective-permute-done.6.c_ref), channel_id=1, source_target_pairs={{0,4},{2,6},{4,0},{6,2},{8,12},{10,14},{12,8},{14,10},{1,5},{3,7},... | collective-permute-start | bytes 3145736 | tf_op jit(solution)/shard_map/ppermute | solution.py:526
  62.9 17.7 %collective-permute-done.9.refs_4_ = bf16[1024,512]{1,0:T(8,128)(2,1)} collective-permute-done((bf16[1024,512]{1,0:T(8,128)(2,1)}, bf16[1024,512]{1,0:T(8,128)(2,1)}, u32[]{:S(2)}, u32[]{:S(2)}) %collective-permute-start.9) | collective-permute-done | bytes 1048608 | tf_op jit(solution)/shard_map/ppermute | solution.py:532
  86.9 17.9 %collective-permute-done.13.refs_1_ = bf16[1024,384]{1,0:T(8,128)(2,1)S(1)} collective-permute-done((bf16[1024,384]{1,0:T(8,128)(2,1)}, bf16[1024,384]{1,0:T(8,128)(2,1)S(1)}, u32[]{:S(2)}, u32[]{:S(2)}) %collective-permute-start.13) | collective-permute-done | bytes 786464 | tf_op jit(solution)/shard_map/ppermute | solution.py:526
  110.5 9.4 %forward.6 = (f32[512,512]{1,0:T(8,128)S(1)}, bf16[8192,512]{1,0:T(8,128)(2,1)}) custom-call(s32[1]{0:T(128)} %bitcast.7.core_ref, bf16[512,8192]{1,0:T(8,128)(2,1)} %mapped_turned.1.mapped_ref, bf16[1024,1024]{1,0:T(8,128)(2,1)} %refs_0_.11, bf16[1024,512]{1,0:T(8,128)(2,1)} %collective-permute-done.refs_1_, bf16[2048,256]{1,0:T(8,128)(2,1)} %copy-done.16, ...), custom_call_target="tpu_custom_call" | custom-call | flops 1 | bytes 1 | tf_op jit(solution)/shard_map/forward/pallas_call | solution.py:174
  119.9 8.4 %collective-permute-done.19.e_ref = bf16[1024,384]{1,0:T(8,128)(2,1)S(1)} collective-permute-done((bf16[1024,384]{1,0:T(8,128)(2,1)}, bf16[1024,384]{1,0:T(8,128)(2,1)S(1)}, u32[]{:S(2)}, u32[]{:S(2)}) %collective-permute-start.19) | collective-permute-done | bytes 786464 | tf_op jit(solution)/shard_map/ppermute | solution.py:526
  128.3 3.8 %collective-permute-done.18.refs_5_ = bf16[2048,256]{1,0:T(8,128)(2,1)S(1)} collective-permute-done((bf16[2048,256]{1,0:T(8,128)(2,1)S(1)}, bf16[2048,256]{1,0:T(8,128)(2,1)S(1)}, u32[]{:S(2)}, u32[]{:S(2)}) %collective-permute-start.18) | collective-permute-done | bytes 1048608 | tf_op jit(solution)/shard_map/ppermute | solution.py:532
  138.8 9.5 %forward.7 = (f32[512,512]{1,0:T(8,128)S(1)}, bf16[8192,512]{1,0:T(8,128)(2,1)}) custom-call(s32[1]{0:T(128)} %bitcast.7.core_ref, bf16[512,8192]{1,0:T(8,128)(2,1)} %mapped_turned.1.mapped_ref, bf16[1024,1024]{1,0:T(8,128)(2,1)} %refs_0_.11, bf16[1024,512]{1,0:T(8,128)(2,1)} %collective-permute-done.refs_1_, bf16[2048,256]{1,0:T(8,128)(2,1)} %copy-done.15, ...), custom_call_target="tpu_custom_call" | custom-call | flops 1 | bytes 1 | tf_op jit(solution)/shard_map/forward/pallas_call | solution.py:174
  148.3 3.9 %collective-permute-done.23.refs_4_ = bf16[1024,384]{1,0:T(8,128)(2,1)S(1)} collective-permute-done((bf16[1024,384]{1,0:T(8,128)(2,1)S(1)}, bf16[1024,384]{1,0:T(8,128)(2,1)S(1)}, u32[]{:S(2)}, u32[]{:S(2)}) %collective-permute-start.23) | collective-permute-done | bytes 786464 | tf_op jit(solution)/shard_map/ppermute | solution.py:532
  160.2 9.0 %collective-permute-done.27.refs_5_ = bf16[2048,128]{1,0:T(8,128)(2,1)S(1)} collective-permute-done((bf16[2048,128]{1,0:T(8,128)(2,1)S(1)}, bf16[2048,128]{1,0:T(8,128)(2,1)S(1)}, u32[]{:S(2)}, u32[]{:S(2)}) %collective-permute-start.27) | collective-permute-done | bytes 524320 | tf_op jit(solution)/shard_map/ppermute | solution.py:532
  175.2 8.0 %forward.8 = (f32[512,256]{1,0:T(8,128)S(1)}, bf16[8192,256]{1,0:T(8,128)(2,1)}) custom-call(s32[1]{0:T(128)} %bitcast.7.core_ref, bf16[512,8192]{1,0:T(8,128)(2,1)} %mapped_turned.1.mapped_ref, bf16[1024,1024]{1,0:T(8,128)(2,1)} %refs_0_.11, bf16[1024,384]{1,0:T(8,128)(2,1)} %copy-done.30, bf16[2048,128]{1,0:T(8,128)(2,1)} %copy-done.19, ...), custom_call_target="tpu_custom_call" | custom-call | flops 1 | bytes 1 | tf_op jit(solution)/shard_map/forward/pallas_call | solution.py:174
  186.1 3.5 %collective-permute-start.37 = (bf16[2048,128]{1,0:T(8,128)(2,1)S(1)}, bf16[2048,128]{1,0:T(8,128)(2,1)S(1)}, u32[]{:S(2)}, u32[]{:S(2)}) collective-permute-start(bf16[2048,128]{1,0:T(8,128)(2,1)S(1)} %collective-permute-done.32.b_ref), channel_id=1, source_target_pairs={{0,4},{2,6},{4,0},{6,2},{8,12},{10,14},{12,8},{14,10},{1,5},{3,7},... | collective-permute-start | bytes 1572872 | tf_op jit(solution)/shard_map/ppermute | solution.py:526
  193.3 8.0 %forward.9 = (f32[512,256]{1,0:T(8,128)S(1)}, bf16[8192,256]{1,0:T(8,128)(2,1)}) custom-call(s32[1]{0:T(128)} %bitcast.7.core_ref, bf16[512,8192]{1,0:T(8,128)(2,1)} %mapped_turned.1.mapped_ref, bf16[1024,1024]{1,0:T(8,128)(2,1)} %refs_0_.11, bf16[1024,384]{1,0:T(8,128)(2,1)} %copy-done.30, bf16[2048,128]{1,0:T(8,128)(2,1)} %copy-done.18, ...), custom_call_target="tpu_custom_call" | custom-call | flops 1 | bytes 1 | tf_op jit(solution)/shard_map/forward/pallas_call | solution.py:174
  202.8 2.9 collective-permute-start.41
  208.6 8.1 %forward.10 = (f32[512,256]{1,0:T(8,128)S(1)}, bf16[8192,256]{1,0:T(8,128)(2,1)}) custom-call(s32[1]{0:T(128)} %bitcast.7.core_ref, bf16[512,8192]{1,0:T(8,128)(2,1)} %mapped_turned.1.mapped_ref, bf16[1024,1024]{1,0:T(8,128)(2,1)} %refs_0_.11, bf16[1024,384]{1,0:T(8,128)(2,1)} %copy-done.30, bf16[2048,128]{1,0:T(8,128)(2,1)} %copy-done.17, ...), custom_call_target="tpu_custom_call" | custom-call | flops 1 | bytes 1 | tf_op jit(solution)/shard_map/forward/pallas_call | solution.py:174
  224.2 2.0 pad_maximum_fusion.1
  228.5 8.0 %forward.11 = (f32[512,256]{1,0:T(8,128)S(1)}, bf16[8192,256]{1,0:T(8,128)(2,1)}) custom-call(s32[1]{0:T(128)} %bitcast.7.core_ref, bf16[512,8192]{1,0:T(8,128)(2,1)} %mapped_turned.1.mapped_ref, bf16[1024,1024]{1,0:T(8,128)(2,1)} %refs_0_.11, bf16[2048,128]{1,0:T(8,128)(2,1)} %copy-done.42, bf16[4096,128]{1,0:T(8,128)(2,1)} %copy-done.8, ...), custom_call_target="tpu_custom_call" | custom-call | flops 1 | bytes 1 | tf_op jit(solution)/shard_map/forward/pallas_call | solution.py:174
  238.9 8.5 %collective-permute-done.49.refs_1_ = f32[512,256]{1,0:T(8,128)S(1)} collective-permute-done((f32[512,256]{1,0:T(8,128)S(1)}, f32[512,256]{1,0:T(8,128)S(1)}, u32[]{:S(2)}, u32[]{:S(2)}) %collective-permute-start.49) | collective-permute-done | bytes 524320 | tf_op jit(solution)/shard_map/ppermute | solution.py:452
  248.4 9.8 %collective-permute-done.50.refs_1_ = f32[512,256]{1,0:T(8,128)S(1)} collective-permute-done((f32[512,256]{1,0:T(8,128)S(1)}, f32[512,256]{1,0:T(8,128)S(1)}, u32[]{:S(2)}, u32[]{:S(2)}) %collective-permute-start.50) | collective-permute-done | bytes 524320 | tf_op jit(solution)/shard_map/ppermute | solution.py:452
  261.6 2.0 collective-permute-start.53
  264.4 3.8 %lay.2.refs_4_ = f32[1024,1024]{1,0:T(8,128)} custom-call(s32[1]{0:T(128)} %bitcast.7.core_ref, f32[512,512]{1,0:T(8,128)} %copy-done.4, f32[512,512]{1,0:T(8,128)} %copy-done.6, f32[512,256]{1,0:T(8,128)} %copy-done.10, f32[512,256]{1,0:T(8,128)} %copy-done.13, f32[512,256]{1,0:T(8,128)} %copy-done.44, f32[512,256]{1,0:T(8,128)} %copy-done.45, ...), custom_call_target="tpu_custom_call" | custom-call | flops 1 | bytes 1 | tf_op jit(solution)/shard_map/lay/pallas_call | solution.py:433
  275.3 2.7 grad_pred.1
  278.1 25.6 %backward.1 = (f32[8192,512]{1,0:T(8,128)}, f32[64,128]{1,0:T(8,128)S(1)}) custom-call(s32[8]{0:T(128)S(1)} %pad_add_fusion.order_ref, f32[8192,512]{1,0:T(8,128)} %logits_ref.5, f32[64,128]{1,0:T(8,128)S(1)} %convert_bitcast_fusion.enable_ref, f32[64,128]{1,0:T(8,128)S(1)} %get-tuple-element.296.retain_ref, f32[3,512]{1,0:T(4,128)S(1)} %pad_maximum_fusion.col_ref, ...), custom_call_target="tpu_custom_call" | custom-call | flops 1 | bytes 1 | tf_op jit(solution)/shard_map/backward/pallas_call | solution.py:346
  303.8 3.2 collective-permute-start.62
  309.6 2.2 lay.3
  (298 shorter events, 89.0 us)
Async XLA Ops:
  2.0 26.4 %collective-permute-start = (bf16[1024,512]{1,0:T(8,128)(2,1)S(1)}, bf16[1024,512]{1,0:T(8,128)(2,1)}, u32[]{:S(2)}, u32[]{:S(2)}) collective-permute-start(bf16[1024,512]{1,0:T(8,128)(2,1)S(1)} %slice.65), channel_id=1, source_target_pairs={{0,4},{2,6},{4,0},{6,2},{8,12},{10,14},{12,8},{14,10},{1,5},{3,7},... | collective-permute-start | bytes 3145736 | tf_op jit(solution)/shard_map/ppermute | solution.py:526
  5.0 23.3 %collective-permute-start.1 = (bf16[1024,512]{1,0:T(8,128)(2,1)S(1)}, bf16[1024,512]{1,0:T(8,128)(2,1)S(1)}, u32[]{:S(2)}, u32[]{:S(2)}) collective-permute-start(bf16[1024,512]{1,0:T(8,128)(2,1)S(1)} %slice.65), channel_id=1, source_target_pairs={{4,8},{6,10},{8,4},{10,6},{5,9},{7,11},{9,5},{11,7},{20,24},{22,26... | collective-permute-start | bytes 3145736 | tf_op jit(solution)/shard_map/ppermute | solution.py:529
  5.8 48.8 %collective-permute-start.4 = (bf16[1024,1024]{1,0:T(8,128)(2,1)}, bf16[1024,1024]{1,0:T(8,128)(2,1)}, u32[]{:S(2)}, u32[]{:S(2)}) collective-permute-start(bf16[1024,1024]{1,0:T(8,128)(2,1)} %refs_0_.11), channel_id=1, source_target_pairs={{0,2},{2,0},{4,6},{6,4},{8,10},{10,8},{12,14},{14,12},{1,3},{3,1},... | collective-permute-start | bytes 6291464 | tf_op jit(solution)/shard_map/ppermute | solution.py:532
  7.4 48.0 %collective-permute-start.7 = (bf16[1024,1024]{1,0:T(8,128)(2,1)}, bf16[1024,1024]{1,0:T(8,128)(2,1)}, u32[]{:S(2)}, u32[]{:S(2)}) collective-permute-start(bf16[1024,1024]{1,0:T(8,128)(2,1)} %refs_0_.11), channel_id=1, source_target_pairs={{0,1},{1,0},{2,3},{3,2},{4,5},{5,4},{6,7},{7,6},{8,9},{9,8},{10,11... | collective-permute-start | bytes 6291464 | tf_op jit(solution)/shard_map/ppermute | solution.py:456
  28.3 27.0 %collective-permute-start.5 = (bf16[1024,512]{1,0:T(8,128)(2,1)S(1)}, bf16[1024,512]{1,0:T(8,128)(2,1)S(1)}, u32[]{:S(2)}, u32[]{:S(2)}) collective-permute-start(bf16[1024,512]{1,0:T(8,128)(2,1)S(1)} %collective-permute-done.1.b_ref), channel_id=1, source_target_pairs={{0,4},{2,6},{4,0},{6,2},{8,12},{10,14},{12,8},{14,10},{1,5},{3,7},... | collective-permute-start | bytes 3145736 | tf_op jit(solution)/shard_map/ppermute | solution.py:526
  33.0 22.4 %collective-permute-start.6 = (bf16[1024,512]{1,0:T(8,128)(2,1)}, bf16[1024,512]{1,0:T(8,128)(2,1)}, u32[]{:S(2)}, u32[]{:S(2)}) collective-permute-start(bf16[1024,512]{1,0:T(8,128)(2,1)} %collective-permute-done.refs_1_), channel_id=1, source_target_pairs={{4,8},{6,10},{8,4},{10,6},{5,9},{7,11},{9,5},{11,7},{20,24},{22,26... | collective-permute-start | bytes 3145736 | tf_op jit(solution)/shard_map/ppermute | solution.py:529
  55.4 25.2 %collective-permute-start.9 = (bf16[1024,512]{1,0:T(8,128)(2,1)}, bf16[1024,512]{1,0:T(8,128)(2,1)}, u32[]{:S(2)}, u32[]{:S(2)}) collective-permute-start(bf16[1024,512]{1,0:T(8,128)(2,1)} %collective-permute-done.refs_1_), channel_id=1, source_target_pairs={{0,2},{2,0},{4,6},{6,4},{8,10},{10,8},{12,14},{14,12},{1,3},{3,1},... | collective-permute-start | bytes 3145736 | tf_op jit(solution)/shard_map/ppermute | solution.py:532
  56.9 25.4 %collective-permute-start.10 = (bf16[1024,512]{1,0:T(8,128)(2,1)}, bf16[1024,512]{1,0:T(8,128)(2,1)}, u32[]{:S(2)}, u32[]{:S(2)}) collective-permute-start(bf16[1024,512]{1,0:T(8,128)(2,1)} %collective-permute-done.6.c_ref), channel_id=1, source_target_pairs={{0,4},{2,6},{4,0},{6,2},{8,12},{10,14},{12,8},{14,10},{1,5},{3,7},... | collective-permute-start | bytes 3145736 | tf_op jit(solution)/shard_map/ppermute | solution.py:526
  60.8 21.5 %collective-permute-start.11 = (bf16[1024,512]{1,0:T(8,128)(2,1)}, bf16[1024,512]{1,0:T(8,128)(2,1)}, u32[]{:S(2)}, u32[]{:S(2)}) collective-permute-start(bf16[1024,512]{1,0:T(8,128)(2,1)} %collective-permute-done.refs_1_), channel_id=1, source_target_pairs={{0,1},{1,0},{2,3},{3,2},{4,5},{5,4},{6,7},{7,6},{8,9},{9,8},{10,11... | collective-permute-start | bytes 3145736 | tf_op jit(solution)/shard_map/ppermute | solution.py:456
  60.8 45.6 %collective-permute-start.16 = (bf16[1024,1024]{1,0:T(8,128)(2,1)}, bf16[1024,1024]{1,0:T(8,128)(2,1)}, u32[]{:S(2)}, u32[]{:S(2)}) collective-permute-start(bf16[1024,1024]{1,0:T(8,128)(2,1)} %collective-permute-done.4.refs_3_), channel_id=1, source_target_pairs={{0,1},{1,0},{2,3},{3,2},{4,5},{5,4},{6,7},{7,6},{8,9},{9,8},{10,11... | collective-permute-start | bytes 6291464 | tf_op jit(solution)/shard_map/ppermute | solution.py:456
  61.3 23.8 %collective-permute-start.17 = (bf16[1024,384]{1,0:T(8,128)(2,1)}, bf16[1024,384]{1,0:T(8,128)(2,1)}, u32[]{:S(2)}, u32[]{:S(2)}) collective-permute-start(bf16[1024,384]{1,0:T(8,128)(2,1)} %slice.67), channel_id=1, source_target_pairs={{4,8},{6,10},{8,4},{10,6},{5,9},{7,11},{9,5},{11,7},{20,24},{22,26... | collective-permute-start | bytes 2359304 | tf_op jit(solution)/shard_map/ppermute | solution.py:529
  84.0 22.4 %collective-permute-start.12 = (bf16[2048,256]{1,0:T(8,128)(2,1)S(1)}, bf16[2048,256]{1,0:T(8,128)(2,1)S(1)}, u32[]{:S(2)}, u32[]{:S(2)}) collective-permute-start(bf16[2048,256]{1,0:T(8,128)(2,1)S(1)} %get-tuple-element.153.refs_2_), channel_id=1, source_target_pairs={{0,2},{2,0},{4,6},{6,4},{8,10},{10,8},{12,14},{14,12},{1,3},{3,1},... | collective-permute-start | bytes 3145736 | tf_op jit(solution)/shard_map/ppermute | solution.py:532
  84.6 21.8 %collective-permute-start.14 = (bf16[2048,256]{1,0:T(8,128)(2,1)S(1)}, bf16[2048,256]{1,0:T(8,128)(2,1)S(1)}, u32[]{:S(2)}, u32[]{:S(2)}) collective-permute-start(bf16[2048,256]{1,0:T(8,128)(2,1)S(1)} %get-tuple-element.153.refs_2_), channel_id=1, source_target_pairs={{0,1},{1,0},{2,3},{3,2},{4,5},{5,4},{6,7},{7,6},{8,9},{9,8},{10,11... | collective-permute-start | bytes 3145736 | tf_op jit(solution)/shard_map/ppermute | solution.py:456
  84.6 21.8 %collective-permute-start.15 = (bf16[1024,512]{1,0:T(8,128)(2,1)}, bf16[1024,512]{1,0:T(8,128)(2,1)S(1)}, u32[]{:S(2)}, u32[]{:S(2)}) collective-permute-start(bf16[1024,512]{1,0:T(8,128)(2,1)} %collective-permute-done.9.refs_4_), channel_id=1, source_target_pairs={{0,1},{1,0},{2,3},{3,2},{4,5},{5,4},{6,7},{7,6},{8,9},{9,8},{10,11... | collective-permute-start | bytes 3145736 | tf_op jit(solution)/shard_map/ppermute | solution.py:456
  85.1 19.7 %collective-permute-start.13 = (bf16[1024,384]{1,0:T(8,128)(2,1)}, bf16[1024,384]{1,0:T(8,128)(2,1)S(1)}, u32[]{:S(2)}, u32[]{:S(2)}) collective-permute-start(bf16[1024,384]{1,0:T(8,128)(2,1)} %slice.67), channel_id=1, source_target_pairs={{0,4},{2,6},{4,0},{6,2},{8,12},{10,14},{12,8},{14,10},{1,5},{3,7},... | collective-permute-start | bytes 2359304 | tf_op jit(solution)/shard_map/ppermute | solution.py:526
  106.5 25.6 %collective-permute-start.18 = (bf16[2048,256]{1,0:T(8,128)(2,1)S(1)}, bf16[2048,256]{1,0:T(8,128)(2,1)S(1)}, u32[]{:S(2)}, u32[]{:S(2)}) collective-permute-start(bf16[2048,256]{1,0:T(8,128)(2,1)S(1)} %get-tuple-element.159.refs_2_), channel_id=1, source_target_pairs={{0,2},{2,0},{4,6},{6,4},{8,10},{10,8},{12,14},{14,12},{1,3},{3,1},... | collective-permute-start | bytes 3145736 | tf_op jit(solution)/shard_map/ppermute | solution.py:532
  108.1 24.0 %collective-permute-start.22 = (bf16[2048,256]{1,0:T(8,128)(2,1)S(1)}, bf16[2048,256]{1,0:T(8,128)(2,1)S(1)}, u32[]{:S(2)}, u32[]{:S(2)}) collective-permute-start(bf16[2048,256]{1,0:T(8,128)(2,1)S(1)} %get-tuple-element.159.refs_2_), channel_id=1, source_target_pairs={{0,1},{1,0},{2,3},{3,2},{4,5},{5,4},{6,7},{7,6},{8,9},{9,8},{10,11... | collective-permute-start | bytes 3145736 | tf_op jit(solution)/shard_map/ppermute | solution.py:456
  108.3 20.0 %collective-permute-start.19 = (bf16[1024,384]{1,0:T(8,128)(2,1)}, bf16[1024,384]{1,0:T(8,128)(2,1)S(1)}, u32[]{:S(2)}, u32[]{:S(2)}) collective-permute-start(bf16[1024,384]{1,0:T(8,128)(2,1)} %collective-permute-done.17.b_ref), channel_id=1, source_target_pairs={{0,4},{2,6},{4,0},{6,2},{8,12},{10,14},{12,8},{14,10},{1,5},{3,7},... | collective-permute-start | bytes 2359304 | tf_op jit(solution)/shard_map/ppermute | solution.py:526
  108.8 19.5 %collective-permute-start.20 = (bf16[1024,384]{1,0:T(8,128)(2,1)S(1)}, bf16[1024,384]{1,0:T(8,128)(2,1)S(1)}, u32[]{:S(2)}, u32[]{:S(2)}) collective-permute-start(bf16[1024,384]{1,0:T(8,128)(2,1)S(1)} %collective-permute-done.13.refs_1_), channel_id=1, source_target_pairs={{4,8},{6,10},{8,4},{10,6},{5,9},{7,11},{9,5},{11,7},{20,24},{22,26... | collective-permute-start | bytes 2359304 | tf_op jit(solution)/shard_map/ppermute | solution.py:529
  132.2 20.0 %collective-permute-start.23 = (bf16[1024,384]{1,0:T(8,128)(2,1)S(1)}, bf16[1024,384]{1,0:T(8,128)(2,1)S(1)}, u32[]{:S(2)}, u32[]{:S(2)}) collective-permute-start(bf16[1024,384]{1,0:T(8,128)(2,1)S(1)} %collective-permute-done.13.refs_1_), channel_id=1, source_target_pairs={{0,2},{2,0},{4,6},{6,4},{8,10},{10,8},{12,14},{14,12},{1,3},{3,1},... | collective-permute-start | bytes 2359304 | tf_op jit(solution)/shard_map/ppermute | solution.py:532
  133.8 19.6 %collective-permute-start.24 = (bf16[1024,384]{1,0:T(8,128)(2,1)S(1)}, bf16[1024,384]{1,0:T(8,128)(2,1)S(1)}, u32[]{:S(2)}, u32[]{:S(2)}) collective-permute-start(bf16[1024,384]{1,0:T(8,128)(2,1)S(1)} %collective-permute-done.20.c_ref), channel_id=1, source_target_pairs={{0,4},{2,6},{4,0},{6,2},{8,12},{10,14},{12,8},{14,10},{1,5},{3,7},... | collective-permute-start | bytes 2359304 | tf_op jit(solution)/shard_map/ppermute | solution.py:526
  134.3 19.1 %collective-permute-start.26 = (bf16[1024,384]{1,0:T(8,128)(2,1)S(1)}, bf16[1024,384]{1,0:T(8,128)(2,1)S(1)}, u32[]{:S(2)}, u32[]{:S(2)}) collective-permute-start(bf16[1024,384]{1,0:T(8,128)(2,1)S(1)} %collective-permute-done.13.refs_1_), channel_id=1, source_target_pairs={{0,1},{1,0},{2,3},{3,2},{4,5},{5,4},{6,7},{7,6},{8,9},{9,8},{10,11... | collective-permute-start | bytes 2359304 | tf_op jit(solution)/shard_map/ppermute | solution.py:456
  134.3 26.0 %collective-permute-start.30 = (f32[512,512]{1,0:T(8,128)S(1)}, f32[512,512]{1,0:T(8,128)S(1)}, u32[]{:S(2)}, u32[]{:S(2)}) collective-permute-start(f32[512,512]{1,0:T(8,128)S(1)} %get-tuple-element.181.refs_0_), channel_id=1, source_target_pairs={{0,16},{16,0},{1,17},{17,1},{2,18},{18,2},{3,19},{19,3},{4,20},{20... | collective-permute-start | bytes 3145736 | tf_op jit(solution)/shard_map/ppermute | solution.py:452
  157.2 26.1 %collective-permute-start.35 = (f32[512,512]{1,0:T(8,128)S(1)}, f32[512,512]{1,0:T(8,128)S(1)}, u32[]{:S(2)}, u32[]{:S(2)}) collective-permute-start(f32[512,512]{1,0:T(8,128)S(1)} %get-tuple-element.191.refs_0_), channel_id=1, source_target_pairs={{0,16},{16,0},{1,17},{17,1},{2,18},{18,2},{3,19},{19,3},{4,20},{20... | collective-permute-start | bytes 3145736 | tf_op jit(solution)/shard_map/ppermute | solution.py:452
  184.6 16.8 %collective-permute-start.36 = (bf16[2048,128]{1,0:T(8,128)(2,1)S(1)}, bf16[2048,128]{1,0:T(8,128)(2,1)}, u32[]{:S(2)}, u32[]{:S(2)}) collective-permute-start(bf16[2048,128]{1,0:T(8,128)(2,1)S(1)} %get-tuple-element.218.refs_2_), channel_id=1, source_target_pairs={{0,2},{2,0},{4,6},{6,4},{8,10},{10,8},{12,14},{14,12},{1,3},{3,1},... | collective-permute-start | bytes 1572872 | tf_op jit(solution)/shard_map/ppermute | solution.py:532
  222.9 24.5 %collective-permute-start.49 = (f32[512,256]{1,0:T(8,128)S(1)}, f32[512,256]{1,0:T(8,128)S(1)}, u32[]{:S(2)}, u32[]{:S(2)}) collective-permute-start(f32[512,256]{1,0:T(8,128)S(1)} %get-tuple-element.237.refs_0_), channel_id=1, source_target_pairs={{0,16},{16,0},{1,17},{17,1},{2,18},{18,2},{3,19},{19,3},{4,20},{20... | collective-permute-start | bytes 1572872 | tf_op jit(solution)/shard_map/ppermute | solution.py:452
  226.2 33.6 %collective-permute-start.54 = (f32[512,256]{1,0:T(8,128)S(1)}, f32[512,256]{1,0:T(8,128)S(1)}, u32[]{:S(2)}, u32[]{:S(2)}) collective-permute-start(f32[512,256]{1,0:T(8,128)S(1)} %copy-done.27), channel_id=1, source_target_pairs={{0,1},{1,0},{2,3},{3,2},{4,5},{5,4},{6,7},{7,6},{8,9},{9,8},{10,11... | collective-permute-start | bytes 1572872 | tf_op jit(solution)/shard_map/ppermute | solution.py:456
  236.5 21.7 %collective-permute-start.50 = (f32[512,256]{1,0:T(8,128)S(1)}, f32[512,256]{1,0:T(8,128)S(1)}, u32[]{:S(2)}, u32[]{:S(2)}) collective-permute-start(f32[512,256]{1,0:T(8,128)S(1)} %get-tuple-element.239.refs_0_), channel_id=1, source_target_pairs={{0,16},{16,0},{1,17},{17,1},{2,18},{18,2},{3,19},{19,3},{4,20},{20... | collective-permute-start | bytes 1572872 | tf_op jit(solution)/shard_map/ppermute | solution.py:452
  238.0 23.5 %collective-permute-start.55 = (f32[512,256]{1,0:T(8,128)S(1)}, f32[512,256]{1,0:T(8,128)S(1)}, u32[]{:S(2)}, u32[]{:S(2)}) collective-permute-start(f32[512,256]{1,0:T(8,128)S(1)} %copy-done.29), channel_id=1, source_target_pairs={{0,1},{1,0},{2,3},{3,2},{4,5},{5,4},{6,7},{7,6},{8,9},{9,8},{10,11... | collective-permute-start | bytes 1572872 | tf_op jit(solution)/shard_map/ppermute | solution.py:456
  238.2 25.4 %collective-permute-start.56 = (f32[512,128]{1,0:T(8,128)S(1)}, f32[512,128]{1,0:T(8,128)S(1)}, u32[]{:S(2)}, u32[]{:S(2)}) collective-permute-start(f32[512,128]{1,0:T(8,128)S(1)} %get-tuple-element.247), channel_id=1, source_target_pairs={{0,1},{1,0},{2,3},{3,2},{4,5},{5,4},{6,7},{7,6},{8,9},{9,8},{10,11... | collective-permute-start | bytes 786440 | tf_op jit(solution)/shard_map/ppermute | solution.py:456
  263.6 44.6 %collective-permute-start.64 = (f32[512,128]{1,0:T(8,128)}, f32[512,128]{1,0:T(8,128)S(1)}, u32[]{:S(2)}, u32[]{:S(2)}) collective-permute-start(f32[512,128]{1,0:T(8,128)} %get-tuple-element.272), channel_id=1, source_target_pairs={{0,1},{1,0},{2,3},{3,2},{4,5},{5,4},{6,7},{7,6},{8,9},{9,8},{10,11... | collective-permute-start | bytes 786440 | tf_op jit(solution)/shard_map/ppermute | solution.py:456
  268.2 39.9 %collective-permute-start.65 = (f32[512,128]{1,0:T(8,128)}, f32[512,128]{1,0:T(8,128)S(1)}, u32[]{:S(2)}, u32[]{:S(2)}) collective-permute-start(f32[512,128]{1,0:T(8,128)} %get-tuple-element.273), channel_id=1, source_target_pairs={{0,1},{1,0},{2,3},{3,2},{4,5},{5,4},{6,7},{7,6},{8,9},{9,8},{10,11... | collective-permute-start | bytes 786440 | tf_op jit(solution)/shard_map/ppermute | solution.py:456
  (103 other events, 1074.2 us)
